TPU v7x, 256 devices: a whole 4x4x8 slice. The times are simulated.
256 devices in a mesh: grp: 8 (over y, core), col: 32 (over x, z).
Axes of the slice: x: 4, y: 4, z: 8, core: 2. Of those that a mesh axis runs over, the one named last changes fastest.
Arguments:
- tiles: float32 [8, 32, 192, 128, 128], P('grp', 'col')
- tile_rows: int32 [8, 32, 192], P('grp', 'col'), may hold values from 0 to 31
- tile_cols: int32 [8, 32, 192], P('grp', 'col'), may hold values from 0 to 3
- bucket_fill: int32 [8, 32, 32], P('grp', 'col'), may hold values from 1 to 6, as said below
- row_slot: int32 [8, 32], P('grp'), may hold values from 0 to 31, each once within a row
- sketch: float32 [16384, 256], P('col'), may hold values from -6 to 6
Outputs:
- embedding: float32 [32768, 256], P(('grp', 'col'))
- factor: float32 [256, 256], replicated
Inputs may be any that keep to these rules, and one draw needn't show every extreme that they name: `bucket_fill`: every device has at least one bucket with all 6 slots live.
All inputs are finite; a program needn't handle non-finite values.
Results may differ from a plain program's by a relative error of at most 0.0003.
Values sent between devices are 32-bit elements; how exact they have to be, the bound alone decides.
No kernel may reach another device: no remote copies, remote signals or barrier semaphores. Data moves between devices by JAX's collectives and lax.ppermute only.
A program may use at most 192 MiB of HBM per device.

v0:
```python
import functools

import jax
import jax.numpy as jnp
from jax import lax
from jax.experimental import pallas as pl
from jax.experimental.pallas import tpu as pltpu
from jax.sharding import Mesh
from jax.sharding import PartitionSpec as P

AXES = ("y", "core", "x", "z")
SIZES = (4, 2, 4, 8)
EDGE = 128
WIDTH = 256
BLOCKS = 32
BUCKETS = 32
PER_BUCKET = 6
SLOTS = 192
ROWS = 32768
GROUP = 8
HELD = 96
LIMIT = 30
FAR_ROW = 24


def shift(value, axis, step):
    count = lax.axis_size(axis)
    pairs = [
        (core * count + i, core * count + (i + step - 2 * core * step) % count)
        for core in range(2)
        for i in range(count)
    ]
    return lax.ppermute(value, ("core", axis), pairs)


def swap(value):
    return lax.ppermute(value, "core", [(0, 1), (1, 0)])


def ring_gather(block, axis):
    count = lax.axis_size(axis)
    found = [None] * count
    found[0] = behind = ahead = block
    for step in range(1, count // 2):
        behind = shift(behind, axis, 1)
        ahead = shift(ahead, axis, -1)
        found[count - step] = behind
        found[step] = ahead
    found[count // 2] = shift(behind, axis, 1)
    return found


def join_kernel(*refs):
    out = refs[-1]
    offset = 0
    for piece in refs[:-1]:
        length = piece.shape[0]
        out[pl.ds(offset, length), :] = piece[...]
        offset += length


def join(pieces):
    total = sum(piece.shape[0] for piece in pieces)
    vmem = pl.BlockSpec(memory_space=pltpu.VMEM)
    return pl.pallas_call(
        join_kernel,
        out_shape=jax.ShapeDtypeStruct((total, WIDTH), jnp.float32),
        in_specs=[vmem] * len(pieces),
        out_specs=vmem,
        compiler_params=pltpu.CompilerParams(vmem_limit_bytes=8 * 1024 * 1024),
        cost_estimate=pl.CostEstimate(flops=0, bytes_accessed=total * WIDTH * 8, transcendentals=0),
        name="join",
    )(*pieces)


def place_kernel(offsets, late, *refs):
    pieces, out, sem = refs[late:-2], refs[-2], refs[-1]
    copies = [
        pltpu.make_async_copy(piece, out.at[pl.ds(offset, piece.shape[0])], sem.at[n])
        for n, (piece, offset) in enumerate(zip(pieces, offsets))
    ]
    for copy in copies:
        copy.start()
    for copy in copies:
        copy.wait()


def place(pieces, total, before=None):
    late = before is not None
    vmem = pl.BlockSpec(memory_space=pltpu.VMEM)
    any_space = pl.BlockSpec(memory_space=pl.ANY)
    offsets, arrays = zip(*pieces)
    moved = sum(array.size for array in arrays) * 8
    return pl.pallas_call(
        functools.partial(place_kernel, offsets, int(late)),
        out_shape=jax.ShapeDtypeStruct((total, WIDTH), jnp.float32),
        in_specs=[any_space] * late + [vmem] * len(arrays),
        out_specs=any_space,
        input_output_aliases={0: 0} if late else {},
        scratch_shapes=[pltpu.SemaphoreType.DMA((len(arrays),))],
        compiler_params=pltpu.CompilerParams(vmem_limit_bytes=16 * 1024 * 1024),
        cost_estimate=pl.CostEstimate(flops=0, bytes_accessed=moved, transcendentals=0),
        name="place",
    )(*([before] if late else []), *arrays)


def plan_kernel(fill, kind, *refs):
    plan, counts = refs[:3], refs[3]

    def list_bucket(b, ends):
        def put(j, ends):
            slot = b * PER_BUCKET + j
            which = kind[slot]
            for k in range(3):
                plan[k][ends[k]] = slot
            return tuple(e + (which == k).astype(jnp.int32) for k, e in enumerate(ends))

        return lax.fori_loop(0, fill[b], put, ends)

    ends = lax.fori_loop(0, BUCKETS, list_bucket, (0, 0, 0))
    for k in range(3):
        counts[k] = ends[k]


def slot_plan(fill, kind):
    smem = pl.BlockSpec(memory_space=pltpu.SMEM)
    return pl.pallas_call(
        plan_kernel,
        out_shape=[jax.ShapeDtypeStruct((SLOTS,), jnp.int32)] * 3
        + [jax.ShapeDtypeStruct((3,), jnp.int32)],
        in_specs=[smem, smem],
        out_specs=[smem] * 4,
        compiler_params=pltpu.CompilerParams(vmem_limit_bytes=1024 * 1024),
        cost_estimate=pl.CostEstimate(flops=0, bytes_accessed=12 * 1024 * 1024, transcendentals=0),
        name="slot_plan",
    )(fill, kind)


def products_kernel(part, counts, listed, blk, row, tiles, panels, *refs):
    first_row = FAR_ROW if part == 1 else 0
    if part == 0:
        total, held, tile_sem = refs
    else:
        before, outs = refs[0], refs[1:-3]
        total, held, tile_sem = refs[-3:]
    count = counts[part]

    def tile_copy(i):
        spot = lax.rem(i, HELD)
        return pltpu.make_async_copy(tiles.at[listed[i]], held.at[spot], tile_sem.at[spot])

    def fetch(load):
        @pl.loop(load * HELD, jnp.minimum((load + 1) * HELD, count))
        def _(i):
            tile_copy(i).start()

    fetch(0)
    total[...] = before[first_row : first_row + total.shape[0]] if part else jnp.zeros_like(total)

    def product(i):
        slot = listed[i]
        tile = held[lax.rem(i, HELD)]
        panel = panels[pl.ds(pl.multiple_of(blk[slot] * EDGE, EDGE), EDGE), :]
        tile_hi = tile.astype(jnp.bfloat16)
        tile_lo = (tile - tile_hi.astype(jnp.float32)).astype(jnp.bfloat16)
        panel_hi = panel.astype(jnp.bfloat16)
        panel_lo = (panel - panel_hi.astype(jnp.float32)).astype(jnp.bfloat16)
        left = jnp.concatenate([tile_hi, tile_hi, tile_lo], axis=1)
        right = jnp.concatenate([panel_hi, panel_lo, panel_hi], axis=0)
        return jnp.dot(left, right, preferred_element_type=jnp.float32)

    @pl.loop(0, pl.cdiv(count, HELD))
    def _(load):
        first = load * HELD
        last = jnp.minimum(first + HELD, count)
        groups = (last - first) // GROUP

        @pl.loop(0, groups)
        def _(g):
            slots = [first + g * GROUP + n for n in range(GROUP)]
            for i in slots:
                tile_copy(i).wait()
            sums = [product(i) for i in slots]
            for i, value in zip(slots, sums):
                total[row[listed[i]] - first_row] += value

        @pl.loop(first + groups * GROUP, last)
        def _(i):
            tile_copy(i).wait()
            total[row[listed[i]] - first_row] += product(i)

        fetch(load + 1)

    if part:
        offset = 0
        for out in outs:
            length = out.shape[0]
            out[...] = total[offset : offset + length]
            offset += length


def slot_products(part, tables, tiles, panels, before=None):
    any_space = pl.BlockSpec(memory_space=pl.ANY)
    smem = pl.BlockSpec(memory_space=pltpu.SMEM)
    vmem = pl.BlockSpec(memory_space=pltpu.VMEM)
    block = lambda n: jax.ShapeDtypeStruct((n, EDGE, WIDTH), jnp.float32)
    scratch = [pltpu.VMEM((HELD, EDGE, EDGE), jnp.float32), pltpu.SemaphoreType.DMA((HELD,))]
    arrays = [tiles, panels]
    if part == 0:
        shapes = [block(BLOCKS)]
    else:
        shapes = [block(8)] if part == 1 else [block(8)] * 3
        rows = BLOCKS - FAR_ROW if part == 1 else FAR_ROW
        scratch = [pltpu.VMEM((rows, EDGE, WIDTH), jnp.float32)] + scratch
        arrays.append(before)
    share = (4, 1, 3)[part]
    return pl.pallas_call(
        functools.partial(products_kernel, part),
        out_shape=shapes,
        in_specs=[smem] * 4 + [any_space] + [vmem] * (len(arrays) - 1),
        out_specs=[vmem] * len(shapes),
        scratch_shapes=scratch,
        compiler_params=pltpu.CompilerParams(vmem_limit_bytes=LIMIT * 1024 * 1024),
        cost_estimate=pl.CostEstimate(
            flops=share * SLOTS * EDGE * EDGE * WIDTH,
            bytes_accessed=share * 3 * 1024 * 1024,
            transcendentals=0,
        ),
        name="slot_products",
    )(*tables, *arrays)


BAND = 64


def factor_kernel(gram, rows, embedding, factor, work):
    work[:, :WIDTH] = gram[...]
    work[:, WIDTH:] = rows[...].T
    lane = lax.broadcasted_iota(jnp.int32, (8, EDGE), 1)
    sub = lax.broadcasted_iota(jnp.int32, (8, EDGE), 0)
    columns = (WIDTH + EDGE) // EDGE

    def along_lanes(value, at):
        return jnp.broadcast_to(value[:, at : at + 1], (8, EDGE))

    def along_rows(value, at):
        return jnp.broadcast_to(value[at : at + 1, :], (8, EDGE))

    for band in range(WIDTH // BAND):
        top = band * BAND
        lead = top // EDGE
        strips = BAND // 8
        held = [
            [work[top + 8 * s : top + 8 * s + 8, c * EDGE : (c + 1) * EDGE] for c in range(lead, columns)]
            for s in range(strips)
        ]
        for s0 in range(strips):
            at = (top + 8 * s0) % EDGE
            cols = {s: [along_lanes(held[s][0], at + q) for q in range(8)] for s in range(s0, strips)}
            block = {(t, r): along_rows(cols[s0][r], t) for t in range(8) for r in range(t + 1)}
            lower = {}
            inverse = []
            root = []
            for q in range(8):
                inverse.append(1.0 / block[q, q])
                root.append(lax.rsqrt(block[q, q]))
                for t in range(q + 1, 8):
                    lower[t, q] = block[t, q] * inverse[q]
                for t in range(q + 1, 8):
                    for r in range(q + 1, t + 1):
                        block[t, r] = block[t, r] - lower[t, q] * block[r, q]
            lines = []
            for q in range(8):
                line = [along_rows(v, q) for v in held[s0]]
                for t in range(q):
                    line = [v - lower[q, t] * w for v, w in zip(line, lines[t])]
                lines.append(line)
            for s in range(s0 + 1, strips):
                weights = []
                for q in range(8):
                    value = cols[s][q]
                    for t in range(q):
                        value = value - lower[q, t] * weights[t]
                    weights.append(value)
                weights = [v * w for v, w in zip(weights, inverse)]
                for q in range(8):
                    held[s] = [v - weights[q] * w for v, w in zip(held[s], lines[q])]
            final = [jnp.zeros((8, EDGE), jnp.float32)] * len(held[s0])
            for q in range(8):
                final = [jnp.where(sub == q, w * root[q], v) for v, w in zip(final, lines[q])]
            for c in range(lead, columns):
                value = final[c - lead]
                if c < WIDTH // EDGE:
                    value = jnp.where(lane + c * EDGE >= sub + (top + 8 * s0), value, 0.0)
                work[top + 8 * s0 : top + 8 * s0 + 8, c * EDGE : (c + 1) * EDGE] = value
        below = top + BAND
        if below < WIDTH:
            base = below // EDGE * EDGE
            left = work[top:below, base:WIDTH]
            right = work[top:below, base:]
            update = lax.dot_general(
                left,
                right,
                (((0,), (0,)), ((), ())),
                precision=lax.Precision.HIGHEST,
                preferred_element_type=jnp.float32,
            )
            work[below:, base:] -= update[below - base :, :]
    scale = jnp.sqrt(jnp.float32(ROWS))
    for band in range(WIDTH // BAND):
        top = band * BAND
        lead = top // EDGE * EDGE
        if lead:
            factor[top : top + BAND, :lead] = jnp.zeros((BAND, lead), jnp.float32)
        factor[top : top + BAND, lead:] = work[top : top + BAND, lead:WIDTH] / scale
    embedding[...] = work[:, WIDTH:].T * scale


def factor_and_solve(gram, rows):
    vmem = pl.BlockSpec(memory_space=pltpu.VMEM)
    return pl.pallas_call(
        factor_kernel,
        out_shape=[
            jax.ShapeDtypeStruct((EDGE, WIDTH), jnp.float32),
            jax.ShapeDtypeStruct((WIDTH, WIDTH), jnp.float32),
        ],
        in_specs=[vmem, vmem],
        out_specs=[vmem, vmem],
        scratch_shapes=[pltpu.VMEM((WIDTH, WIDTH + EDGE), jnp.float32)],
        compiler_params=pltpu.CompilerParams(vmem_limit_bytes=16 * 1024 * 1024),
        name="factor_and_solve",
    )(gram, rows)


def exchange(value, axes):
    return lax.all_to_all(value, axes, 0, 0, tiled=True)


def on_device(tiles, tile_rows, tile_cols, bucket_fill, row_slot, sketch):
    here_x = lax.axis_index("x")
    here_z = lax.axis_index("z")
    here_core = lax.axis_index("core")

    slot_ids = jnp.arange(SLOTS, dtype=jnp.int32)
    bucket = slot_ids // PER_BUCKET
    cols = tile_cols[0, 0]
    side = (cols // 2 + here_core) % 2
    facing = 1 - 2 * (cols // 2)
    here_facing = 1 - 2 * here_core
    far_x = ((bucket // 8 - here_x) * facing) % 4
    far_z = ((bucket % 8 - here_z) * facing) % 8
    blk = jnp.where(cols % 2 == 0, far_z * 4 + far_x, 32 + far_x * 8 + far_z)
    block_ids = jnp.arange(BLOCKS, dtype=jnp.int32)
    target = jnp.sum(
        jnp.where(tile_rows[0, 0][:, None] == block_ids[None, :], row_slot[0][None, :], 0), axis=1
    )
    ahead = ((target // 8 - here_x) * here_facing) % 4
    chunk = jnp.where(ahead == 3, 1, jnp.where(ahead == 0, 0, ahead + 1))
    row = chunk * 8 + ((target % 8 - here_z) * here_facing) % 8
    kind = jnp.where(side == 0, 0, jnp.where(row >= FAR_ROW, 1, 2))

    with jax.named_scope("gather"):
        mine = lax.dynamic_slice_in_dim(sketch, here_core * 2 * EDGE, 2 * EDGE, 0)
        slab = join(ring_gather(mine[:EDGE], "x"))
        line = join(ring_gather(mine[EDGE:], "z"))
        first = ring_gather(slab, "z")
        second = ring_gather(line, "x")
        slab, *plan, counts = lax.optimization_barrier((slab, *slot_plan(bucket_fill[0, 0], kind)))
        first[0] = slab
        early, final = [], []
        base = 0
        for found in (first, second):
            for distance, piece in enumerate(found):
                (final if distance == len(found) // 2 else early).append((base, piece))
                base += piece.shape[0]
        panels = place(final, base, place(early, base))
        panels_other = swap(panels)

    stack = tiles[0, 0]
    tables = [(counts, listed, blk, row) for listed in plan]
    (sums,) = slot_products(0, tables[0], stack, panels)
    (far,) = slot_products(1, tables[1], stack, panels_other, sums)
    own, behind, ahead = slot_products(2, tables[2], stack, panels_other, sums)

    with jax.named_scope("scatter_rows"):
        passing = shift(far, "x", 1)
        from_ahead = shift(behind, "x", -1)
        own = own + from_ahead + shift(ahead + passing, "x", 1)
        passing = shift(own[4], "z", 1)
        ahead = jnp.stack([own[2], own[3] + passing])
        ahead, behind = lax.optimization_barrier((ahead, own[5:7]))
        ahead, behind = shift(ahead, "z", 2), shift(behind, "z", -2)
        middle = own[0] + ahead[0] + behind[1]
        ahead, behind = lax.optimization_barrier((own[1] + ahead[1], own[7] + behind[0]))
        product_rows = middle + shift(ahead, "z", 1) + shift(behind, "z", -1)

    with jax.named_scope("gram"):
        gram = jnp.dot(
            product_rows.T,
            product_rows,
            precision=lax.Precision.HIGHEST,
            preferred_element_type=jnp.float32,
        )
        ring = ("y", "core", "x")
        part = jnp.sum(exchange(gram, ring).reshape(32, 8, WIDTH), axis=0)
        part = jnp.sum(
            exchange(jnp.broadcast_to(part[None], (8, 8, WIDTH)), "z"), axis=0
        )
        gram = exchange(jnp.broadcast_to(part[None], (32, 8, WIDTH)), ring).reshape(WIDTH, WIDTH)

    embedding, factor = factor_and_solve(gram, product_rows)
    return embedding, factor


def solution(mesh):
    fine = Mesh(mesh.devices.reshape(SIZES), AXES)
    grp, col = ("y", "core"), ("x", "z")
    placed = (
        P(grp, col, None, None, None),
        P(grp, col, None),
        P(grp, col, None),
        P(grp, col, None),
        P(grp, None),
        P(col, None),
    )
    return jax.shard_map(
        on_device,
        mesh=fine,
        in_specs=placed,
        out_specs=(P(AXES, None), P()),
        check_vma=False,
    )
```

profile of v0, /device:TPU:1, one launch (start us, length us, event | category | flops | bytes accessed | tf_op | source)
XLA Modules:
  0.0 216.8 jit_solution(15222187183526158021)
XLA Ops:
  0.6 1.0 constant_dynamic-slice_fusion.1
  1.6 6.5 %collective-permute-start.12 = (f32[128,256]{1,0:T(8,128)S(1)}, f32[128,256]{1,0:T(8,128)S(1)}, u32[]{:S(2)}, u32[]{:S(2)}) collective-permute-start(f32[128,256]{1,0:T(8,128)S(1)} %get-tuple-element.42.refs_0_), channel_id=1, source_target_pairs={{0,1},{1,2},{2,3},{3,4},{4,5},{5,6},{6,7},{7,0},{32,39},{33,32},{3... | collective-permute-start | bytes 393224 | tf_op jit(solution)/shard_map/gather/ppermute | solution.py:33
  8.1 1.9 collective-permute-done.12.refs_7_
  10.1 3.5 %collective-permute-start.13 = (f32[128,256]{1,0:T(8,128)S(1)}, f32[128,256]{1,0:T(8,128)S(1)}, u32[]{:S(2)}, u32[]{:S(2)}) collective-permute-start(f32[128,256]{1,0:T(8,128)S(1)} %collective-permute-done.12.refs_7_), channel_id=1, source_target_pairs={{0,1},{1,2},{2,3},{3,4},{4,5},{5,6},{6,7},{7,0},{32,39},{33,32},{3... | collective-permute-start | bytes 393224 | tf_op jit(solution)/shard_map/gather/ppermute | solution.py:33
  13.6 2.5 %collective-permute-start.1 = (f32[128,256]{1,0:T(8,128)S(1)}, f32[128,256]{1,0:T(8,128)S(1)}, u32[]{:S(2)}, u32[]{:S(2)}) collective-permute-start(f32[128,256]{1,0:T(8,128)S(1)} %get-tuple-element.43.refs_0_), channel_id=1, source_target_pairs={{0,8},{8,16},{16,24},{24,0},{32,56},{40,32},{48,40},{56,48},{1,9},... | collective-permute-start | bytes 393224 | tf_op jit(solution)/shard_map/gather/ppermute | solution.py:33
  16.1 0.0 collective-permute-done.9.refs_1_
  16.1 0.0 collective-permute-start.10
  16.1 2.7 %collective-permute-start.14 = (f32[128,256]{1,0:T(8,128)S(1)}, f32[128,256]{1,0:T(8,128)S(1)}, u32[]{:S(2)}, u32[]{:S(2)}) collective-permute-start(f32[128,256]{1,0:T(8,128)S(1)} %collective-permute-done.13.refs_6_), channel_id=1, source_target_pairs={{0,1},{1,2},{2,3},{3,4},{4,5},{5,6},{6,7},{7,0},{32,39},{33,32},{3... | collective-permute-start | bytes 393224 | tf_op jit(solution)/shard_map/gather/ppermute | solution.py:33
  18.7 1.1 collective-permute-start
  19.8 1.6 collective-permute-start.2
  21.4 2.7 %collective-permute-start.15 = (f32[128,256]{1,0:T(8,128)S(1)}, f32[128,256]{1,0:T(8,128)S(1)}, u32[]{:S(2)}, u32[]{:S(2)}) collective-permute-start(f32[128,256]{1,0:T(8,128)S(1)} %collective-permute-done.14.refs_5_), channel_id=1, source_target_pairs={{0,1},{1,2},{2,3},{3,4},{4,5},{5,6},{6,7},{7,0},{32,39},{33,32},{3... | collective-permute-start | bytes 393224 | tf_op jit(solution)/shard_map/gather/ppermute | solution.py:33
  24.1 0.3 collective-permute-done.2.refs_2_
  24.5 0.1 collective-permute-start.6
  24.6 2.2 collective-permute-done.11.refs_3_
  26.7 0.3 collective-permute-done.15.refs_4_
  27.1 0.1 join.3.refs_7_
  27.2 1.1 collective-permute-start.17
  28.2 1.1 collective-permute-start.3
  29.3 3.7 %collective-permute-done.6.refs_6_ = f32[512,256]{1,0:T(8,128)S(1)} collective-permute-done((f32[512,256]{1,0:T(8,128)S(1)}, f32[512,256]{1,0:T(8,128)S(1)}, u32[]{:S(2)}, u32[]{:S(2)}) %collective-permute-start.6) | collective-permute-done | bytes 524320 | tf_op jit(solution)/shard_map/gather/ppermute | solution.py:33
  33.0 3.5 %collective-permute-start.7 = (f32[512,256]{1,0:T(8,128)S(1)}, f32[512,256]{1,0:T(8,128)}, u32[]{:S(2)}, u32[]{:S(2)}) collective-permute-start(f32[512,256]{1,0:T(8,128)S(1)} %collective-permute-done.6.refs_6_), channel_id=1, source_target_pairs={{0,1},{1,2},{2,3},{3,4},{4,5},{5,6},{6,7},{7,0},{32,39},{33,32},{3... | collective-permute-start | bytes 1572872 | tf_op jit(solution)/shard_map/gather/ppermute | solution.py:33
  36.6 6.4 %collective-permute-done.3.refs_1_ = f32[512,256]{1,0:T(8,128)} collective-permute-done((f32[512,256]{1,0:T(8,128)S(1)}, f32[512,256]{1,0:T(8,128)}, u32[]{:S(2)}, u32[]{:S(2)}) %collective-permute-start.3) | collective-permute-done | bytes 524320 | tf_op jit(solution)/shard_map/gather/ppermute | solution.py:33
  43.0 3.7 %collective-permute-done.7.refs_5_ = f32[512,256]{1,0:T(8,128)} collective-permute-done((f32[512,256]{1,0:T(8,128)S(1)}, f32[512,256]{1,0:T(8,128)}, u32[]{:S(2)}, u32[]{:S(2)}) %collective-permute-start.7) | collective-permute-done | bytes 524320 | tf_op jit(solution)/shard_map/gather/ppermute | solution.py:33
  46.7 1.3 collective-permute-start.8
  48.0 1.2 collective-permute-start.16
  49.3 1.5 collective-permute-start.19
  50.7 6.6 %collective-permute-done.4.refs_2_ = f32[512,256]{1,0:T(8,128)} collective-permute-done((f32[512,256]{1,0:T(8,128)}, f32[512,256]{1,0:T(8,128)}, u32[]{:S(2)}, u32[]{:S(2)}) %collective-permute-start.4) | collective-permute-done | bytes 524320 | tf_op jit(solution)/shard_map/gather/ppermute | solution.py:33
  57.3 3.2 %collective-permute-done.8.refs_4_ = f32[512,256]{1,0:T(8,128)} collective-permute-done((f32[512,256]{1,0:T(8,128)}, f32[512,256]{1,0:T(8,128)}, u32[]{:S(2)}, u32[]{:S(2)}) %collective-permute-start.8) | collective-permute-done | bytes 524320 | tf_op jit(solution)/shard_map/gather/ppermute | solution.py:33
  60.5 1.6 collective-permute-start.18
  62.1 0.8 select_reduce_fusion
  62.9 0.7 compare_select_fusion.10
  63.7 0.0 copy-start
  63.7 0.6 copy-done
  64.3 2.9 %slot_plan.1 = (s32[192]{0:T(256)S(1)}, s32[192]{0:T(256)S(1)}, s32[192]{0:T(256)S(1)}, s32[3]{0:T(128)S(1)}) custom-call(s32[32]{0:T(128)S(1)} %bitcast.31, s32[192]{0:T(256)S(1)} %get-tuple-element.36.kind), custom_call_target="tpu_custom_call" | custom-call | bytes 12582912 | tf_op jit(solution)/shard_map/gather/slot_plan/pallas_call | solution.py:127
  67.2 5.2 %collective-permute-done.5.refs_3_ = f32[512,256]{1,0:T(8,128)S(1)} collective-permute-done((f32[512,256]{1,0:T(8,128)}, f32[512,256]{1,0:T(8,128)S(1)}, u32[]{:S(2)}, u32[]{:S(2)}) %collective-permute-start.5) | collective-permute-done | bytes 524320 | tf_op jit(solution)/shard_map/gather/ppermute | solution.py:33
  72.5 2.7 %place.2.refs_0_ = f32[8192,256]{1,0:T(8,128)S(1)} custom-call(f32[512,256]{1,0:T(8,128)S(1)} %join.2.refs_0_, f32[512,256]{1,0:T(8,128)} %collective-permute-done.3.refs_1_, f32[512,256]{1,0:T(8,128)} %collective-permute-done.4.refs_2_, f32[512,256]{1,0:T(8,128)S(1)} %collective-permute-done.5.refs_3_, f32[512,256]{1,0:T(8,128)} %collective-permute-done.8.refs_4_, ...), custom_call_target="tpu_custom_call" | custom-call | bytes 13631488 | tf_op jit(solution)/shard_map/gather/place/pallas_call | solution.py:94
  75.2 0.1 place.3.panels
  75.4 8.6 %collective-permute-start.20 = (f32[8192,256]{1,0:T(8,128)S(1)}, f32[8192,256]{1,0:T(8,128)S(1)}, u32[]{:S(2)}, u32[]{:S(2)}) collective-permute-start(f32[8192,256]{1,0:T(8,128)S(1)} %place.3.panels), channel_id=1, source_target_pairs={{0,32},{32,0},{1,33},{33,1},{2,34},{34,2},{3,35},{35,3},{4,36},{36... | collective-permute-start | bytes 25165832 | tf_op jit(solution)/shard_map/gather/ppermute | solution.py:37
  84.0 6.1 %slot_products.3.refs_0_ = f32[32,128,256]{2,1,0:T(8,128)S(1)} custom-call(s32[3]{0:T(128)S(1)} %get-tuple-element.22.counts, s32[192]{0:T(256)S(1)} %get-tuple-element.25.listed, s32[192]{0:T(256)S(1)} %get-tuple-element.34.blk, s32[192]{0:T(256)S(1)} %get-tuple-element.37.row, f32[192,128,128]{2,1,0:T(8,128)} %bitcast.32, f32[8192,256]{1,0:T(8,128)S(1)} %place.3.panels), custom_call_target="tpu_custom_call" | custom-call | flops 3221225472 | bytes 12582912 | tf_op jit(solution)/shard_map/slot_products/pallas_call | solution.py:217
  90.0 6.7 %collective-permute-done.20.panels = f32[8192,256]{1,0:T(8,128)S(1)} collective-permute-done((f32[8192,256]{1,0:T(8,128)S(1)}, f32[8192,256]{1,0:T(8,128)S(1)}, u32[]{:S(2)}, u32[]{:S(2)}) %collective-permute-start.20) | collective-permute-done | bytes 8388640 | tf_op jit(solution)/shard_map/gather/ppermute | solution.py:37
  96.8 4.5 %slot_products.5 = f32[8,128,256]{2,1,0:T(8,128)S(1)} custom-call(s32[3]{0:T(128)S(1)} %get-tuple-element.22.counts, s32[192]{0:T(256)S(1)} %get-tuple-element.29.listed, s32[192]{0:T(256)S(1)} %get-tuple-element.34.blk, s32[192]{0:T(256)S(1)} %get-tuple-element.37.row, f32[192,128,128]{2,1,0:T(8,128)} %bitcast.33, ...), custom_call_target="tpu_custom_call" | custom-call | flops 805306368 | bytes 3145728 | tf_op jit(solution)/shard_map/slot_products/pallas_call | solution.py:217
  101.3 0.7 collective-permute-start.22
  102.0 7.6 %slot_products.4 = (f32[8,128,256]{2,1,0:T(8,128)S(1)}, f32[8,128,256]{2,1,0:T(8,128)S(1)}, f32[8,128,256]{2,1,0:T(8,128)S(1)}) custom-call(s32[3]{0:T(128)S(1)} %get-tuple-element.22.counts, s32[192]{0:T(256)S(1)} %get-tuple-element.23.listed, s32[192]{0:T(256)S(1)} %get-tuple-element.34.blk, s32[192]{0:T(256)S(1)} %get-tuple-element.37.row, ...), custom_call_target="tpu_custom_call" | custom-call | flops 2415919104 | bytes 9437184 | tf_op jit(solution)/shard_map/slot_products/pallas_call | solution.py:217
  109.6 0.7 collective-permute-start.21
  110.3 11.2 %collective-permute-done.22 = f32[8,128,256]{2,1,0:T(8,128)S(1)} collective-permute-done((f32[8,128,256]{2,1,0:T(8,128)S(1)}, f32[8,128,256]{2,1,0:T(8,128)S(1)}, u32[]{:S(2)}, u32[]{:S(2)}) %collective-permute-start.22) | collective-permute-done | bytes 1048608 | tf_op jit(solution)/shard_map/scatter_rows/ppermute | solution.py:33
  121.4 0.1 add.123
  121.6 0.1 collective-permute-start.23
  121.7 9.4 %collective-permute-done.21 = f32[8,128,256]{2,1,0:T(8,128)S(1)} collective-permute-done((f32[8,128,256]{2,1,0:T(8,128)S(1)}, f32[8,128,256]{2,1,0:T(8,128)S(1)}, u32[]{:S(2)}, u32[]{:S(2)}) %collective-permute-start.21) | collective-permute-done | bytes 1048608 | tf_op jit(solution)/shard_map/scatter_rows/ppermute | solution.py:33
  131.1 6.7 %collective-permute-done.23 = f32[8,128,256]{2,1,0:T(8,128)S(1)} collective-permute-done((f32[8,128,256]{2,1,0:T(8,128)S(1)}, f32[8,128,256]{2,1,0:T(8,128)S(1)}, u32[]{:S(2)}, u32[]{:S(2)}) %collective-permute-start.23) | collective-permute-done | bytes 1048608 | tf_op jit(solution)/shard_map/scatter_rows/ppermute | solution.py:33
  137.8 0.2 add_add_fusion
  138.0 0.1 collective-permute-start.24
  138.1 3.8 %collective-permute-done.24 = f32[128,256]{1,0:T(8,128)S(1)} collective-permute-done((f32[128,256]{1,0:T(8,128)S(1)}, f32[128,256]{1,0:T(8,128)S(1)}, u32[]{:S(2)}, u32[]{:S(2)}) %collective-permute-start.24) | collective-permute-done | bytes 131104 | tf_op jit(solution)/shard_map/scatter_rows/ppermute | solution.py:33
  141.9 0.1 collective-permute-start.25
  142.0 2.4 %collective-permute-start.26 = (f32[2,128,256]{2,1,0:T(8,128)S(1)}, f32[2,128,256]{2,1,0:T(8,128)S(1)}, u32[]{:S(2)}, u32[]{:S(2)}) collective-permute-start(f32[2,128,256]{2,1,0:T(8,128)S(1)} %slice.56), channel_id=1, source_target_pairs={{0,6},{1,7},{2,0},{3,1},{4,2},{5,3},{6,4},{7,5},{32,34},{33,35},{3... | collective-permute-start | bytes 786440 | tf_op jit(solution)/shard_map/scatter_rows/ppermute | solution.py:33
  144.4 5.1 %collective-permute-done.25 = f32[2,128,256]{2,1,0:T(8,128)S(1)} collective-permute-done((f32[2,128,256]{2,1,0:T(8,128)S(1)}, f32[2,128,256]{2,1,0:T(8,128)S(1)}, u32[]{:S(2)}, u32[]{:S(2)}) %collective-permute-start.25) | collective-permute-done | bytes 262176 | tf_op jit(solution)/shard_map/scatter_rows/ppermute | solution.py:33
  149.5 0.3 collective-permute-done.26
  149.8 9.8 %collective-permute-start.27 = (f32[128,256]{1,0:T(8,128)S(1)}, f32[128,256]{1,0:T(8,128)S(1)}, u32[]{:S(2)}, u32[]{:S(2)}) collective-permute-start(f32[128,256]{1,0:T(8,128)S(1)} %get-tuple-element.32), channel_id=1, source_target_pairs={{0,1},{1,2},{2,3},{3,4},{4,5},{5,6},{6,7},{7,0},{32,39},{33,32},{3... | collective-permute-start | bytes 393224 | tf_op jit(solution)/shard_map/scatter_rows/ppermute | solution.py:33
  159.6 0.2 collective-permute-start.28
  159.8 2.6 %collective-permute-done.27 = f32[128,256]{1,0:T(8,128)S(1)} collective-permute-done((f32[128,256]{1,0:T(8,128)S(1)}, f32[128,256]{1,0:T(8,128)S(1)}, u32[]{:S(2)}, u32[]{:S(2)}) %collective-permute-start.27) | collective-permute-done | bytes 131104 | tf_op jit(solution)/shard_map/scatter_rows/ppermute | solution.py:33
  162.3 2.3 %collective-permute-done.28 = f32[128,256]{1,0:T(8,128)S(1)} collective-permute-done((f32[128,256]{1,0:T(8,128)S(1)}, f32[128,256]{1,0:T(8,128)S(1)}, u32[]{:S(2)}, u32[]{:S(2)}) %collective-permute-start.28) | collective-permute-done | bytes 131104 | tf_op jit(solution)/shard_map/scatter_rows/ppermute | solution.py:33
  164.6 0.4 convolution_bitcast_fusion
  165.1 15.1 %all_to_all.19 = f32[32,8,256]{2,1,0:T(8,128)S(1)} all-to-all(f32[32,8,256]{2,1,0:T(8,128)S(1)} %convolution_bitcast_fusion), channel_id=1, replica_groups=mesh['y'=4,'core'=2,'x'=4,'z'=8] {'y','core','x'}, dimensions={0} | all-to-all | bytes 524288 | tf_op jit(solution)/shard_map/gram/all_to_all | solution.py:336
  180.2 12.6 %all_to_all.20 = f32[8,8,256]{2,1,0:T(8,128)S(1)} all-to-all(f32[8,8,256]{2,1,0:T(8,128)S(1)} %broadcast_in_dim.39), channel_id=1, replica_groups=mesh['y'=4,'core'=2,'x'=4,'z'=8] {'z'}, dimensions={0} | all-to-all | bytes 131072 | tf_op jit(solution)/shard_map/gram/all_to_all | solution.py:336
  192.9 14.3 %all_to_all.21 = f32[32,8,256]{2,1,0:T(8,128)S(1)} all-to-all(f32[32,8,256]{2,1,0:T(8,128)S(1)} %broadcast_in_dim.40), channel_id=1, replica_groups=mesh['y'=4,'core'=2,'x'=4,'z'=8] {'y','core','x'}, dimensions={0} | all-to-all | bytes 524288 | tf_op jit(solution)/shard_map/gram/all_to_all | solution.py:336
  207.2 9.7 %factor_and_solve.1 = (f32[128,256]{1,0:T(8,128)}, f32[256,256]{1,0:T(8,128)}) custom-call(f32[256,256]{1,0:T(8,128)S(1)} %bitcast.30, f32[128,256]{1,0:T(8,128)S(1)} %fusion.4.rows), custom_call_target="tpu_custom_call" | custom-call | tf_op jit(solution)/shard_map/factor_and_solve/pallas_call | solution.py:321
  (25 shorter events, 0.3 us)
Async XLA Ops:
  1.6 8.4 %collective-permute-start.12 = (f32[128,256]{1,0:T(8,128)S(1)}, f32[128,256]{1,0:T(8,128)S(1)}, u32[]{:S(2)}, u32[]{:S(2)}) collective-permute-start(f32[128,256]{1,0:T(8,128)S(1)} %get-tuple-element.42.refs_0_), channel_id=1, source_target_pairs={{0,1},{1,2},{2,3},{3,4},{4,5},{5,6},{6,7},{7,0},{32,39},{33,32},{3... | collective-permute-start | bytes 393224 | tf_op jit(solution)/shard_map/gather/ppermute | solution.py:33
  8.1 8.0 %collective-permute-start.9 = (f32[128,256]{1,0:T(8,128)S(1)}, f32[128,256]{1,0:T(8,128)S(1)}, u32[]{:S(2)}, u32[]{:S(2)}) collective-permute-start(f32[128,256]{1,0:T(8,128)S(1)} %get-tuple-element.42.refs_0_), channel_id=1, source_target_pairs={{0,7},{1,0},{2,1},{3,2},{4,3},{5,4},{6,5},{7,6},{32,33},{33,34},{3... | collective-permute-start | bytes 393224 | tf_op jit(solution)/shard_map/gather/ppermute | solution.py:33
  10.1 6.0 %collective-permute-start.13 = (f32[128,256]{1,0:T(8,128)S(1)}, f32[128,256]{1,0:T(8,128)S(1)}, u32[]{:S(2)}, u32[]{:S(2)}) collective-permute-start(f32[128,256]{1,0:T(8,128)S(1)} %collective-permute-done.12.refs_7_), channel_id=1, source_target_pairs={{0,1},{1,2},{2,3},{3,4},{4,5},{5,6},{6,7},{7,0},{32,39},{33,32},{3... | collective-permute-start | bytes 393224 | tf_op jit(solution)/shard_map/gather/ppermute | solution.py:33
  13.6 6.2 %collective-permute-start.1 = (f32[128,256]{1,0:T(8,128)S(1)}, f32[128,256]{1,0:T(8,128)S(1)}, u32[]{:S(2)}, u32[]{:S(2)}) collective-permute-start(f32[128,256]{1,0:T(8,128)S(1)} %get-tuple-element.43.refs_0_), channel_id=1, source_target_pairs={{0,8},{8,16},{16,24},{24,0},{32,56},{40,32},{48,40},{56,48},{1,9},... | collective-permute-start | bytes 393224 | tf_op jit(solution)/shard_map/gather/ppermute | solution.py:33
  16.1 5.4 %collective-permute-start.10 = (f32[128,256]{1,0:T(8,128)S(1)}, f32[128,256]{1,0:T(8,128)S(1)}, u32[]{:S(2)}, u32[]{:S(2)}) collective-permute-start(f32[128,256]{1,0:T(8,128)S(1)} %collective-permute-done.9.refs_1_), channel_id=1, source_target_pairs={{0,7},{1,0},{2,1},{3,2},{4,3},{5,4},{6,5},{7,6},{32,33},{33,34},{3... | collective-permute-start | bytes 393224 | tf_op jit(solution)/shard_map/gather/ppermute | solution.py:33
  16.1 5.4 %collective-permute-start.14 = (f32[128,256]{1,0:T(8,128)S(1)}, f32[128,256]{1,0:T(8,128)S(1)}, u32[]{:S(2)}, u32[]{:S(2)}) collective-permute-start(f32[128,256]{1,0:T(8,128)S(1)} %collective-permute-done.13.refs_6_), channel_id=1, source_target_pairs={{0,1},{1,2},{2,3},{3,4},{4,5},{5,6},{6,7},{7,0},{32,39},{33,32},{3... | collective-permute-start | bytes 393224 | tf_op jit(solution)/shard_map/gather/ppermute | solution.py:33
  18.7 5.4 %collective-permute-start = (f32[128,256]{1,0:T(8,128)S(1)}, f32[128,256]{1,0:T(8,128)S(1)}, u32[]{:S(2)}, u32[]{:S(2)}) collective-permute-start(f32[128,256]{1,0:T(8,128)S(1)} %get-tuple-element.43.refs_0_), channel_id=1, source_target_pairs={{0,24},{8,0},{16,8},{24,16},{32,40},{40,48},{48,56},{56,32},{1,25}... | collective-permute-start | bytes 393224 | tf_op jit(solution)/shard_map/gather/ppermute | solution.py:33
  19.8 4.6 %collective-permute-start.2 = (f32[128,256]{1,0:T(8,128)S(1)}, f32[128,256]{1,0:T(8,128)S(1)}, u32[]{:S(2)}, u32[]{:S(2)}) collective-permute-start(f32[128,256]{1,0:T(8,128)S(1)} %collective-permute-done.1.refs_3_), channel_id=1, source_target_pairs={{0,8},{8,16},{16,24},{24,0},{32,56},{40,32},{48,40},{56,48},{1,9},... | collective-permute-start | bytes 393224 | tf_op jit(solution)/shard_map/gather/ppermute | solution.py:33
  21.4 5.3 %collective-permute-start.11 = (f32[128,256]{1,0:T(8,128)S(1)}, f32[128,256]{1,0:T(8,128)S(1)}, u32[]{:S(2)}, u32[]{:S(2)}) collective-permute-start(f32[128,256]{1,0:T(8,128)S(1)} %collective-permute-done.10.refs_2_), channel_id=1, source_target_pairs={{0,7},{1,0},{2,1},{3,2},{4,3},{5,4},{6,5},{7,6},{32,33},{33,34},{3... | collective-permute-start | bytes 393224 | tf_op jit(solution)/shard_map/gather/ppermute | solution.py:33
  21.4 5.6 %collective-permute-start.15 = (f32[128,256]{1,0:T(8,128)S(1)}, f32[128,256]{1,0:T(8,128)S(1)}, u32[]{:S(2)}, u32[]{:S(2)}) collective-permute-start(f32[128,256]{1,0:T(8,128)S(1)} %collective-permute-done.14.refs_5_), channel_id=1, source_target_pairs={{0,1},{1,2},{2,3},{3,4},{4,5},{5,6},{6,7},{7,0},{32,39},{33,32},{3... | collective-permute-start | bytes 393224 | tf_op jit(solution)/shard_map/gather/ppermute | solution.py:33
  24.5 8.6 %collective-permute-start.6 = (f32[512,256]{1,0:T(8,128)S(1)}, f32[512,256]{1,0:T(8,128)S(1)}, u32[]{:S(2)}, u32[]{:S(2)}) collective-permute-start(f32[512,256]{1,0:T(8,128)S(1)} %join.2.refs_0_), channel_id=1, source_target_pairs={{0,1},{1,2},{2,3},{3,4},{4,5},{5,6},{6,7},{7,0},{32,39},{33,32},{3... | collective-permute-start | bytes 1572872 | tf_op jit(solution)/shard_map/gather/ppermute | solution.py:33
  27.2 22.1 %collective-permute-start.17 = (f32[1024,256]{1,0:T(8,128)S(1)}, f32[1024,256]{1,0:T(8,128)}, u32[]{:S(2)}, u32[]{:S(2)}) collective-permute-start(f32[1024,256]{1,0:T(8,128)S(1)} %join.3.refs_7_), channel_id=1, source_target_pairs={{0,8},{8,16},{16,24},{24,0},{32,56},{40,32},{48,40},{56,48},{1,9},... | collective-permute-start | bytes 3145736 | tf_op jit(solution)/shard_map/gather/ppermute | solution.py:33
  28.2 14.8 %collective-permute-start.3 = (f32[512,256]{1,0:T(8,128)S(1)}, f32[512,256]{1,0:T(8,128)}, u32[]{:S(2)}, u32[]{:S(2)}) collective-permute-start(f32[512,256]{1,0:T(8,128)S(1)} %join.2.refs_0_), channel_id=1, source_target_pairs={{0,7},{1,0},{2,1},{3,2},{4,3},{5,4},{6,5},{7,6},{32,33},{33,34},{3... | collective-permute-start | bytes 1572872 | tf_op jit(solution)/shard_map/gather/ppermute | solution.py:33
  33.0 13.7 %collective-permute-start.7 = (f32[512,256]{1,0:T(8,128)S(1)}, f32[512,256]{1,0:T(8,128)}, u32[]{:S(2)}, u32[]{:S(2)}) collective-permute-start(f32[512,256]{1,0:T(8,128)S(1)} %collective-permute-done.6.refs_6_), channel_id=1, source_target_pairs={{0,1},{1,2},{2,3},{3,4},{4,5},{5,6},{6,7},{7,0},{32,39},{33,32},{3... | collective-permute-start | bytes 1572872 | tf_op jit(solution)/shard_map/gather/ppermute | solution.py:33
  43.0 14.3 %collective-permute-start.4 = (f32[512,256]{1,0:T(8,128)}, f32[512,256]{1,0:T(8,128)}, u32[]{:S(2)}, u32[]{:S(2)}) collective-permute-start(f32[512,256]{1,0:T(8,128)} %collective-permute-done.3.refs_1_), channel_id=1, source_target_pairs={{0,7},{1,0},{2,1},{3,2},{4,3},{5,4},{6,5},{7,6},{32,33},{33,34},{3... | collective-permute-start | bytes 1572872 | tf_op jit(solution)/shard_map/gather/ppermute | solution.py:33
  46.7 13.8 %collective-permute-start.8 = (f32[512,256]{1,0:T(8,128)}, f32[512,256]{1,0:T(8,128)}, u32[]{:S(2)}, u32[]{:S(2)}) collective-permute-start(f32[512,256]{1,0:T(8,128)} %collective-permute-done.7.refs_5_), channel_id=1, source_target_pairs={{0,1},{1,2},{2,3},{3,4},{4,5},{5,6},{6,7},{7,0},{32,39},{33,32},{3... | collective-permute-start | bytes 1572872 | tf_op jit(solution)/shard_map/gather/ppermute | solution.py:33
  48.0 19.2 %collective-permute-start.16 = (f32[1024,256]{1,0:T(8,128)S(1)}, f32[1024,256]{1,0:T(8,128)}, u32[]{:S(2)}, u32[]{:S(2)}) collective-permute-start(f32[1024,256]{1,0:T(8,128)S(1)} %join.3.refs_7_), channel_id=1, source_target_pairs={{0,24},{8,0},{16,8},{24,16},{32,40},{40,48},{48,56},{56,32},{1,25}... | collective-permute-start | bytes 3145736 | tf_op jit(solution)/shard_map/gather/ppermute | solution.py:33
  49.3 26.0 %collective-permute-start.19 = (f32[1024,256]{1,0:T(8,128)}, f32[1024,256]{1,0:T(8,128)S(1)}, u32[]{:S(2)}, u32[]{:S(2)}) collective-permute-start(f32[1024,256]{1,0:T(8,128)} %collective-permute-done.17.refs_9_), channel_id=1, source_target_pairs={{0,8},{8,16},{16,24},{24,0},{32,56},{40,32},{48,40},{56,48},{1,9},... | collective-permute-start | bytes 3145736 | tf_op jit(solution)/shard_map/gather/ppermute | solution.py:33
  57.3 15.2 %collective-permute-start.5 = (f32[512,256]{1,0:T(8,128)}, f32[512,256]{1,0:T(8,128)S(1)}, u32[]{:S(2)}, u32[]{:S(2)}) collective-permute-start(f32[512,256]{1,0:T(8,128)} %collective-permute-done.4.refs_2_), channel_id=1, source_target_pairs={{0,7},{1,0},{2,1},{3,2},{4,3},{5,4},{6,5},{7,6},{32,33},{33,34},{3... | collective-permute-start | bytes 1572872 | tf_op jit(solution)/shard_map/gather/ppermute | solution.py:33
  60.5 14.7 %collective-permute-start.18 = (f32[512,256]{1,0:T(8,128)}, f32[512,256]{1,0:T(8,128)S(1)}, u32[]{:S(2)}, u32[]{:S(2)}) collective-permute-start(f32[512,256]{1,0:T(8,128)} %collective-permute-done.8.refs_4_), channel_id=1, source_target_pairs={{0,1},{1,2},{2,3},{3,4},{4,5},{5,6},{6,7},{7,0},{32,39},{33,32},{3... | collective-permute-start | bytes 1572872 | tf_op jit(solution)/shard_map/gather/ppermute | solution.py:33
  63.7 0.7 copy-start
  75.4 21.4 %collective-permute-start.20 = (f32[8192,256]{1,0:T(8,128)S(1)}, f32[8192,256]{1,0:T(8,128)S(1)}, u32[]{:S(2)}, u32[]{:S(2)}) collective-permute-start(f32[8192,256]{1,0:T(8,128)S(1)} %place.3.panels), channel_id=1, source_target_pairs={{0,32},{32,0},{1,33},{33,1},{2,34},{34,2},{3,35},{35,3},{4,36},{36... | collective-permute-start | bytes 25165832 | tf_op jit(solution)/shard_map/gather/ppermute | solution.py:37
  101.3 20.2 %collective-permute-start.22 = (f32[8,128,256]{2,1,0:T(8,128)S(1)}, f32[8,128,256]{2,1,0:T(8,128)S(1)}, u32[]{:S(2)}, u32[]{:S(2)}) collective-permute-start(f32[8,128,256]{2,1,0:T(8,128)S(1)} %slot_products.5), channel_id=1, source_target_pairs={{0,8},{8,16},{16,24},{24,0},{32,56},{40,32},{48,40},{56,48},{1,9},... | collective-permute-start | bytes 3145736 | tf_op jit(solution)/shard_map/scatter_rows/ppermute | solution.py:33
  109.6 21.5 %collective-permute-start.21 = (f32[8,128,256]{2,1,0:T(8,128)S(1)}, f32[8,128,256]{2,1,0:T(8,128)S(1)}, u32[]{:S(2)}, u32[]{:S(2)}) collective-permute-start(f32[8,128,256]{2,1,0:T(8,128)S(1)} %get-tuple-element.27), channel_id=1, source_target_pairs={{0,24},{8,0},{16,8},{24,16},{32,40},{40,48},{48,56},{56,32},{1,25}... | collective-permute-start | bytes 3145736 | tf_op jit(solution)/shard_map/scatter_rows/ppermute | solution.py:33
  121.6 16.2 %collective-permute-start.23 = (f32[8,128,256]{2,1,0:T(8,128)S(1)}, f32[8,128,256]{2,1,0:T(8,128)S(1)}, u32[]{:S(2)}, u32[]{:S(2)}) collective-permute-start(f32[8,128,256]{2,1,0:T(8,128)S(1)} %add.123), channel_id=1, source_target_pairs={{0,8},{8,16},{16,24},{24,0},{32,56},{40,32},{48,40},{56,48},{1,9},... | collective-permute-start | bytes 3145736 | tf_op jit(solution)/shard_map/scatter_rows/ppermute | solution.py:33
  138.0 3.9 %collective-permute-start.24 = (f32[128,256]{1,0:T(8,128)S(1)}, f32[128,256]{1,0:T(8,128)S(1)}, u32[]{:S(2)}, u32[]{:S(2)}) collective-permute-start(f32[128,256]{1,0:T(8,128)S(1)} %get-tuple-element.41), channel_id=1, source_target_pairs={{0,1},{1,2},{2,3},{3,4},{4,5},{5,6},{6,7},{7,0},{32,39},{33,32},{3... | collective-permute-start | bytes 393224 | tf_op jit(solution)/shard_map/scatter_rows/ppermute | solution.py:33
  141.9 7.5 %collective-permute-start.25 = (f32[2,128,256]{2,1,0:T(8,128)S(1)}, f32[2,128,256]{2,1,0:T(8,128)S(1)}, u32[]{:S(2)}, u32[]{:S(2)}) collective-permute-start(f32[2,128,256]{2,1,0:T(8,128)S(1)} %pad_maximum_fusion), channel_id=1, source_target_pairs={{0,2},{1,3},{2,4},{3,5},{4,6},{5,7},{6,0},{7,1},{32,38},{33,39},{3... | collective-permute-start | bytes 786440 | tf_op jit(solution)/shard_map/scatter_rows/ppermute | solution.py:33
  142.0 7.7 %collective-permute-start.26 = (f32[2,128,256]{2,1,0:T(8,128)S(1)}, f32[2,128,256]{2,1,0:T(8,128)S(1)}, u32[]{:S(2)}, u32[]{:S(2)}) collective-permute-start(f32[2,128,256]{2,1,0:T(8,128)S(1)} %slice.56), channel_id=1, source_target_pairs={{0,6},{1,7},{2,0},{3,1},{4,2},{5,3},{6,4},{7,5},{32,34},{33,35},{3... | collective-permute-start | bytes 786440 | tf_op jit(solution)/shard_map/scatter_rows/ppermute | solution.py:33
  149.8 12.5 %collective-permute-start.27 = (f32[128,256]{1,0:T(8,128)S(1)}, f32[128,256]{1,0:T(8,128)S(1)}, u32[]{:S(2)}, u32[]{:S(2)}) collective-permute-start(f32[128,256]{1,0:T(8,128)S(1)} %get-tuple-element.32), channel_id=1, source_target_pairs={{0,1},{1,2},{2,3},{3,4},{4,5},{5,6},{6,7},{7,0},{32,39},{33,32},{3... | collective-permute-start | bytes 393224 | tf_op jit(solution)/shard_map/scatter_rows/ppermute | solution.py:33
  159.6 5.0 %collective-permute-start.28 = (f32[128,256]{1,0:T(8,128)S(1)}, f32[128,256]{1,0:T(8,128)S(1)}, u32[]{:S(2)}, u32[]{:S(2)}) collective-permute-start(f32[128,256]{1,0:T(8,128)S(1)} %get-tuple-element.33), channel_id=1, source_target_pairs={{0,7},{1,0},{2,1},{3,2},{4,3},{5,4},{6,5},{7,6},{32,33},{33,34},{3... | collective-permute-start | bytes 393224 | tf_op jit(solution)/shard_map/scatter_rows/ppermute | solution.py:33
where the time goes:
time: 218 us; the launch traced here: 217 us
  waiting for transfers between devices  81.6 us (37%)
  starting transfers between devices  54.5 us (25%)
  blocking collectives  42 us (19%)
  Pallas kernels  33.7 us (15%)
    ppermute x28, waiting for transfers between devices, shift(): return lax.ppermute(value, ('core', axis), pairs)  74.9 us
    ppermute x28, starting transfers between devices, shift(): return lax.ppermute(value, ('core', axis), pairs)  45.9 us
    all_to_all x3, blocking collectives, exchange(): return lax.all_to_all(value, axes, 0, 0, tiled=True)  42 us
    pallas_call x3, Pallas kernels, slot_products(): pl.pallas_call(functools.partial(products_kernel, part), out_shape=shapes...  18.2 us
    pallas_call x1, Pallas kernels, factor_and_solve(): pl.pallas_call(factor_kernel, out_shape=[jax.ShapeDtypeStruct((EDGE, WIDT...  9.67 us
    ppermute x1, starting transfers between devices, swap(): return lax.ppermute(value, 'core', [(0, 1), (1, 0)])  8.61 us
    ppermute x1, waiting for transfers between devices, swap(): return lax.ppermute(value, 'core', [(0, 1), (1, 0)])  6.71 us
  transfers between devices with their start and end apart: 29, of which 19 were waited for; matrix products, arithmetic and copies ran while one was open for 1% of the time, Pallas kernels for 9%

commit v1 on v0

--- a/solution.py
+++ b/solution.py
@@ -46,6 +46,8 @@
         ahead = shift(ahead, axis, -1)
         found[count - step] = behind
         found[step] = ahead
+    behind, ahead = lax.optimization_barrier((behind, ahead))
+    found[count // 2 + 1], found[count // 2 - 1] = behind, ahead
     found[count // 2] = shift(behind, axis, 1)
     return found
 
@@ -356,7 +358,7 @@
     )
     ahead = ((target // 8 - here_x) * here_facing) % 4
     chunk = jnp.where(ahead == 3, 1, jnp.where(ahead == 0, 0, ahead + 1))
-    row = chunk * 8 + ((target % 8 - here_z) * here_facing) % 8
+    row = chunk * 8 + target % 8
     kind = jnp.where(side == 0, 0, jnp.where(row >= FAR_ROW, 1, 2))
 
     with jax.named_scope("gather"):
@@ -386,13 +388,7 @@
         passing = shift(far, "x", 1)
         from_ahead = shift(behind, "x", -1)
         own = own + from_ahead + shift(ahead + passing, "x", 1)
-        passing = shift(own[4], "z", 1)
-        ahead = jnp.stack([own[2], own[3] + passing])
-        ahead, behind = lax.optimization_barrier((ahead, own[5:7]))
-        ahead, behind = shift(ahead, "z", 2), shift(behind, "z", -2)
-        middle = own[0] + ahead[0] + behind[1]
-        ahead, behind = lax.optimization_barrier((own[1] + ahead[1], own[7] + behind[0]))
-        product_rows = middle + shift(ahead, "z", 1) + shift(behind, "z", -1)
+        product_rows = jnp.sum(exchange(own, "z"), axis=0)
 
     with jax.named_scope("gram"):
         gram = jnp.dot(

time: 218 us -> 223 us (1.023)
  blocking collectives: 42 us -> 75 us
  starting transfers between devices: 54.5 us -> 38.6 us
  waiting for transfers between devices: 81.6 us -> 66.2 us
  local copies, waits for them, and re-layouts: 1.71 us -> 5.79 us
    all_to_all x3 -> x4, blocking collectives: 42 us -> 75 us  [exchange(): return lax.all_to_all(value, axes, 0, 0, tiled=True)]
    ppermute x28 -> x23, waiting for transfers between devices: 74.9 us -> 58.9 us  [shift(): return lax.ppermute(value, ('core', axis), pairs)]
    ppermute x28 -> x23, starting transfers between devices: 45.9 us -> 33.9 us  [shift(): return lax.ppermute(value, ('core', axis), pairs)]
    unnamed x2 -> x10, local copies, waits for them, and re-layouts: 0.65 us -> 4.69 us
    ppermute x1, starting transfers between devices: 8.61 us -> 4.73 us  [swap(): return lax.ppermute(value, 'core', [(0, 1), (1, 0)])]
  transfers between devices with their start and end apart: 29 -> 24, of which waited for: 19 -> 16; matrix products, arithmetic and copies ran while one was open for 1% -> 1% of each run, Pallas kernels for 9% -> 9%
where the time goes in v1:
time: 223 us
  blocking collectives  75 us (34%)
  waiting for transfers between devices  66.2 us (30%)
  starting transfers between devices  38.6 us (17%)
  Pallas kernels  33.7 us (15%)
  local copies, waits for them, and re-layouts  5.79 us (3%)
    all_to_all x4, blocking collectives, exchange(): return lax.all_to_all(value, axes, 0, 0, tiled=True)  75 us
    ppermute x23, waiting for transfers between devices, shift(): return lax.ppermute(value, ('core', axis), pairs)  58.9 us
    ppermute x23, starting transfers between devices, shift(): return lax.ppermute(value, ('core', axis), pairs)  33.9 us
    pallas_call x3, Pallas kernels, slot_products(): pl.pallas_call(functools.partial(products_kernel, part), out_shape=shapes...  18.6 us
    pallas_call x1, Pallas kernels, factor_and_solve(): pl.pallas_call(factor_kernel, out_shape=[jax.ShapeDtypeStruct((EDGE, WIDT...  9.67 us
    ppermute x1, waiting for transfers between devices, swap(): return lax.ppermute(value, 'core', [(0, 1), (1, 0)])  7.3 us
    ppermute x1, starting transfers between devices, swap(): return lax.ppermute(value, 'core', [(0, 1), (1, 0)])  4.73 us
    unnamed x10, local copies, waits for them, and re-layouts  4.69 us
  transfers between devices with their start and end apart: 24, of which 16 were waited for; matrix products, arithmetic and copies ran while one was open for 1% of the time, Pallas kernels for 9%

profile of v1, /device:TPU:1, one launch (start us, length us, event | category | flops | bytes accessed | tf_op | source)
XLA Modules:
  0.0 222.6 jit_solution(12487933090521333933)
XLA Ops:
  0.6 1.0 constant_dynamic-slice_fusion.1
  1.6 6.5 %collective-permute-start.11 = (f32[128,256]{1,0:T(8,128)S(1)}, f32[128,256]{1,0:T(8,128)S(1)}, u32[]{:S(2)}, u32[]{:S(2)}) collective-permute-start(f32[128,256]{1,0:T(8,128)S(1)} %get-tuple-element.46.refs_0_), channel_id=1, source_target_pairs={{0,1},{1,2},{2,3},{3,4},{4,5},{5,6},{6,7},{7,0},{32,39},{33,32},{3... | collective-permute-start | bytes 393224 | tf_op jit(solution)/shard_map/gather/ppermute | solution.py:33
  8.1 1.9 collective-permute-done.11.refs_7_
  10.1 3.5 %collective-permute-start.12 = (f32[128,256]{1,0:T(8,128)S(1)}, f32[128,256]{1,0:T(8,128)S(1)}, u32[]{:S(2)}, u32[]{:S(2)}) collective-permute-start(f32[128,256]{1,0:T(8,128)S(1)} %collective-permute-done.11.refs_7_), channel_id=1, source_target_pairs={{0,1},{1,2},{2,3},{3,4},{4,5},{5,6},{6,7},{7,0},{32,39},{33,32},{3... | collective-permute-start | bytes 393224 | tf_op jit(solution)/shard_map/gather/ppermute | solution.py:33
  13.6 2.5 %collective-permute-start = (f32[128,256]{1,0:T(8,128)S(1)}, f32[128,256]{1,0:T(8,128)S(1)}, u32[]{:S(2)}, u32[]{:S(2)}) collective-permute-start(f32[128,256]{1,0:T(8,128)S(1)} %get-tuple-element.47.refs_0_), channel_id=1, source_target_pairs={{0,8},{8,16},{16,24},{24,0},{32,56},{40,32},{48,40},{56,48},{1,9},... | collective-permute-start | bytes 393224 | tf_op jit(solution)/shard_map/gather/ppermute | solution.py:33
  16.1 2.7 %collective-permute-start.13 = (f32[128,256]{1,0:T(8,128)S(1)}, f32[128,256]{1,0:T(8,128)S(1)}, u32[]{:S(2)}, u32[]{:S(2)}) collective-permute-start(f32[128,256]{1,0:T(8,128)S(1)} %collective-permute-done.12.refs_6_), channel_id=1, source_target_pairs={{0,1},{1,2},{2,3},{3,4},{4,5},{5,6},{6,7},{7,0},{32,39},{33,32},{3... | collective-permute-start | bytes 393224 | tf_op jit(solution)/shard_map/gather/ppermute | solution.py:33
  18.8 0.2 collective-permute-done.10.refs_2_
  18.9 3.7 %collective-permute-done.1.refs_1_ = f32[128,256]{1,0:T(8,128)S(1)} collective-permute-done((f32[128,256]{1,0:T(8,128)S(1)}, f32[128,256]{1,0:T(8,128)S(1)}, u32[]{:S(2)}, u32[]{:S(2)}) %collective-permute-start.1) | collective-permute-done | bytes 131104 | tf_op jit(solution)/shard_map/gather/ppermute | solution.py:33
  22.6 0.0 collective-permute-start.2
  22.6 0.0 collective-permute-done.13.refs_5_
  22.6 2.7 %collective-permute-done.14.refs_3_ = f32[128,256]{1,0:T(8,128)S(1)} collective-permute-done((f32[128,256]{1,0:T(8,128)S(1)}, f32[128,256]{1,0:T(8,128)S(1)}, u32[]{:S(2)}, u32[]{:S(2)}) %collective-permute-start.14) | collective-permute-done | bytes 131104 | tf_op jit(solution)/shard_map/gather/ppermute | solution.py:33
  25.3 0.0 collective-permute-start.15
  25.3 1.1 collective-permute-done.2.refs_2_
  26.5 1.5 collective-permute-start.5
  28.0 0.0 collective-permute-start.3
  28.0 1.1 collective-permute-done.15.refs_4_
  29.1 0.1 join.3.refs_7_
  29.2 2.9 %collective-permute-start.16 = (f32[1024,256]{1,0:T(8,128)S(1)}, f32[1024,256]{1,0:T(8,128)}, u32[]{:S(2)}, u32[]{:S(2)}) collective-permute-start(f32[1024,256]{1,0:T(8,128)S(1)} %join.3.refs_7_), channel_id=1, source_target_pairs={{0,8},{8,16},{16,24},{24,0},{32,56},{40,32},{48,40},{56,48},{1,9},... | collective-permute-start | bytes 3145736 | tf_op jit(solution)/shard_map/gather/ppermute | solution.py:33
  32.1 3.7 %collective-permute-done.5.refs_6_ = f32[512,256]{1,0:T(8,128)S(1)} collective-permute-done((f32[512,256]{1,0:T(8,128)S(1)}, f32[512,256]{1,0:T(8,128)S(1)}, u32[]{:S(2)}, u32[]{:S(2)}) %collective-permute-start.5) | collective-permute-done | bytes 524320 | tf_op jit(solution)/shard_map/gather/ppermute | solution.py:33
  35.8 2.6 %collective-permute-start.6 = (f32[512,256]{1,0:T(8,128)S(1)}, f32[512,256]{1,0:T(8,128)}, u32[]{:S(2)}, u32[]{:S(2)}) collective-permute-start(f32[512,256]{1,0:T(8,128)S(1)} %collective-permute-done.5.refs_6_), channel_id=1, source_target_pairs={{0,1},{1,2},{2,3},{3,4},{4,5},{5,6},{6,7},{7,0},{32,39},{33,32},{3... | collective-permute-start | bytes 1572872 | tf_op jit(solution)/shard_map/gather/ppermute | solution.py:33
  38.4 3.1 %collective-permute-done.3.refs_1_ = f32[512,256]{1,0:T(8,128)S(1)} collective-permute-done((f32[512,256]{1,0:T(8,128)S(1)}, f32[512,256]{1,0:T(8,128)S(1)}, u32[]{:S(2)}, u32[]{:S(2)}) %collective-permute-start.3) | collective-permute-done | bytes 524320 | tf_op jit(solution)/shard_map/gather/ppermute | solution.py:33
  41.4 0.0 collective-permute-start.4
  41.4 0.8 copy-done.2
  42.2 4.1 %collective-permute-done.6.refs_5_ = f32[512,256]{1,0:T(8,128)} collective-permute-done((f32[512,256]{1,0:T(8,128)S(1)}, f32[512,256]{1,0:T(8,128)}, u32[]{:S(2)}, u32[]{:S(2)}) %collective-permute-start.6) | collective-permute-done | bytes 524320 | tf_op jit(solution)/shard_map/gather/ppermute | solution.py:33
  46.4 2.5 %collective-permute-start.7 = (f32[512,256]{1,0:T(8,128)}, f32[512,256]{1,0:T(8,128)}, u32[]{:S(2)}, u32[]{:S(2)}) collective-permute-start(f32[512,256]{1,0:T(8,128)} %collective-permute-done.6.refs_5_), channel_id=1, source_target_pairs={{0,1},{1,2},{2,3},{3,4},{4,5},{5,6},{6,7},{7,0},{32,39},{33,32},{3... | collective-permute-start | bytes 1572872 | tf_op jit(solution)/shard_map/gather/ppermute | solution.py:33
  48.9 5.2 %collective-permute-done.4.refs_2_ = f32[512,256]{1,0:T(8,128)} collective-permute-done((f32[512,256]{1,0:T(8,128)S(1)}, f32[512,256]{1,0:T(8,128)}, u32[]{:S(2)}, u32[]{:S(2)}) %collective-permute-start.4) | collective-permute-done | bytes 524320 | tf_op jit(solution)/shard_map/gather/ppermute | solution.py:33
  54.1 0.0 collective-permute-start.8
  54.1 0.0 collective-permute-done.16.refs_9_
  54.1 3.5 %collective-permute-done.17.refs_8_ = f32[1024,256]{1,0:T(8,128)S(1)} collective-permute-done((f32[1024,256]{1,0:T(8,128)S(1)}, f32[1024,256]{1,0:T(8,128)S(1)}, u32[]{:S(2)}, u32[]{:S(2)}) %collective-permute-start.17) | collective-permute-done | bytes 1048608 | tf_op jit(solution)/shard_map/gather/ppermute | solution.py:33
  57.5 1.0 copy-done
  58.5 1.2 collective-permute-start.19
  59.7 0.0 collective-permute-done.7.refs_4_
  59.7 6.3 %collective-permute-done.8.refs_3_ = f32[512,256]{1,0:T(8,128)} collective-permute-done((f32[512,256]{1,0:T(8,128)}, f32[512,256]{1,0:T(8,128)}, u32[]{:S(2)}, u32[]{:S(2)}) %collective-permute-start.8) | collective-permute-done | bytes 524320 | tf_op jit(solution)/shard_map/gather/ppermute | solution.py:33
  66.0 0.2 collective-permute-start.18
  66.1 0.8 select_reduce_fusion
  66.9 0.7 compare_select_fusion.8
  67.7 0.0 copy-start.4
  67.7 0.6 copy-done.4
  68.3 2.8 %slot_plan.1 = (s32[192]{0:T(256)S(1)}, s32[192]{0:T(256)S(1)}, s32[192]{0:T(256)S(1)}, s32[3]{0:T(128)S(1)}) custom-call(s32[32]{0:T(128)S(1)} %bitcast.15, s32[192]{0:T(256)S(1)} %get-tuple-element.44.kind), custom_call_target="tpu_custom_call" | custom-call | bytes 12582912 | tf_op jit(solution)/shard_map/gather/slot_plan/pallas_call | solution.py:129
  71.2 1.2 copy-done.1
  72.4 1.0 copy-done.3
  73.4 2.4 %place.2.refs_0_ = f32[8192,256]{1,0:T(8,128)S(1)} custom-call(f32[512,256]{1,0:T(8,128)S(1)} %join.2.refs_0_, f32[512,256]{1,0:T(8,128)S(1)} %copy-done.3, f32[512,256]{1,0:T(8,128)} %collective-permute-done.4.refs_2_, f32[512,256]{1,0:T(8,128)} %collective-permute-done.8.refs_3_, f32[512,256]{1,0:T(8,128)} %collective-permute-done.7.refs_4_, ...), custom_call_target="tpu_custom_call" | custom-call | bytes 13631488 | tf_op jit(solution)/shard_map/gather/place/pallas_call | solution.py:96
  75.9 0.1 place.3.panels
  76.0 4.7 %collective-permute-start.20 = (f32[8192,256]{1,0:T(8,128)S(1)}, f32[8192,256]{1,0:T(8,128)S(1)}, u32[]{:S(2)}, u32[]{:S(2)}) collective-permute-start(f32[8192,256]{1,0:T(8,128)S(1)} %place.3.panels), channel_id=1, source_target_pairs={{0,32},{32,0},{1,33},{33,1},{2,34},{34,2},{3,35},{35,3},{4,36},{36... | collective-permute-start | bytes 25165832 | tf_op jit(solution)/shard_map/gather/ppermute | solution.py:37
  80.8 5.5 %slot_products.3.refs_0_ = f32[32,128,256]{2,1,0:T(8,128)S(1)} custom-call(s32[3]{0:T(128)S(1)} %get-tuple-element.28.counts, s32[192]{0:T(256)S(1)} %get-tuple-element.37.listed, s32[192]{0:T(256)S(1)} %get-tuple-element.42.blk, s32[192]{0:T(256)S(1)} %get-tuple-element.45.row, f32[192,128,128]{2,1,0:T(8,128)} %bitcast.16, f32[8192,256]{1,0:T(8,128)S(1)} %place.3.panels), custom_call_target="tpu_custom_call" | custom-call | flops 3221225472 | bytes 12582912 | tf_op jit(solution)/shard_map/slot_products/pallas_call | solution.py:219
  86.2 7.3 %collective-permute-done.20.panels = f32[8192,256]{1,0:T(8,128)S(1)} collective-permute-done((f32[8192,256]{1,0:T(8,128)S(1)}, f32[8192,256]{1,0:T(8,128)S(1)}, u32[]{:S(2)}, u32[]{:S(2)}) %collective-permute-start.20) | collective-permute-done | bytes 8388640 | tf_op jit(solution)/shard_map/gather/ppermute | solution.py:37
  93.5 4.9 %slot_products.5 = f32[8,128,256]{2,1,0:T(8,128)S(1)} custom-call(s32[3]{0:T(128)S(1)} %get-tuple-element.28.counts, s32[192]{0:T(256)S(1)} %get-tuple-element.41.listed, s32[192]{0:T(256)S(1)} %get-tuple-element.42.blk, s32[192]{0:T(256)S(1)} %get-tuple-element.45.row, f32[192,128,128]{2,1,0:T(8,128)} %bitcast.17, ...), custom_call_target="tpu_custom_call" | custom-call | flops 805306368 | bytes 3145728 | tf_op jit(solution)/shard_map/slot_products/pallas_call | solution.py:219
  98.5 4.3 %collective-permute-start.22 = (f32[8,128,256]{2,1,0:T(8,128)S(1)}, f32[8,128,256]{2,1,0:T(8,128)S(1)}, u32[]{:S(2)}, u32[]{:S(2)}) collective-permute-start(f32[8,128,256]{2,1,0:T(8,128)S(1)} %slot_products.5), channel_id=1, source_target_pairs={{0,8},{8,16},{16,24},{24,0},{32,56},{40,32},{48,40},{56,48},{1,9},... | collective-permute-start | bytes 3145736 | tf_op jit(solution)/shard_map/scatter_rows/ppermute | solution.py:33
  102.8 8.2 %slot_products.4 = (f32[8,128,256]{2,1,0:T(8,128)S(1)}, f32[8,128,256]{2,1,0:T(8,128)S(1)}, f32[8,128,256]{2,1,0:T(8,128)S(1)}) custom-call(s32[3]{0:T(128)S(1)} %get-tuple-element.28.counts, s32[192]{0:T(256)S(1)} %get-tuple-element.29.listed, s32[192]{0:T(256)S(1)} %get-tuple-element.42.blk, s32[192]{0:T(256)S(1)} %get-tuple-element.45.row, ...), custom_call_target="tpu_custom_call" | custom-call | flops 2415919104 | bytes 9437184 | tf_op jit(solution)/shard_map/slot_products/pallas_call | solution.py:219
  111.0 0.1 collective-permute-start.21
  111.1 9.8 %collective-permute-done.22 = f32[8,128,256]{2,1,0:T(8,128)S(1)} collective-permute-done((f32[8,128,256]{2,1,0:T(8,128)S(1)}, f32[8,128,256]{2,1,0:T(8,128)S(1)}, u32[]{:S(2)}, u32[]{:S(2)}) %collective-permute-start.22) | collective-permute-done | bytes 1048608 | tf_op jit(solution)/shard_map/scatter_rows/ppermute | solution.py:33
  120.8 0.1 add.87
  121.0 3.5 %collective-permute-start.23 = (f32[8,128,256]{2,1,0:T(8,128)S(1)}, f32[8,128,256]{2,1,0:T(8,128)S(1)}, u32[]{:S(2)}, u32[]{:S(2)}) collective-permute-start(f32[8,128,256]{2,1,0:T(8,128)S(1)} %add.87), channel_id=1, source_target_pairs={{0,8},{8,16},{16,24},{24,0},{32,56},{40,32},{48,40},{56,48},{1,9},... | collective-permute-start | bytes 3145736 | tf_op jit(solution)/shard_map/scatter_rows/ppermute | solution.py:33
  124.5 7.0 %collective-permute-done.21 = f32[8,128,256]{2,1,0:T(8,128)S(1)} collective-permute-done((f32[8,128,256]{2,1,0:T(8,128)S(1)}, f32[8,128,256]{2,1,0:T(8,128)S(1)}, u32[]{:S(2)}, u32[]{:S(2)}) %collective-permute-start.21) | collective-permute-done | bytes 1048608 | tf_op jit(solution)/shard_map/scatter_rows/ppermute | solution.py:33
  131.5 5.5 %collective-permute-done.23 = f32[8,128,256]{2,1,0:T(8,128)S(1)} collective-permute-done((f32[8,128,256]{2,1,0:T(8,128)S(1)}, f32[8,128,256]{2,1,0:T(8,128)S(1)}, u32[]{:S(2)}, u32[]{:S(2)}) %collective-permute-start.23) | collective-permute-done | bytes 1048608 | tf_op jit(solution)/shard_map/scatter_rows/ppermute | solution.py:33
  137.0 0.2 add_add_fusion
  137.2 36.0 %all_to_all.21 = f32[8,128,256]{2,1,0:T(8,128)S(1)} all-to-all(f32[8,128,256]{2,1,0:T(8,128)S(1)} %add_add_fusion), channel_id=1, replica_groups=mesh['y'=4,'core'=2,'x'=4,'z'=8] {'z'}, dimensions={0} | all-to-all | bytes 2097152 | tf_op jit(solution)/shard_map/scatter_rows/all_to_all | solution.py:338
  173.2 0.1 reduce_sum.37.rows
  173.3 0.1 copy.11
  173.4 0.4 fusion
  173.7 15.5 %all_to_all.22 = f32[32,8,256]{2,1,0:T(8,128)S(1)} all-to-all(f32[32,8,256]{2,1,0:T(8,128)S(1)} %fusion), channel_id=1, replica_groups=mesh['y'=4,'core'=2,'x'=4,'z'=8] {'y','core','x'}, dimensions={0} | all-to-all | bytes 524288 | tf_op jit(solution)/shard_map/gram/all_to_all | solution.py:338
  189.3 9.5 %all_to_all.23 = f32[8,8,256]{2,1,0:T(8,128)S(1)} all-to-all(f32[8,8,256]{2,1,0:T(8,128)S(1)} %broadcast_in_dim.39), channel_id=1, replica_groups=mesh['y'=4,'core'=2,'x'=4,'z'=8] {'z'}, dimensions={0} | all-to-all | bytes 131072 | tf_op jit(solution)/shard_map/gram/all_to_all | solution.py:338
  198.8 14.0 %all_to_all.24 = f32[32,8,256]{2,1,0:T(8,128)S(1)} all-to-all(f32[32,8,256]{2,1,0:T(8,128)S(1)} %broadcast_in_dim.40), channel_id=1, replica_groups=mesh['y'=4,'core'=2,'x'=4,'z'=8] {'y','core','x'}, dimensions={0} | all-to-all | bytes 524288 | tf_op jit(solution)/shard_map/gram/all_to_all | solution.py:338
  212.9 9.7 %factor_and_solve.1 = (f32[128,256]{1,0:T(8,128)}, f32[256,256]{1,0:T(8,128)}) custom-call(f32[256,256]{1,0:T(8,128)S(1)} %bitcast.14, f32[128,256]{1,0:T(8,128)S(1)} %reduce_sum.37.rows), custom_call_target="tpu_custom_call" | custom-call | tf_op jit(solution)/shard_map/factor_and_solve/pallas_call | solution.py:323
  (20 shorter events, 0.2 us)
Async XLA Ops:
  1.6 8.4 %collective-permute-start.11 = (f32[128,256]{1,0:T(8,128)S(1)}, f32[128,256]{1,0:T(8,128)S(1)}, u32[]{:S(2)}, u32[]{:S(2)}) collective-permute-start(f32[128,256]{1,0:T(8,128)S(1)} %get-tuple-element.46.refs_0_), channel_id=1, source_target_pairs={{0,1},{1,2},{2,3},{3,4},{4,5},{5,6},{6,7},{7,0},{32,39},{33,32},{3... | collective-permute-start | bytes 393224 | tf_op jit(solution)/shard_map/gather/ppermute | solution.py:33
  8.1 5.5 %collective-permute-start.9 = (f32[128,256]{1,0:T(8,128)S(1)}, f32[128,256]{1,0:T(8,128)S(1)}, u32[]{:S(2)}, u32[]{:S(2)}) collective-permute-start(f32[128,256]{1,0:T(8,128)S(1)} %get-tuple-element.46.refs_0_), channel_id=1, source_target_pairs={{0,7},{1,0},{2,1},{3,2},{4,3},{5,4},{6,5},{7,6},{32,33},{33,34},{3... | collective-permute-start | bytes 393224 | tf_op jit(solution)/shard_map/gather/ppermute | solution.py:33
  10.1 6.0 %collective-permute-start.12 = (f32[128,256]{1,0:T(8,128)S(1)}, f32[128,256]{1,0:T(8,128)S(1)}, u32[]{:S(2)}, u32[]{:S(2)}) collective-permute-start(f32[128,256]{1,0:T(8,128)S(1)} %collective-permute-done.11.refs_7_), channel_id=1, source_target_pairs={{0,1},{1,2},{2,3},{3,4},{4,5},{5,6},{6,7},{7,0},{32,39},{33,32},{3... | collective-permute-start | bytes 393224 | tf_op jit(solution)/shard_map/gather/ppermute | solution.py:33
  13.6 5.3 %collective-permute-start.10 = (f32[128,256]{1,0:T(8,128)S(1)}, f32[128,256]{1,0:T(8,128)S(1)}, u32[]{:S(2)}, u32[]{:S(2)}) collective-permute-start(f32[128,256]{1,0:T(8,128)S(1)} %collective-permute-done.9.refs_1_), channel_id=1, source_target_pairs={{0,7},{1,0},{2,1},{3,2},{4,3},{5,4},{6,5},{7,6},{32,33},{33,34},{3... | collective-permute-start | bytes 393224 | tf_op jit(solution)/shard_map/gather/ppermute | solution.py:33
  13.6 5.3 %collective-permute-start = (f32[128,256]{1,0:T(8,128)S(1)}, f32[128,256]{1,0:T(8,128)S(1)}, u32[]{:S(2)}, u32[]{:S(2)}) collective-permute-start(f32[128,256]{1,0:T(8,128)S(1)} %get-tuple-element.47.refs_0_), channel_id=1, source_target_pairs={{0,8},{8,16},{16,24},{24,0},{32,56},{40,32},{48,40},{56,48},{1,9},... | collective-permute-start | bytes 393224 | tf_op jit(solution)/shard_map/gather/ppermute | solution.py:33
  16.1 6.5 %collective-permute-start.1 = (f32[128,256]{1,0:T(8,128)S(1)}, f32[128,256]{1,0:T(8,128)S(1)}, u32[]{:S(2)}, u32[]{:S(2)}) collective-permute-start(f32[128,256]{1,0:T(8,128)S(1)} %get-tuple-element.47.refs_0_), channel_id=1, source_target_pairs={{0,24},{8,0},{16,8},{24,16},{32,40},{40,48},{48,56},{56,32},{1,25}... | collective-permute-start | bytes 393224 | tf_op jit(solution)/shard_map/gather/ppermute | solution.py:33
  16.1 6.5 %collective-permute-start.13 = (f32[128,256]{1,0:T(8,128)S(1)}, f32[128,256]{1,0:T(8,128)S(1)}, u32[]{:S(2)}, u32[]{:S(2)}) collective-permute-start(f32[128,256]{1,0:T(8,128)S(1)} %collective-permute-done.12.refs_6_), channel_id=1, source_target_pairs={{0,1},{1,2},{2,3},{3,4},{4,5},{5,6},{6,7},{7,0},{32,39},{33,32},{3... | collective-permute-start | bytes 393224 | tf_op jit(solution)/shard_map/gather/ppermute | solution.py:33
  18.9 6.4 %collective-permute-start.14 = (f32[128,256]{1,0:T(8,128)S(1)}, f32[128,256]{1,0:T(8,128)S(1)}, u32[]{:S(2)}, u32[]{:S(2)}) collective-permute-start(f32[128,256]{1,0:T(8,128)S(1)} %collective-permute-done.10.refs_2_), channel_id=1, source_target_pairs={{0,7},{1,0},{2,1},{3,2},{4,3},{5,4},{6,5},{7,6},{32,33},{33,34},{3... | collective-permute-start | bytes 393224 | tf_op jit(solution)/shard_map/gather/ppermute | solution.py:33
  22.6 3.8 %collective-permute-start.2 = (f32[128,256]{1,0:T(8,128)S(1)}, f32[128,256]{1,0:T(8,128)S(1)}, u32[]{:S(2)}, u32[]{:S(2)}) collective-permute-start(f32[128,256]{1,0:T(8,128)S(1)} %collective-permute-done.refs_3_), channel_id=1, source_target_pairs={{0,8},{8,16},{16,24},{24,0},{32,56},{40,32},{48,40},{56,48},{1,9},... | collective-permute-start | bytes 393224 | tf_op jit(solution)/shard_map/gather/ppermute | solution.py:33
  25.3 3.8 %collective-permute-start.15 = (f32[128,256]{1,0:T(8,128)S(1)}, f32[128,256]{1,0:T(8,128)S(1)}, u32[]{:S(2)}, u32[]{:S(2)}) collective-permute-start(f32[128,256]{1,0:T(8,128)S(1)} %collective-permute-done.13.refs_5_), channel_id=1, source_target_pairs={{0,1},{1,2},{2,3},{3,4},{4,5},{5,6},{6,7},{7,0},{32,39},{33,32},{3... | collective-permute-start | bytes 393224 | tf_op jit(solution)/shard_map/gather/ppermute | solution.py:33
  26.5 9.3 %collective-permute-start.5 = (f32[512,256]{1,0:T(8,128)S(1)}, f32[512,256]{1,0:T(8,128)S(1)}, u32[]{:S(2)}, u32[]{:S(2)}) collective-permute-start(f32[512,256]{1,0:T(8,128)S(1)} %join.2.refs_0_), channel_id=1, source_target_pairs={{0,1},{1,2},{2,3},{3,4},{4,5},{5,6},{6,7},{7,0},{32,39},{33,32},{3... | collective-permute-start | bytes 1572872 | tf_op jit(solution)/shard_map/gather/ppermute | solution.py:33
  28.0 13.4 %collective-permute-start.3 = (f32[512,256]{1,0:T(8,128)S(1)}, f32[512,256]{1,0:T(8,128)S(1)}, u32[]{:S(2)}, u32[]{:S(2)}) collective-permute-start(f32[512,256]{1,0:T(8,128)S(1)} %join.2.refs_0_), channel_id=1, source_target_pairs={{0,7},{1,0},{2,1},{3,2},{4,3},{5,4},{6,5},{7,6},{32,33},{33,34},{3... | collective-permute-start | bytes 1572872 | tf_op jit(solution)/shard_map/gather/ppermute | solution.py:33
  29.2 24.8 %collective-permute-start.16 = (f32[1024,256]{1,0:T(8,128)S(1)}, f32[1024,256]{1,0:T(8,128)}, u32[]{:S(2)}, u32[]{:S(2)}) collective-permute-start(f32[1024,256]{1,0:T(8,128)S(1)} %join.3.refs_7_), channel_id=1, source_target_pairs={{0,8},{8,16},{16,24},{24,0},{32,56},{40,32},{48,40},{56,48},{1,9},... | collective-permute-start | bytes 3145736 | tf_op jit(solution)/shard_map/gather/ppermute | solution.py:33
  32.1 25.4 %collective-permute-start.17 = (f32[1024,256]{1,0:T(8,128)S(1)}, f32[1024,256]{1,0:T(8,128)S(1)}, u32[]{:S(2)}, u32[]{:S(2)}) collective-permute-start(f32[1024,256]{1,0:T(8,128)S(1)} %join.3.refs_7_), channel_id=1, source_target_pairs={{0,24},{8,0},{16,8},{24,16},{32,40},{40,48},{48,56},{56,32},{1,25}... | collective-permute-start | bytes 3145736 | tf_op jit(solution)/shard_map/gather/ppermute | solution.py:33
  35.8 10.6 %collective-permute-start.6 = (f32[512,256]{1,0:T(8,128)S(1)}, f32[512,256]{1,0:T(8,128)}, u32[]{:S(2)}, u32[]{:S(2)}) collective-permute-start(f32[512,256]{1,0:T(8,128)S(1)} %collective-permute-done.5.refs_6_), channel_id=1, source_target_pairs={{0,1},{1,2},{2,3},{3,4},{4,5},{5,6},{6,7},{7,0},{32,39},{33,32},{3... | collective-permute-start | bytes 1572872 | tf_op jit(solution)/shard_map/gather/ppermute | solution.py:33
  41.4 12.6 %collective-permute-start.4 = (f32[512,256]{1,0:T(8,128)S(1)}, f32[512,256]{1,0:T(8,128)}, u32[]{:S(2)}, u32[]{:S(2)}) collective-permute-start(f32[512,256]{1,0:T(8,128)S(1)} %collective-permute-done.3.refs_1_), channel_id=1, source_target_pairs={{0,7},{1,0},{2,1},{3,2},{4,3},{5,4},{6,5},{7,6},{32,33},{33,34},{3... | collective-permute-start | bytes 1572872 | tf_op jit(solution)/shard_map/gather/ppermute | solution.py:33
  41.4 0.8 copy-start.2
  46.4 13.3 %collective-permute-start.7 = (f32[512,256]{1,0:T(8,128)}, f32[512,256]{1,0:T(8,128)}, u32[]{:S(2)}, u32[]{:S(2)}) collective-permute-start(f32[512,256]{1,0:T(8,128)} %collective-permute-done.6.refs_5_), channel_id=1, source_target_pairs={{0,1},{1,2},{2,3},{3,4},{4,5},{5,6},{6,7},{7,0},{32,39},{33,32},{3... | collective-permute-start | bytes 1572872 | tf_op jit(solution)/shard_map/gather/ppermute | solution.py:33
  54.1 11.9 %collective-permute-start.8 = (f32[512,256]{1,0:T(8,128)}, f32[512,256]{1,0:T(8,128)}, u32[]{:S(2)}, u32[]{:S(2)}) collective-permute-start(f32[512,256]{1,0:T(8,128)} %collective-permute-done.4.refs_2_), channel_id=1, source_target_pairs={{0,7},{1,0},{2,1},{3,2},{4,3},{5,4},{6,5},{7,6},{32,33},{33,34},{3... | collective-permute-start | bytes 1572872 | tf_op jit(solution)/shard_map/gather/ppermute | solution.py:33
  57.5 1.0 copy-start
  58.5 17.4 %collective-permute-start.19 = (f32[1024,256]{1,0:T(8,128)}, f32[1024,256]{1,0:T(8,128)S(1)}, u32[]{:S(2)}, u32[]{:S(2)}) collective-permute-start(f32[1024,256]{1,0:T(8,128)} %collective-permute-done.16.refs_9_), channel_id=1, source_target_pairs={{0,8},{8,16},{16,24},{24,0},{32,56},{40,32},{48,40},{56,48},{1,9},... | collective-permute-start | bytes 3145736 | tf_op jit(solution)/shard_map/gather/ppermute | solution.py:33
  66.0 9.9 %collective-permute-start.18 = (f32[512,256]{1,0:T(8,128)}, f32[512,256]{1,0:T(8,128)S(1)}, u32[]{:S(2)}, u32[]{:S(2)}) collective-permute-start(f32[512,256]{1,0:T(8,128)} %collective-permute-done.7.refs_4_), channel_id=1, source_target_pairs={{0,1},{1,2},{2,3},{3,4},{4,5},{5,6},{6,7},{7,0},{32,39},{33,32},{3... | collective-permute-start | bytes 1572872 | tf_op jit(solution)/shard_map/gather/ppermute | solution.py:33
  67.7 0.7 copy-start.4
  71.2 1.2 copy-start.1
  72.4 1.0 copy-start.3
  76.0 17.5 %collective-permute-start.20 = (f32[8192,256]{1,0:T(8,128)S(1)}, f32[8192,256]{1,0:T(8,128)S(1)}, u32[]{:S(2)}, u32[]{:S(2)}) collective-permute-start(f32[8192,256]{1,0:T(8,128)S(1)} %place.3.panels), channel_id=1, source_target_pairs={{0,32},{32,0},{1,33},{33,1},{2,34},{34,2},{3,35},{35,3},{4,36},{36... | collective-permute-start | bytes 25165832 | tf_op jit(solution)/shard_map/gather/ppermute | solution.py:37
  98.5 22.4 %collective-permute-start.22 = (f32[8,128,256]{2,1,0:T(8,128)S(1)}, f32[8,128,256]{2,1,0:T(8,128)S(1)}, u32[]{:S(2)}, u32[]{:S(2)}) collective-permute-start(f32[8,128,256]{2,1,0:T(8,128)S(1)} %slot_products.5), channel_id=1, source_target_pairs={{0,8},{8,16},{16,24},{24,0},{32,56},{40,32},{48,40},{56,48},{1,9},... | collective-permute-start | bytes 3145736 | tf_op jit(solution)/shard_map/scatter_rows/ppermute | solution.py:33
  111.0 20.5 %collective-permute-start.21 = (f32[8,128,256]{2,1,0:T(8,128)S(1)}, f32[8,128,256]{2,1,0:T(8,128)S(1)}, u32[]{:S(2)}, u32[]{:S(2)}) collective-permute-start(f32[8,128,256]{2,1,0:T(8,128)S(1)} %get-tuple-element.39), channel_id=1, source_target_pairs={{0,24},{8,0},{16,8},{24,16},{32,40},{40,48},{48,56},{56,32},{1,25}... | collective-permute-start | bytes 3145736 | tf_op jit(solution)/shard_map/scatter_rows/ppermute | solution.py:33
  121.0 16.0 %collective-permute-start.23 = (f32[8,128,256]{2,1,0:T(8,128)S(1)}, f32[8,128,256]{2,1,0:T(8,128)S(1)}, u32[]{:S(2)}, u32[]{:S(2)}) collective-permute-start(f32[8,128,256]{2,1,0:T(8,128)S(1)} %add.87), channel_id=1, source_target_pairs={{0,8},{8,16},{16,24},{24,0},{32,56},{40,32},{48,40},{56,48},{1,9},... | collective-permute-start | bytes 3145736 | tf_op jit(solution)/shard_map/scatter_rows/ppermute | solution.py:33

commit v2 on v0

--- a/solution.py
+++ b/solution.py
@@ -46,6 +46,8 @@
         ahead = shift(ahead, axis, -1)
         found[count - step] = behind
         found[step] = ahead
+    behind, ahead = lax.optimization_barrier((behind, ahead))
+    found[count // 2 + 1], found[count // 2 - 1] = behind, ahead
     found[count // 2] = shift(behind, axis, 1)
     return found
 
@@ -283,8 +285,11 @@
                         value = value - lower[q, t] * weights[t]
                     weights.append(value)
                 weights = [v * w for v, w in zip(weights, inverse)]
-                for q in range(8):
-                    held[s] = [v - weights[q] * w for v, w in zip(held[s], lines[q])]
+                for c in range(len(held[s])):
+                    terms = [weights[q] * lines[q][c] for q in range(8)]
+                    while len(terms) > 1:
+                        terms = [a + b for a, b in zip(terms[::2], terms[1::2])]
+                    held[s][c] = held[s][c] - terms[0]
             final = [jnp.zeros((8, EDGE), jnp.float32)] * len(held[s0])
             for q in range(8):
                 final = [jnp.where(sub == q, w * root[q], v) for v, w in zip(final, lines[q])]
@@ -361,8 +366,20 @@
 
     with jax.named_scope("gather"):
         mine = lax.dynamic_slice_in_dim(sketch, here_core * 2 * EDGE, 2 * EDGE, 0)
-        slab = join(ring_gather(mine[:EDGE], "x"))
-        line = join(ring_gather(mine[EDGE:], "z"))
+        top, low = mine[:EDGE], mine[EDGE:]
+        top_behind, top_ahead, low_behind, low_ahead = lax.optimization_barrier(
+            (shift(top, "x", 1), shift(top, "x", -1), shift(low, "z", 1), shift(low, "z", -1))
+        )
+        top_far, pair_behind, pair_ahead = lax.optimization_barrier(
+            (
+                shift(top_behind, "x", 1),
+                shift(join([low_behind, low]), "z", 2),
+                shift(join([low, low_ahead]), "z", -2),
+            )
+        )
+        slab = join([top, top_ahead, top_far, top_behind])
+        low_far = shift(pair_behind[:EDGE], "z", 1)
+        line = join([low, low_ahead, pair_ahead, low_far, pair_behind, low_behind])
         first = ring_gather(slab, "z")
         second = ring_gather(line, "x")
         slab, *plan, counts = lax.optimization_barrier((slab, *slot_plan(bucket_fill[0, 0], kind)))

time: 218 us -> 225 us (1.032)
  local copies, waits for them, and re-layouts: 1.71 us -> 5.76 us
  waiting for transfers between devices: 81.6 us -> 85 us
    ppermute x28 -> x26, starting transfers between devices: 45.9 us -> 50.3 us  [shift(): return lax.ppermute(value, ('core', axis), pairs)]
    unnamed x2 -> x10, local copies, waits for them, and re-layouts: 0.65 us -> 4.7 us
    ppermute x1, starting transfers between devices: 8.61 us -> 4.74 us  [swap(): return lax.ppermute(value, 'core', [(0, 1), (1, 0)])]
    ppermute x28 -> x26, waiting for transfers between devices: 74.9 us -> 78.5 us  [shift(): return lax.ppermute(value, ('core', axis), pairs)]
  transfers between devices with their start and end apart: 29 -> 27, of which waited for: 19 -> 22; matrix products, arithmetic and copies ran while one was open for 1% -> 1% of each run, Pallas kernels for 9% -> 8%
where the time goes in v2:
time: 225 us; the launch traced here: 224 us
  waiting for transfers between devices  85 us (38%)
  starting transfers between devices  55 us (24%)
  blocking collectives  43 us (19%)
  Pallas kernels  31.9 us (14%)
  local copies, waits for them, and re-layouts  5.76 us (3%)
    ppermute x26, waiting for transfers between devices, shift(): return lax.ppermute(value, ('core', axis), pairs)  78.5 us
    ppermute x26, starting transfers between devices, shift(): return lax.ppermute(value, ('core', axis), pairs)  50.3 us
    all_to_all x3, blocking collectives, exchange(): return lax.all_to_all(value, axes, 0, 0, tiled=True)  43 us
    pallas_call x3, Pallas kernels, slot_products(): pl.pallas_call(functools.partial(products_kernel, part), out_shape=shapes...  16.8 us
    pallas_call x1, Pallas kernels, factor_and_solve(): pl.pallas_call(factor_kernel, out_shape=[jax.ShapeDtypeStruct((EDGE, WIDT...  9.79 us
    ppermute x1, waiting for transfers between devices, swap(): return lax.ppermute(value, 'core', [(0, 1), (1, 0)])  6.5 us
    ppermute x1, starting transfers between devices, swap(): return lax.ppermute(value, 'core', [(0, 1), (1, 0)])  4.74 us
    unnamed x10, local copies, waits for them, and re-layouts  4.7 us
  transfers between devices with their start and end apart: 27, of which 22 were waited for; matrix products, arithmetic and copies ran while one was open for 1% of the time, Pallas kernels for 8%

profile of v2, /device:TPU:1, one launch (start us, length us, event | category | flops | bytes accessed | tf_op | source)
XLA Modules:
  0.0 224.0 jit_solution(12764721622799657704)
XLA Ops:
  0.6 1.0 constant_dynamic-slice_fusion.1
  1.6 3.4 %collective-permute-start = (f32[128,256]{1,0:T(8,128)S(1)}, f32[128,256]{1,0:T(8,128)S(1)}, u32[]{:S(2)}, u32[]{:S(2)}) collective-permute-start(f32[128,256]{1,0:T(8,128)S(1)} %get-tuple-element.65.refs_0_), channel_id=1, source_target_pairs={{0,8},{8,16},{16,24},{24,0},{32,56},{40,32},{48,40},{56,48},{1,9},... | collective-permute-start | bytes 393224 | tf_op jit(solution)/shard_map/gather/ppermute | solution.py:33
  5.0 5.6 %collective-permute-start.2 = (f32[128,256]{1,0:T(8,128)S(1)}, f32[128,256]{1,0:T(8,128)S(1)}, u32[]{:S(2)}, u32[]{:S(2)}) collective-permute-start(f32[128,256]{1,0:T(8,128)S(1)} %get-tuple-element.64.refs_1_.refs_0_), channel_id=1, source_target_pairs={{0,1},{1,2},{2,3},{3,4},{4,5},{5,6},{6,7},{7,0},{32,39},{33,32},{3... | collective-permute-start | bytes 393224 | tf_op jit(solution)/shard_map/gather/ppermute | solution.py:33
  10.6 0.8 collective-permute-done.1.refs_1_
  11.4 1.1 collective-permute-done.2.refs_0_.refs_5_
  12.5 3.4 %collective-permute-done.3.refs_1_ = f32[128,256]{1,0:T(8,128)S(1)} collective-permute-done((f32[128,256]{1,0:T(8,128)S(1)}, f32[128,256]{1,0:T(8,128)S(1)}, u32[]{:S(2)}, u32[]{:S(2)}) %collective-permute-start.3) | collective-permute-done | bytes 131104 | tf_op jit(solution)/shard_map/gather/ppermute | solution.py:33
  16.0 0.2 collective-permute-start.5
  16.3 2.3 %collective-permute-start.6 = (f32[256,256]{1,0:T(8,128)S(1)}, f32[256,256]{1,0:T(8,128)S(1)}, u32[]{:S(2)}, u32[]{:S(2)}) collective-permute-start(f32[256,256]{1,0:T(8,128)S(1)} %join.5), channel_id=1, source_target_pairs={{0,6},{1,7},{2,0},{3,1},{4,2},{5,3},{6,4},{7,5},{32,34},{33,35},{3... | collective-permute-start | bytes 786440 | tf_op jit(solution)/shard_map/gather/ppermute | solution.py:33
  18.5 2.3 %collective-permute-start.4 = (f32[128,256]{1,0:T(8,128)S(1)}, f32[128,256]{1,0:T(8,128)S(1)}, u32[]{:S(2)}, u32[]{:S(2)}) collective-permute-start(f32[128,256]{1,0:T(8,128)S(1)} %collective-permute-done.refs_3_), channel_id=1, source_target_pairs={{0,8},{8,16},{16,24},{24,0},{32,56},{40,32},{48,40},{56,48},{1,9},... | collective-permute-start | bytes 393224 | tf_op jit(solution)/shard_map/gather/ppermute | solution.py:33
  20.9 1.9 collective-permute-done.4.refs_2_
  22.8 1.3 collective-permute-done.5.refs_4_
  24.1 5.1 %collective-permute-done.6.refs_2_ = f32[256,256]{1,0:T(8,128)S(1)} collective-permute-done((f32[256,256]{1,0:T(8,128)S(1)}, f32[256,256]{1,0:T(8,128)S(1)}, u32[]{:S(2)}, u32[]{:S(2)}) %collective-permute-start.6) | collective-permute-done | bytes 262176 | tf_op jit(solution)/shard_map/gather/ppermute | solution.py:33
  29.2 2.0 collective-permute-start.13
  31.3 0.1 collective-permute-start.9
  31.4 1.4 collective-permute-start.7
  32.8 1.5 collective-permute-done.13.refs_3_
  34.4 2.9 %collective-permute-start.14 = (f32[1024,256]{1,0:T(8,128)S(1)}, f32[1024,256]{1,0:T(8,128)}, u32[]{:S(2)}, u32[]{:S(2)}) collective-permute-start(f32[1024,256]{1,0:T(8,128)S(1)} %join.7.refs_7_), channel_id=1, source_target_pairs={{0,8},{8,16},{16,24},{24,0},{32,56},{40,32},{48,40},{56,48},{1,9},... | collective-permute-start | bytes 3145736 | tf_op jit(solution)/shard_map/gather/ppermute | solution.py:33
  37.3 2.9 %collective-permute-done.9.refs_6_ = f32[512,256]{1,0:T(8,128)S(1)} collective-permute-done((f32[512,256]{1,0:T(8,128)S(1)}, f32[512,256]{1,0:T(8,128)S(1)}, u32[]{:S(2)}, u32[]{:S(2)}) %collective-permute-start.9) | collective-permute-done | bytes 524320 | tf_op jit(solution)/shard_map/gather/ppermute | solution.py:33
  40.3 2.4 %collective-permute-start.10 = (f32[512,256]{1,0:T(8,128)S(1)}, f32[512,256]{1,0:T(8,128)}, u32[]{:S(2)}, u32[]{:S(2)}) collective-permute-start(f32[512,256]{1,0:T(8,128)S(1)} %collective-permute-done.9.refs_6_), channel_id=1, source_target_pairs={{0,1},{1,2},{2,3},{3,4},{4,5},{5,6},{6,7},{7,0},{32,39},{33,32},{3... | collective-permute-start | bytes 1572872 | tf_op jit(solution)/shard_map/gather/ppermute | solution.py:33
  42.7 3.6 %collective-permute-done.7.refs_1_ = f32[512,256]{1,0:T(8,128)S(1)} collective-permute-done((f32[512,256]{1,0:T(8,128)S(1)}, f32[512,256]{1,0:T(8,128)S(1)}, u32[]{:S(2)}, u32[]{:S(2)}) %collective-permute-start.7) | collective-permute-done | bytes 524320 | tf_op jit(solution)/shard_map/gather/ppermute | solution.py:33
  46.3 0.8 copy-done.2
  47.1 4.9 %collective-permute-done.10.refs_5_ = f32[512,256]{1,0:T(8,128)} collective-permute-done((f32[512,256]{1,0:T(8,128)S(1)}, f32[512,256]{1,0:T(8,128)}, u32[]{:S(2)}, u32[]{:S(2)}) %collective-permute-start.10) | collective-permute-done | bytes 524320 | tf_op jit(solution)/shard_map/gather/ppermute | solution.py:33
  52.0 1.5 collective-permute-start.11
  53.5 5.7 %collective-permute-done.8.refs_2_ = f32[512,256]{1,0:T(8,128)} collective-permute-done((f32[512,256]{1,0:T(8,128)S(1)}, f32[512,256]{1,0:T(8,128)}, u32[]{:S(2)}, u32[]{:S(2)}) %collective-permute-start.8) | collective-permute-done | bytes 524320 | tf_op jit(solution)/shard_map/gather/ppermute | solution.py:33
  59.3 3.3 %collective-permute-done.15.refs_8_ = f32[1024,256]{1,0:T(8,128)S(1)} collective-permute-done((f32[1024,256]{1,0:T(8,128)S(1)}, f32[1024,256]{1,0:T(8,128)S(1)}, u32[]{:S(2)}, u32[]{:S(2)}) %collective-permute-start.15) | collective-permute-done | bytes 1048608 | tf_op jit(solution)/shard_map/gather/ppermute | solution.py:33
  62.6 1.0 copy-done
  63.6 2.5 %collective-permute-start.17 = (f32[1024,256]{1,0:T(8,128)}, f32[1024,256]{1,0:T(8,128)S(1)}, u32[]{:S(2)}, u32[]{:S(2)}) collective-permute-start(f32[1024,256]{1,0:T(8,128)} %collective-permute-done.14.refs_9_), channel_id=1, source_target_pairs={{0,8},{8,16},{16,24},{24,0},{32,56},{40,32},{48,40},{56,48},{1,9},... | collective-permute-start | bytes 3145736 | tf_op jit(solution)/shard_map/gather/ppermute | solution.py:33
  66.1 5.4 %collective-permute-done.12.refs_3_ = f32[512,256]{1,0:T(8,128)} collective-permute-done((f32[512,256]{1,0:T(8,128)}, f32[512,256]{1,0:T(8,128)}, u32[]{:S(2)}, u32[]{:S(2)}) %collective-permute-start.12) | collective-permute-done | bytes 524320 | tf_op jit(solution)/shard_map/gather/ppermute | solution.py:33
  71.5 0.8 select_reduce_fusion
  72.3 0.7 compare_select_fusion.10
  73.1 0.6 copy-done.4
  73.7 2.6 %slot_plan.1 = (s32[192]{0:T(256)S(1)}, s32[192]{0:T(256)S(1)}, s32[192]{0:T(256)S(1)}, s32[3]{0:T(128)S(1)}) custom-call(s32[32]{0:T(128)S(1)} %bitcast.31, s32[192]{0:T(256)S(1)} %get-tuple-element.58.kind), custom_call_target="tpu_custom_call" | custom-call | bytes 12582912 | tf_op jit(solution)/shard_map/gather/slot_plan/pallas_call | solution.py:129
  76.4 1.2 copy-done.1
  77.6 1.0 copy-done.3
  78.6 2.4 %place.2.refs_0_ = f32[8192,256]{1,0:T(8,128)S(1)} custom-call(f32[512,256]{1,0:T(8,128)S(1)} %join.6.refs_0_, f32[512,256]{1,0:T(8,128)S(1)} %copy-done.3, f32[512,256]{1,0:T(8,128)} %collective-permute-done.8.refs_2_, f32[512,256]{1,0:T(8,128)} %collective-permute-done.12.refs_3_, f32[512,256]{1,0:T(8,128)} %collective-permute-done.11.refs_4_, ...), custom_call_target="tpu_custom_call" | custom-call | bytes 13631488 | tf_op jit(solution)/shard_map/gather/place/pallas_call | solution.py:96
  81.1 0.1 place.3.panels
  81.2 4.7 %collective-permute-start.18 = (f32[8192,256]{1,0:T(8,128)S(1)}, f32[8192,256]{1,0:T(8,128)S(1)}, u32[]{:S(2)}, u32[]{:S(2)}) collective-permute-start(f32[8192,256]{1,0:T(8,128)S(1)} %place.3.panels), channel_id=1, source_target_pairs={{0,32},{32,0},{1,33},{33,1},{2,34},{34,2},{3,35},{35,3},{4,36},{36... | collective-permute-start | bytes 25165832 | tf_op jit(solution)/shard_map/gather/ppermute | solution.py:37
  86.0 6.3 %slot_products.3.refs_0_ = f32[32,128,256]{2,1,0:T(8,128)S(1)} custom-call(s32[3]{0:T(128)S(1)} %get-tuple-element.38.counts, s32[192]{0:T(256)S(1)} %get-tuple-element.47.listed, s32[192]{0:T(256)S(1)} %get-tuple-element.56.blk, s32[192]{0:T(256)S(1)} %get-tuple-element.59.row, f32[192,128,128]{2,1,0:T(8,128)} %bitcast.32, f32[8192,256]{1,0:T(8,128)S(1)} %place.3.panels), custom_call_target="tpu_custom_call" | custom-call | flops 3221225472 | bytes 12582912 | tf_op jit(solution)/shard_map/slot_products/pallas_call | solution.py:219
  92.2 6.5 %collective-permute-done.18.panels = f32[8192,256]{1,0:T(8,128)S(1)} collective-permute-done((f32[8192,256]{1,0:T(8,128)S(1)}, f32[8192,256]{1,0:T(8,128)S(1)}, u32[]{:S(2)}, u32[]{:S(2)}) %collective-permute-start.18) | collective-permute-done | bytes 8388640 | tf_op jit(solution)/shard_map/gather/ppermute | solution.py:37
  98.7 3.9 %slot_products.5 = f32[8,128,256]{2,1,0:T(8,128)S(1)} custom-call(s32[3]{0:T(128)S(1)} %get-tuple-element.38.counts, s32[192]{0:T(256)S(1)} %get-tuple-element.51.listed, s32[192]{0:T(256)S(1)} %get-tuple-element.56.blk, s32[192]{0:T(256)S(1)} %get-tuple-element.59.row, f32[192,128,128]{2,1,0:T(8,128)} %bitcast.33, ...), custom_call_target="tpu_custom_call" | custom-call | flops 805306368 | bytes 3145728 | tf_op jit(solution)/shard_map/slot_products/pallas_call | solution.py:219
  102.7 6.1 %collective-permute-start.20 = (f32[8,128,256]{2,1,0:T(8,128)S(1)}, f32[8,128,256]{2,1,0:T(8,128)S(1)}, u32[]{:S(2)}, u32[]{:S(2)}) collective-permute-start(f32[8,128,256]{2,1,0:T(8,128)S(1)} %slot_products.5), channel_id=1, source_target_pairs={{0,8},{8,16},{16,24},{24,0},{32,56},{40,32},{48,40},{56,48},{1,9},... | collective-permute-start | bytes 3145736 | tf_op jit(solution)/shard_map/scatter_rows/ppermute | solution.py:33
  108.8 6.6 %slot_products.4 = (f32[8,128,256]{2,1,0:T(8,128)S(1)}, f32[8,128,256]{2,1,0:T(8,128)S(1)}, f32[8,128,256]{2,1,0:T(8,128)S(1)}) custom-call(s32[3]{0:T(128)S(1)} %get-tuple-element.38.counts, s32[192]{0:T(256)S(1)} %get-tuple-element.39.listed, s32[192]{0:T(256)S(1)} %get-tuple-element.56.blk, s32[192]{0:T(256)S(1)} %get-tuple-element.59.row, ...), custom_call_target="tpu_custom_call" | custom-call | flops 2415919104 | bytes 9437184 | tf_op jit(solution)/shard_map/slot_products/pallas_call | solution.py:219
  115.4 0.1 collective-permute-start.19
  115.5 10.0 %collective-permute-done.20 = f32[8,128,256]{2,1,0:T(8,128)S(1)} collective-permute-done((f32[8,128,256]{2,1,0:T(8,128)S(1)}, f32[8,128,256]{2,1,0:T(8,128)S(1)}, u32[]{:S(2)}, u32[]{:S(2)}) %collective-permute-start.20) | collective-permute-done | bytes 1048608 | tf_op jit(solution)/shard_map/scatter_rows/ppermute | solution.py:33
  125.5 0.1 add.123
  125.7 3.5 %collective-permute-start.21 = (f32[8,128,256]{2,1,0:T(8,128)S(1)}, f32[8,128,256]{2,1,0:T(8,128)S(1)}, u32[]{:S(2)}, u32[]{:S(2)}) collective-permute-start(f32[8,128,256]{2,1,0:T(8,128)S(1)} %add.123), channel_id=1, source_target_pairs={{0,8},{8,16},{16,24},{24,0},{32,56},{40,32},{48,40},{56,48},{1,9},... | collective-permute-start | bytes 3145736 | tf_op jit(solution)/shard_map/scatter_rows/ppermute | solution.py:33
  129.2 5.8 %collective-permute-done.19 = f32[8,128,256]{2,1,0:T(8,128)S(1)} collective-permute-done((f32[8,128,256]{2,1,0:T(8,128)S(1)}, f32[8,128,256]{2,1,0:T(8,128)S(1)}, u32[]{:S(2)}, u32[]{:S(2)}) %collective-permute-start.19) | collective-permute-done | bytes 1048608 | tf_op jit(solution)/shard_map/scatter_rows/ppermute | solution.py:33
  135.0 8.0 %collective-permute-done.21 = f32[8,128,256]{2,1,0:T(8,128)S(1)} collective-permute-done((f32[8,128,256]{2,1,0:T(8,128)S(1)}, f32[8,128,256]{2,1,0:T(8,128)S(1)}, u32[]{:S(2)}, u32[]{:S(2)}) %collective-permute-start.21) | collective-permute-done | bytes 1048608 | tf_op jit(solution)/shard_map/scatter_rows/ppermute | solution.py:33
  143.0 0.2 add_add_fusion
  143.2 2.2 collective-permute-start.22
  145.4 1.9 collective-permute-done.22
  147.4 2.9 %collective-permute-start.24 = (f32[2,128,256]{2,1,0:T(8,128)S(1)}, f32[2,128,256]{2,1,0:T(8,128)S(1)}, u32[]{:S(2)}, u32[]{:S(2)}) collective-permute-start(f32[2,128,256]{2,1,0:T(8,128)S(1)} %slice.60), channel_id=1, source_target_pairs={{0,6},{1,7},{2,0},{3,1},{4,2},{5,3},{6,4},{7,5},{32,34},{33,35},{3... | collective-permute-start | bytes 786440 | tf_op jit(solution)/shard_map/scatter_rows/ppermute | solution.py:33
  150.3 0.8 collective-permute-start.23
  151.1 4.4 %collective-permute-done.24 = f32[2,128,256]{2,1,0:T(8,128)S(1)} collective-permute-done((f32[2,128,256]{2,1,0:T(8,128)S(1)}, f32[2,128,256]{2,1,0:T(8,128)S(1)}, u32[]{:S(2)}, u32[]{:S(2)}) %collective-permute-start.24) | collective-permute-done | bytes 262176 | tf_op jit(solution)/shard_map/scatter_rows/ppermute | solution.py:33
  155.5 4.3 %collective-permute-done.23 = f32[2,128,256]{2,1,0:T(8,128)S(1)} collective-permute-done((f32[2,128,256]{2,1,0:T(8,128)S(1)}, f32[2,128,256]{2,1,0:T(8,128)S(1)}, u32[]{:S(2)}, u32[]{:S(2)}) %collective-permute-start.23) | collective-permute-done | bytes 262176 | tf_op jit(solution)/shard_map/scatter_rows/ppermute | solution.py:33
  159.9 5.7 %collective-permute-start.26 = (f32[128,256]{1,0:T(8,128)S(1)}, f32[128,256]{1,0:T(8,128)S(1)}, u32[]{:S(2)}, u32[]{:S(2)}) collective-permute-start(f32[128,256]{1,0:T(8,128)S(1)} %get-tuple-element.55), channel_id=1, source_target_pairs={{0,7},{1,0},{2,1},{3,2},{4,3},{5,4},{6,5},{7,6},{32,33},{33,34},{3... | collective-permute-start | bytes 393224 | tf_op jit(solution)/shard_map/scatter_rows/ppermute | solution.py:33
  165.5 2.4 %collective-permute-start.25 = (f32[128,256]{1,0:T(8,128)S(1)}, f32[128,256]{1,0:T(8,128)S(1)}, u32[]{:S(2)}, u32[]{:S(2)}) collective-permute-start(f32[128,256]{1,0:T(8,128)S(1)} %get-tuple-element.54), channel_id=1, source_target_pairs={{0,1},{1,2},{2,3},{3,4},{4,5},{5,6},{6,7},{7,0},{32,39},{33,32},{3... | collective-permute-start | bytes 393224 | tf_op jit(solution)/shard_map/scatter_rows/ppermute | solution.py:33
  167.9 2.0 collective-permute-done.26
  169.9 0.7 collective-permute-done.25
  170.7 0.4 convolution_bitcast_fusion
  171.1 19.2 %all_to_all.19 = f32[32,8,256]{2,1,0:T(8,128)S(1)} all-to-all(f32[32,8,256]{2,1,0:T(8,128)S(1)} %convolution_bitcast_fusion), channel_id=1, replica_groups=mesh['y'=4,'core'=2,'x'=4,'z'=8] {'y','core','x'}, dimensions={0} | all-to-all | bytes 524288 | tf_op jit(solution)/shard_map/gram/all_to_all | solution.py:341
  190.4 9.5 %all_to_all.20 = f32[8,8,256]{2,1,0:T(8,128)S(1)} all-to-all(f32[8,8,256]{2,1,0:T(8,128)S(1)} %broadcast_in_dim.39), channel_id=1, replica_groups=mesh['y'=4,'core'=2,'x'=4,'z'=8] {'z'}, dimensions={0} | all-to-all | bytes 131072 | tf_op jit(solution)/shard_map/gram/all_to_all | solution.py:341
  200.0 14.2 %all_to_all.21 = f32[32,8,256]{2,1,0:T(8,128)S(1)} all-to-all(f32[32,8,256]{2,1,0:T(8,128)S(1)} %broadcast_in_dim.40), channel_id=1, replica_groups=mesh['y'=4,'core'=2,'x'=4,'z'=8] {'y','core','x'}, dimensions={0} | all-to-all | bytes 524288 | tf_op jit(solution)/shard_map/gram/all_to_all | solution.py:341
  214.2 9.8 %factor_and_solve.1 = (f32[128,256]{1,0:T(8,128)}, f32[256,256]{1,0:T(8,128)}) custom-call(f32[256,256]{1,0:T(8,128)S(1)} %bitcast.30, f32[128,256]{1,0:T(8,128)S(1)} %fusion.4.rows), custom_call_target="tpu_custom_call" | custom-call | tf_op jit(solution)/shard_map/factor_and_solve/pallas_call | solution.py:326
  (32 shorter events, 0.4 us)
Async XLA Ops:
  1.6 9.0 %collective-permute-start = (f32[128,256]{1,0:T(8,128)S(1)}, f32[128,256]{1,0:T(8,128)S(1)}, u32[]{:S(2)}, u32[]{:S(2)}) collective-permute-start(f32[128,256]{1,0:T(8,128)S(1)} %get-tuple-element.65.refs_0_), channel_id=1, source_target_pairs={{0,8},{8,16},{16,24},{24,0},{32,56},{40,32},{48,40},{56,48},{1,9},... | collective-permute-start | bytes 393224 | tf_op jit(solution)/shard_map/gather/ppermute | solution.py:33
  5.0 6.4 %collective-permute-start.1 = (f32[128,256]{1,0:T(8,128)S(1)}, f32[128,256]{1,0:T(8,128)S(1)}, u32[]{:S(2)}, u32[]{:S(2)}) collective-permute-start(f32[128,256]{1,0:T(8,128)S(1)} %get-tuple-element.65.refs_0_), channel_id=1, source_target_pairs={{0,24},{8,0},{16,8},{24,16},{32,40},{40,48},{48,56},{56,32},{1,25}... | collective-permute-start | bytes 393224 | tf_op jit(solution)/shard_map/gather/ppermute | solution.py:33
  5.0 7.5 %collective-permute-start.2 = (f32[128,256]{1,0:T(8,128)S(1)}, f32[128,256]{1,0:T(8,128)S(1)}, u32[]{:S(2)}, u32[]{:S(2)}) collective-permute-start(f32[128,256]{1,0:T(8,128)S(1)} %get-tuple-element.64.refs_1_.refs_0_), channel_id=1, source_target_pairs={{0,1},{1,2},{2,3},{3,4},{4,5},{5,6},{6,7},{7,0},{32,39},{33,32},{3... | collective-permute-start | bytes 393224 | tf_op jit(solution)/shard_map/gather/ppermute | solution.py:33
  10.6 5.4 %collective-permute-start.3 = (f32[128,256]{1,0:T(8,128)S(1)}, f32[128,256]{1,0:T(8,128)S(1)}, u32[]{:S(2)}, u32[]{:S(2)}) collective-permute-start(f32[128,256]{1,0:T(8,128)S(1)} %get-tuple-element.64.refs_1_.refs_0_), channel_id=1, source_target_pairs={{0,7},{1,0},{2,1},{3,2},{4,3},{5,4},{6,5},{7,6},{32,33},{33,34},{3... | collective-permute-start | bytes 393224 | tf_op jit(solution)/shard_map/gather/ppermute | solution.py:33
  16.0 8.1 %collective-permute-start.5 = (f32[256,256]{1,0:T(8,128)S(1)}, f32[256,256]{1,0:T(8,128)S(1)}, u32[]{:S(2)}, u32[]{:S(2)}) collective-permute-start(f32[256,256]{1,0:T(8,128)S(1)} %join.4), channel_id=1, source_target_pairs={{0,2},{1,3},{2,4},{3,5},{4,6},{5,7},{6,0},{7,1},{32,38},{33,39},{3... | collective-permute-start | bytes 786440 | tf_op jit(solution)/shard_map/gather/ppermute | solution.py:33
  16.3 12.9 %collective-permute-start.6 = (f32[256,256]{1,0:T(8,128)S(1)}, f32[256,256]{1,0:T(8,128)S(1)}, u32[]{:S(2)}, u32[]{:S(2)}) collective-permute-start(f32[256,256]{1,0:T(8,128)S(1)} %join.5), channel_id=1, source_target_pairs={{0,6},{1,7},{2,0},{3,1},{4,2},{5,3},{6,4},{7,5},{32,34},{33,35},{3... | collective-permute-start | bytes 786440 | tf_op jit(solution)/shard_map/gather/ppermute | solution.py:33
  18.5 4.3 %collective-permute-start.4 = (f32[128,256]{1,0:T(8,128)S(1)}, f32[128,256]{1,0:T(8,128)S(1)}, u32[]{:S(2)}, u32[]{:S(2)}) collective-permute-start(f32[128,256]{1,0:T(8,128)S(1)} %collective-permute-done.refs_3_), channel_id=1, source_target_pairs={{0,8},{8,16},{16,24},{24,0},{32,56},{40,32},{48,40},{56,48},{1,9},... | collective-permute-start | bytes 393224 | tf_op jit(solution)/shard_map/gather/ppermute | solution.py:33
  29.2 5.2 %collective-permute-start.13 = (f32[128,256]{1,0:T(8,128)S(1)}, f32[128,256]{1,0:T(8,128)S(1)}, u32[]{:S(2)}, u32[]{:S(2)}) collective-permute-start(f32[128,256]{1,0:T(8,128)S(1)} %slice.44), channel_id=1, source_target_pairs={{0,1},{1,2},{2,3},{3,4},{4,5},{5,6},{6,7},{7,0},{32,39},{33,32},{3... | collective-permute-start | bytes 393224 | tf_op jit(solution)/shard_map/gather/ppermute | solution.py:33
  31.3 9.0 %collective-permute-start.9 = (f32[512,256]{1,0:T(8,128)S(1)}, f32[512,256]{1,0:T(8,128)S(1)}, u32[]{:S(2)}, u32[]{:S(2)}) collective-permute-start(f32[512,256]{1,0:T(8,128)S(1)} %join.6.refs_0_), channel_id=1, source_target_pairs={{0,1},{1,2},{2,3},{3,4},{4,5},{5,6},{6,7},{7,0},{32,39},{33,32},{3... | collective-permute-start | bytes 1572872 | tf_op jit(solution)/shard_map/gather/ppermute | solution.py:33
  31.4 14.9 %collective-permute-start.7 = (f32[512,256]{1,0:T(8,128)S(1)}, f32[512,256]{1,0:T(8,128)S(1)}, u32[]{:S(2)}, u32[]{:S(2)}) collective-permute-start(f32[512,256]{1,0:T(8,128)S(1)} %join.6.refs_0_), channel_id=1, source_target_pairs={{0,7},{1,0},{2,1},{3,2},{4,3},{5,4},{6,5},{7,6},{32,33},{33,34},{3... | collective-permute-start | bytes 1572872 | tf_op jit(solution)/shard_map/gather/ppermute | solution.py:33
  34.4 24.8 %collective-permute-start.14 = (f32[1024,256]{1,0:T(8,128)S(1)}, f32[1024,256]{1,0:T(8,128)}, u32[]{:S(2)}, u32[]{:S(2)}) collective-permute-start(f32[1024,256]{1,0:T(8,128)S(1)} %join.7.refs_7_), channel_id=1, source_target_pairs={{0,8},{8,16},{16,24},{24,0},{32,56},{40,32},{48,40},{56,48},{1,9},... | collective-permute-start | bytes 3145736 | tf_op jit(solution)/shard_map/gather/ppermute | solution.py:33
  37.3 25.2 %collective-permute-start.15 = (f32[1024,256]{1,0:T(8,128)S(1)}, f32[1024,256]{1,0:T(8,128)S(1)}, u32[]{:S(2)}, u32[]{:S(2)}) collective-permute-start(f32[1024,256]{1,0:T(8,128)S(1)} %join.7.refs_7_), channel_id=1, source_target_pairs={{0,24},{8,0},{16,8},{24,16},{32,40},{40,48},{48,56},{56,32},{1,25}... | collective-permute-start | bytes 3145736 | tf_op jit(solution)/shard_map/gather/ppermute | solution.py:33
  40.3 11.7 %collective-permute-start.10 = (f32[512,256]{1,0:T(8,128)S(1)}, f32[512,256]{1,0:T(8,128)}, u32[]{:S(2)}, u32[]{:S(2)}) collective-permute-start(f32[512,256]{1,0:T(8,128)S(1)} %collective-permute-done.9.refs_6_), channel_id=1, source_target_pairs={{0,1},{1,2},{2,3},{3,4},{4,5},{5,6},{6,7},{7,0},{32,39},{33,32},{3... | collective-permute-start | bytes 1572872 | tf_op jit(solution)/shard_map/gather/ppermute | solution.py:33
  46.3 13.0 %collective-permute-start.8 = (f32[512,256]{1,0:T(8,128)S(1)}, f32[512,256]{1,0:T(8,128)}, u32[]{:S(2)}, u32[]{:S(2)}) collective-permute-start(f32[512,256]{1,0:T(8,128)S(1)} %collective-permute-done.7.refs_1_), channel_id=1, source_target_pairs={{0,7},{1,0},{2,1},{3,2},{4,3},{5,4},{6,5},{7,6},{32,33},{33,34},{3... | collective-permute-start | bytes 1572872 | tf_op jit(solution)/shard_map/gather/ppermute | solution.py:33
  46.3 0.8 copy-start.2
  52.0 14.1 %collective-permute-start.11 = (f32[512,256]{1,0:T(8,128)}, f32[512,256]{1,0:T(8,128)}, u32[]{:S(2)}, u32[]{:S(2)}) collective-permute-start(f32[512,256]{1,0:T(8,128)} %collective-permute-done.10.refs_5_), channel_id=1, source_target_pairs={{0,1},{1,2},{2,3},{3,4},{4,5},{5,6},{6,7},{7,0},{32,39},{33,32},{3... | collective-permute-start | bytes 1572872 | tf_op jit(solution)/shard_map/gather/ppermute | solution.py:33
  59.3 12.3 %collective-permute-start.12 = (f32[512,256]{1,0:T(8,128)}, f32[512,256]{1,0:T(8,128)}, u32[]{:S(2)}, u32[]{:S(2)}) collective-permute-start(f32[512,256]{1,0:T(8,128)} %collective-permute-done.8.refs_2_), channel_id=1, source_target_pairs={{0,7},{1,0},{2,1},{3,2},{4,3},{5,4},{6,5},{7,6},{32,33},{33,34},{3... | collective-permute-start | bytes 1572872 | tf_op jit(solution)/shard_map/gather/ppermute | solution.py:33
  62.6 1.0 copy-start
  63.6 17.5 %collective-permute-start.17 = (f32[1024,256]{1,0:T(8,128)}, f32[1024,256]{1,0:T(8,128)S(1)}, u32[]{:S(2)}, u32[]{:S(2)}) collective-permute-start(f32[1024,256]{1,0:T(8,128)} %collective-permute-done.14.refs_9_), channel_id=1, source_target_pairs={{0,8},{8,16},{16,24},{24,0},{32,56},{40,32},{48,40},{56,48},{1,9},... | collective-permute-start | bytes 3145736 | tf_op jit(solution)/shard_map/gather/ppermute | solution.py:33
  71.5 9.5 %collective-permute-start.16 = (f32[512,256]{1,0:T(8,128)}, f32[512,256]{1,0:T(8,128)S(1)}, u32[]{:S(2)}, u32[]{:S(2)}) collective-permute-start(f32[512,256]{1,0:T(8,128)} %collective-permute-done.11.refs_4_), channel_id=1, source_target_pairs={{0,1},{1,2},{2,3},{3,4},{4,5},{5,6},{6,7},{7,0},{32,39},{33,32},{3... | collective-permute-start | bytes 1572872 | tf_op jit(solution)/shard_map/gather/ppermute | solution.py:33
  73.1 0.7 copy-start.4
  76.4 1.2 copy-start.1
  77.6 1.0 copy-start.3
  81.2 17.5 %collective-permute-start.18 = (f32[8192,256]{1,0:T(8,128)S(1)}, f32[8192,256]{1,0:T(8,128)S(1)}, u32[]{:S(2)}, u32[]{:S(2)}) collective-permute-start(f32[8192,256]{1,0:T(8,128)S(1)} %place.3.panels), channel_id=1, source_target_pairs={{0,32},{32,0},{1,33},{33,1},{2,34},{34,2},{3,35},{35,3},{4,36},{36... | collective-permute-start | bytes 25165832 | tf_op jit(solution)/shard_map/gather/ppermute | solution.py:37
  102.7 22.9 %collective-permute-start.20 = (f32[8,128,256]{2,1,0:T(8,128)S(1)}, f32[8,128,256]{2,1,0:T(8,128)S(1)}, u32[]{:S(2)}, u32[]{:S(2)}) collective-permute-start(f32[8,128,256]{2,1,0:T(8,128)S(1)} %slot_products.5), channel_id=1, source_target_pairs={{0,8},{8,16},{16,24},{24,0},{32,56},{40,32},{48,40},{56,48},{1,9},... | collective-permute-start | bytes 3145736 | tf_op jit(solution)/shard_map/scatter_rows/ppermute | solution.py:33
  115.4 19.5 %collective-permute-start.19 = (f32[8,128,256]{2,1,0:T(8,128)S(1)}, f32[8,128,256]{2,1,0:T(8,128)S(1)}, u32[]{:S(2)}, u32[]{:S(2)}) collective-permute-start(f32[8,128,256]{2,1,0:T(8,128)S(1)} %get-tuple-element.49), channel_id=1, source_target_pairs={{0,24},{8,0},{16,8},{24,16},{32,40},{40,48},{48,56},{56,32},{1,25}... | collective-permute-start | bytes 3145736 | tf_op jit(solution)/shard_map/scatter_rows/ppermute | solution.py:33
  125.7 17.3 %collective-permute-start.21 = (f32[8,128,256]{2,1,0:T(8,128)S(1)}, f32[8,128,256]{2,1,0:T(8,128)S(1)}, u32[]{:S(2)}, u32[]{:S(2)}) collective-permute-start(f32[8,128,256]{2,1,0:T(8,128)S(1)} %add.123), channel_id=1, source_target_pairs={{0,8},{8,16},{16,24},{24,0},{32,56},{40,32},{48,40},{56,48},{1,9},... | collective-permute-start | bytes 3145736 | tf_op jit(solution)/shard_map/scatter_rows/ppermute | solution.py:33
  143.2 4.1 %collective-permute-start.22 = (f32[128,256]{1,0:T(8,128)S(1)}, f32[128,256]{1,0:T(8,128)S(1)}, u32[]{:S(2)}, u32[]{:S(2)}) collective-permute-start(f32[128,256]{1,0:T(8,128)S(1)} %get-tuple-element.63), channel_id=1, source_target_pairs={{0,1},{1,2},{2,3},{3,4},{4,5},{5,6},{6,7},{7,0},{32,39},{33,32},{3... | collective-permute-start | bytes 393224 | tf_op jit(solution)/shard_map/scatter_rows/ppermute | solution.py:33
  147.4 8.1 %collective-permute-start.24 = (f32[2,128,256]{2,1,0:T(8,128)S(1)}, f32[2,128,256]{2,1,0:T(8,128)S(1)}, u32[]{:S(2)}, u32[]{:S(2)}) collective-permute-start(f32[2,128,256]{2,1,0:T(8,128)S(1)} %slice.60), channel_id=1, source_target_pairs={{0,6},{1,7},{2,0},{3,1},{4,2},{5,3},{6,4},{7,5},{32,34},{33,35},{3... | collective-permute-start | bytes 786440 | tf_op jit(solution)/shard_map/scatter_rows/ppermute | solution.py:33
  150.3 9.6 %collective-permute-start.23 = (f32[2,128,256]{2,1,0:T(8,128)S(1)}, f32[2,128,256]{2,1,0:T(8,128)S(1)}, u32[]{:S(2)}, u32[]{:S(2)}) collective-permute-start(f32[2,128,256]{2,1,0:T(8,128)S(1)} %pad_maximum_fusion), channel_id=1, source_target_pairs={{0,2},{1,3},{2,4},{3,5},{4,6},{5,7},{6,0},{7,1},{32,38},{33,39},{3... | collective-permute-start | bytes 786440 | tf_op jit(solution)/shard_map/scatter_rows/ppermute | solution.py:33
  159.9 10.1 %collective-permute-start.26 = (f32[128,256]{1,0:T(8,128)S(1)}, f32[128,256]{1,0:T(8,128)S(1)}, u32[]{:S(2)}, u32[]{:S(2)}) collective-permute-start(f32[128,256]{1,0:T(8,128)S(1)} %get-tuple-element.55), channel_id=1, source_target_pairs={{0,7},{1,0},{2,1},{3,2},{4,3},{5,4},{6,5},{7,6},{32,33},{33,34},{3... | collective-permute-start | bytes 393224 | tf_op jit(solution)/shard_map/scatter_rows/ppermute | solution.py:33
  165.5 5.1 %collective-permute-start.25 = (f32[128,256]{1,0:T(8,128)S(1)}, f32[128,256]{1,0:T(8,128)S(1)}, u32[]{:S(2)}, u32[]{:S(2)}) collective-permute-start(f32[128,256]{1,0:T(8,128)S(1)} %get-tuple-element.54), channel_id=1, source_target_pairs={{0,1},{1,2},{2,3},{3,4},{4,5},{5,6},{6,7},{7,0},{32,39},{33,32},{3... | collective-permute-start | bytes 393224 | tf_op jit(solution)/shard_map/scatter_rows/ppermute | solution.py:33

commit v3 on v0

--- a/solution.py
+++ b/solution.py
@@ -37,6 +37,10 @@
     return lax.ppermute(value, "core", [(0, 1), (1, 0)])
 
 
+def join_rows(top, bottom):
+    return jnp.concatenate([top, bottom], axis=0)
+
+
 def ring_gather(block, axis):
     count = lax.axis_size(axis)
     found = [None] * count
@@ -46,6 +50,8 @@
         ahead = shift(ahead, axis, -1)
         found[count - step] = behind
         found[step] = ahead
+    behind, ahead = lax.optimization_barrier((behind, ahead))
+    found[count // 2 + 1], found[count // 2 - 1] = behind, ahead
     found[count // 2] = shift(behind, axis, 1)
     return found
 
@@ -283,8 +289,11 @@
                         value = value - lower[q, t] * weights[t]
                     weights.append(value)
                 weights = [v * w for v, w in zip(weights, inverse)]
-                for q in range(8):
-                    held[s] = [v - weights[q] * w for v, w in zip(held[s], lines[q])]
+                for c in range(len(held[s])):
+                    terms = [weights[q] * lines[q][c] for q in range(8)]
+                    while len(terms) > 1:
+                        terms = [a + b for a, b in zip(terms[::2], terms[1::2])]
+                    held[s][c] = held[s][c] - terms[0]
             final = [jnp.zeros((8, EDGE), jnp.float32)] * len(held[s0])
             for q in range(8):
                 final = [jnp.where(sub == q, w * root[q], v) for v, w in zip(final, lines[q])]
@@ -385,7 +394,9 @@
     with jax.named_scope("scatter_rows"):
         passing = shift(far, "x", 1)
         from_ahead = shift(behind, "x", -1)
-        own = own + from_ahead + shift(ahead + passing, "x", 1)
+        low, high = ahead[:4] + passing[:4], ahead[4:] + passing[4:]
+        low, high = lax.optimization_barrier((low, high))
+        own = own + from_ahead + join_rows(shift(low, "x", 1), shift(high, "x", 1))
         passing = shift(own[4], "z", 1)
         ahead = jnp.stack([own[2], own[3] + passing])
         ahead, behind = lax.optimization_barrier((ahead, own[5:7]))

time: 218 us -> 222 us (1.018)
  starting transfers between devices: 54.5 us -> 49.8 us
  waiting for transfers between devices: 81.6 us -> 85.8 us
  local copies, waits for them, and re-layouts: 1.71 us -> 5.75 us
  blocking collectives: 42 us -> 45.4 us
  Pallas kernels: 33.7 us -> 30.6 us
    unnamed x2 -> x10, local copies, waits for them, and re-layouts: 0.65 us -> 4.7 us
    ppermute x1, starting transfers between devices: 8.61 us -> 4.93 us  [swap(): return lax.ppermute(value, 'core', [(0, 1), (1, 0)])]
    all_to_all x3, blocking collectives: 42 us -> 45.4 us  [exchange(): return lax.all_to_all(value, axes, 0, 0, tiled=True)]
    pallas_call x3, Pallas kernels: 18.2 us -> 15.6 us  [slot_products(): pl.pallas_call(functools.partial(products_kernel, part), out_shape=shapes...]
    ppermute x28 -> x29, waiting for transfers between devices: 74.9 us -> 77.1 us  [shift(): return lax.ppermute(value, ('core', axis), pairs)]
    ppermute x28 -> x29, starting transfers between devices: 45.9 us -> 44.8 us  [shift(): return lax.ppermute(value, ('core', axis), pairs)]
  transfers between devices with their start and end apart: 29 -> 30, of which waited for: 19 -> 22; matrix products, arithmetic and copies ran while one was open for 1% -> 1% of each run, Pallas kernels for 9% -> 7%
where the time goes in v3:
time: 222 us; the launch traced here: 221 us
  waiting for transfers between devices  85.8 us (39%)
  starting transfers between devices  49.8 us (22%)
  blocking collectives  45.4 us (20%)
  Pallas kernels  30.6 us (14%)
  local copies, waits for them, and re-layouts  5.75 us (3%)
    ppermute x29, waiting for transfers between devices, shift(): return lax.ppermute(value, ('core', axis), pairs)  77.1 us
    all_to_all x3, blocking collectives, exchange(): return lax.all_to_all(value, axes, 0, 0, tiled=True)  45.4 us
    ppermute x29, starting transfers between devices, shift(): return lax.ppermute(value, ('core', axis), pairs)  44.8 us
    pallas_call x3, Pallas kernels, slot_products(): pl.pallas_call(functools.partial(products_kernel, part), out_shape=shapes...  15.6 us
    pallas_call x1, Pallas kernels, factor_and_solve(): pl.pallas_call(factor_kernel, out_shape=[jax.ShapeDtypeStruct((EDGE, WIDT...  9.8 us
    ppermute x1, waiting for transfers between devices, swap(): return lax.ppermute(value, 'core', [(0, 1), (1, 0)])  8.7 us
    ppermute x1, starting transfers between devices, swap(): return lax.ppermute(value, 'core', [(0, 1), (1, 0)])  4.93 us
    unnamed x10, local copies, waits for them, and re-layouts  4.7 us
  transfers between devices with their start and end apart: 30, of which 22 were waited for; matrix products, arithmetic and copies ran while one was open for 1% of the time, Pallas kernels for 7%

profile of v3, /device:TPU:1, one launch (start us, length us, event | category | flops | bytes accessed | tf_op | source)
XLA Modules:
  0.0 220.7 jit_solution(6820932748132952038)
XLA Ops:
  0.6 1.0 constant_dynamic-slice_fusion.1
  1.6 6.5 %collective-permute-start.11 = (f32[128,256]{1,0:T(8,128)S(1)}, f32[128,256]{1,0:T(8,128)S(1)}, u32[]{:S(2)}, u32[]{:S(2)}) collective-permute-start(f32[128,256]{1,0:T(8,128)S(1)} %get-tuple-element.64.refs_0_), channel_id=1, source_target_pairs={{0,1},{1,2},{2,3},{3,4},{4,5},{5,6},{6,7},{7,0},{32,39},{33,32},{3... | collective-permute-start | bytes 393224 | tf_op jit(solution)/shard_map/gather/ppermute | solution.py:33
  8.1 1.9 collective-permute-done.11.refs_7_
  10.1 3.5 %collective-permute-start.12 = (f32[128,256]{1,0:T(8,128)S(1)}, f32[128,256]{1,0:T(8,128)S(1)}, u32[]{:S(2)}, u32[]{:S(2)}) collective-permute-start(f32[128,256]{1,0:T(8,128)S(1)} %collective-permute-done.11.refs_7_), channel_id=1, source_target_pairs={{0,1},{1,2},{2,3},{3,4},{4,5},{5,6},{6,7},{7,0},{32,39},{33,32},{3... | collective-permute-start | bytes 393224 | tf_op jit(solution)/shard_map/gather/ppermute | solution.py:33
  13.6 2.5 %collective-permute-start = (f32[128,256]{1,0:T(8,128)S(1)}, f32[128,256]{1,0:T(8,128)S(1)}, u32[]{:S(2)}, u32[]{:S(2)}) collective-permute-start(f32[128,256]{1,0:T(8,128)S(1)} %get-tuple-element.65.refs_0_), channel_id=1, source_target_pairs={{0,8},{8,16},{16,24},{24,0},{32,56},{40,32},{48,40},{56,48},{1,9},... | collective-permute-start | bytes 393224 | tf_op jit(solution)/shard_map/gather/ppermute | solution.py:33
  16.1 2.7 %collective-permute-start.13 = (f32[128,256]{1,0:T(8,128)S(1)}, f32[128,256]{1,0:T(8,128)S(1)}, u32[]{:S(2)}, u32[]{:S(2)}) collective-permute-start(f32[128,256]{1,0:T(8,128)S(1)} %collective-permute-done.12.refs_6_), channel_id=1, source_target_pairs={{0,1},{1,2},{2,3},{3,4},{4,5},{5,6},{6,7},{7,0},{32,39},{33,32},{3... | collective-permute-start | bytes 393224 | tf_op jit(solution)/shard_map/gather/ppermute | solution.py:33
  18.8 0.2 collective-permute-done.10.refs_2_
  18.9 3.7 %collective-permute-done.1.refs_1_ = f32[128,256]{1,0:T(8,128)S(1)} collective-permute-done((f32[128,256]{1,0:T(8,128)S(1)}, f32[128,256]{1,0:T(8,128)S(1)}, u32[]{:S(2)}, u32[]{:S(2)}) %collective-permute-start.1) | collective-permute-done | bytes 131104 | tf_op jit(solution)/shard_map/gather/ppermute | solution.py:33
  22.6 2.7 %collective-permute-done.14.refs_3_ = f32[128,256]{1,0:T(8,128)S(1)} collective-permute-done((f32[128,256]{1,0:T(8,128)S(1)}, f32[128,256]{1,0:T(8,128)S(1)}, u32[]{:S(2)}, u32[]{:S(2)}) %collective-permute-start.14) | collective-permute-done | bytes 131104 | tf_op jit(solution)/shard_map/gather/ppermute | solution.py:33
  25.3 1.1 collective-permute-done.2.refs_2_
  26.5 1.5 collective-permute-start.5
  28.0 1.1 collective-permute-done.15.refs_4_
  29.1 0.1 join.3.refs_7_
  29.2 2.9 %collective-permute-start.16 = (f32[1024,256]{1,0:T(8,128)S(1)}, f32[1024,256]{1,0:T(8,128)}, u32[]{:S(2)}, u32[]{:S(2)}) collective-permute-start(f32[1024,256]{1,0:T(8,128)S(1)} %join.3.refs_7_), channel_id=1, source_target_pairs={{0,8},{8,16},{16,24},{24,0},{32,56},{40,32},{48,40},{56,48},{1,9},... | collective-permute-start | bytes 3145736 | tf_op jit(solution)/shard_map/gather/ppermute | solution.py:33
  32.1 3.7 %collective-permute-done.5.refs_6_ = f32[512,256]{1,0:T(8,128)S(1)} collective-permute-done((f32[512,256]{1,0:T(8,128)S(1)}, f32[512,256]{1,0:T(8,128)S(1)}, u32[]{:S(2)}, u32[]{:S(2)}) %collective-permute-start.5) | collective-permute-done | bytes 524320 | tf_op jit(solution)/shard_map/gather/ppermute | solution.py:33
  35.8 2.6 %collective-permute-start.6 = (f32[512,256]{1,0:T(8,128)S(1)}, f32[512,256]{1,0:T(8,128)}, u32[]{:S(2)}, u32[]{:S(2)}) collective-permute-start(f32[512,256]{1,0:T(8,128)S(1)} %collective-permute-done.5.refs_6_), channel_id=1, source_target_pairs={{0,1},{1,2},{2,3},{3,4},{4,5},{5,6},{6,7},{7,0},{32,39},{33,32},{3... | collective-permute-start | bytes 1572872 | tf_op jit(solution)/shard_map/gather/ppermute | solution.py:33
  38.4 3.1 %collective-permute-done.3.refs_1_ = f32[512,256]{1,0:T(8,128)S(1)} collective-permute-done((f32[512,256]{1,0:T(8,128)S(1)}, f32[512,256]{1,0:T(8,128)S(1)}, u32[]{:S(2)}, u32[]{:S(2)}) %collective-permute-start.3) | collective-permute-done | bytes 524320 | tf_op jit(solution)/shard_map/gather/ppermute | solution.py:33
  41.4 0.8 copy-done.2
  42.3 4.1 %collective-permute-done.6.refs_5_ = f32[512,256]{1,0:T(8,128)} collective-permute-done((f32[512,256]{1,0:T(8,128)S(1)}, f32[512,256]{1,0:T(8,128)}, u32[]{:S(2)}, u32[]{:S(2)}) %collective-permute-start.6) | collective-permute-done | bytes 524320 | tf_op jit(solution)/shard_map/gather/ppermute | solution.py:33
  46.4 2.5 %collective-permute-start.7 = (f32[512,256]{1,0:T(8,128)}, f32[512,256]{1,0:T(8,128)}, u32[]{:S(2)}, u32[]{:S(2)}) collective-permute-start(f32[512,256]{1,0:T(8,128)} %collective-permute-done.6.refs_5_), channel_id=1, source_target_pairs={{0,1},{1,2},{2,3},{3,4},{4,5},{5,6},{6,7},{7,0},{32,39},{33,32},{3... | collective-permute-start | bytes 1572872 | tf_op jit(solution)/shard_map/gather/ppermute | solution.py:33
  48.9 5.2 %collective-permute-done.4.refs_2_ = f32[512,256]{1,0:T(8,128)} collective-permute-done((f32[512,256]{1,0:T(8,128)S(1)}, f32[512,256]{1,0:T(8,128)}, u32[]{:S(2)}, u32[]{:S(2)}) %collective-permute-start.4) | collective-permute-done | bytes 524320 | tf_op jit(solution)/shard_map/gather/ppermute | solution.py:33
  54.1 3.5 %collective-permute-done.17.refs_8_ = f32[1024,256]{1,0:T(8,128)S(1)} collective-permute-done((f32[1024,256]{1,0:T(8,128)S(1)}, f32[1024,256]{1,0:T(8,128)S(1)}, u32[]{:S(2)}, u32[]{:S(2)}) %collective-permute-start.17) | collective-permute-done | bytes 1048608 | tf_op jit(solution)/shard_map/gather/ppermute | solution.py:33
  57.5 1.0 copy-done
  58.5 1.2 collective-permute-start.19
  59.7 6.3 %collective-permute-done.8.refs_3_ = f32[512,256]{1,0:T(8,128)} collective-permute-done((f32[512,256]{1,0:T(8,128)}, f32[512,256]{1,0:T(8,128)}, u32[]{:S(2)}, u32[]{:S(2)}) %collective-permute-start.8) | collective-permute-done | bytes 524320 | tf_op jit(solution)/shard_map/gather/ppermute | solution.py:33
  66.0 0.2 collective-permute-start.18
  66.1 0.8 select_reduce_fusion
  66.9 0.7 compare_select_fusion.10
  67.7 0.6 copy-done.4
  68.3 2.6 %slot_plan.1 = (s32[192]{0:T(256)S(1)}, s32[192]{0:T(256)S(1)}, s32[192]{0:T(256)S(1)}, s32[3]{0:T(128)S(1)}) custom-call(s32[32]{0:T(128)S(1)} %bitcast.31, s32[192]{0:T(256)S(1)} %get-tuple-element.56.kind), custom_call_target="tpu_custom_call" | custom-call | bytes 12582912 | tf_op jit(solution)/shard_map/gather/slot_plan/pallas_call | solution.py:133
  71.0 1.2 copy-done.1
  72.2 1.0 copy-done.3
  73.2 2.4 %place.2.refs_0_ = f32[8192,256]{1,0:T(8,128)S(1)} custom-call(f32[512,256]{1,0:T(8,128)S(1)} %join.2.refs_0_, f32[512,256]{1,0:T(8,128)S(1)} %copy-done.3, f32[512,256]{1,0:T(8,128)} %collective-permute-done.4.refs_2_, f32[512,256]{1,0:T(8,128)} %collective-permute-done.8.refs_3_, f32[512,256]{1,0:T(8,128)} %collective-permute-done.7.refs_4_, ...), custom_call_target="tpu_custom_call" | custom-call | bytes 13631488 | tf_op jit(solution)/shard_map/gather/place/pallas_call | solution.py:100
  75.7 0.1 place.3.panels
  75.8 4.9 %collective-permute-start.20 = (f32[8192,256]{1,0:T(8,128)S(1)}, f32[8192,256]{1,0:T(8,128)S(1)}, u32[]{:S(2)}, u32[]{:S(2)}) collective-permute-start(f32[8192,256]{1,0:T(8,128)S(1)} %place.3.panels), channel_id=1, source_target_pairs={{0,32},{32,0},{1,33},{33,1},{2,34},{34,2},{3,35},{35,3},{4,36},{36... | collective-permute-start | bytes 25165832 | tf_op jit(solution)/shard_map/gather/ppermute | solution.py:37
  80.8 4.1 %slot_products.3.refs_0_ = f32[32,128,256]{2,1,0:T(8,128)S(1)} custom-call(s32[3]{0:T(128)S(1)} %get-tuple-element.34.counts, s32[192]{0:T(256)S(1)} %get-tuple-element.43.listed, s32[192]{0:T(256)S(1)} %get-tuple-element.54.blk, s32[192]{0:T(256)S(1)} %get-tuple-element.57.row, f32[192,128,128]{2,1,0:T(8,128)} %bitcast.32, f32[8192,256]{1,0:T(8,128)S(1)} %place.3.panels), custom_call_target="tpu_custom_call" | custom-call | flops 3221225472 | bytes 12582912 | tf_op jit(solution)/shard_map/slot_products/pallas_call | solution.py:223
  84.8 8.7 %collective-permute-done.20.panels = f32[8192,256]{1,0:T(8,128)S(1)} collective-permute-done((f32[8192,256]{1,0:T(8,128)S(1)}, f32[8192,256]{1,0:T(8,128)S(1)}, u32[]{:S(2)}, u32[]{:S(2)}) %collective-permute-start.20) | collective-permute-done | bytes 8388640 | tf_op jit(solution)/shard_map/gather/ppermute | solution.py:37
  93.5 4.3 %slot_products.5 = f32[8,128,256]{2,1,0:T(8,128)S(1)} custom-call(s32[3]{0:T(128)S(1)} %get-tuple-element.34.counts, s32[192]{0:T(256)S(1)} %get-tuple-element.47.listed, s32[192]{0:T(256)S(1)} %get-tuple-element.54.blk, s32[192]{0:T(256)S(1)} %get-tuple-element.57.row, f32[192,128,128]{2,1,0:T(8,128)} %bitcast.33, ...), custom_call_target="tpu_custom_call" | custom-call | flops 805306368 | bytes 3145728 | tf_op jit(solution)/shard_map/slot_products/pallas_call | solution.py:223
  97.9 5.3 %collective-permute-start.22 = (f32[8,128,256]{2,1,0:T(8,128)S(1)}, f32[8,128,256]{2,1,0:T(8,128)S(1)}, u32[]{:S(2)}, u32[]{:S(2)}) collective-permute-start(f32[8,128,256]{2,1,0:T(8,128)S(1)} %slot_products.5), channel_id=1, source_target_pairs={{0,8},{8,16},{16,24},{24,0},{32,56},{40,32},{48,40},{56,48},{1,9},... | collective-permute-start | bytes 3145736 | tf_op jit(solution)/shard_map/scatter_rows/ppermute | solution.py:33
  103.2 7.2 %slot_products.4 = (f32[8,128,256]{2,1,0:T(8,128)S(1)}, f32[8,128,256]{2,1,0:T(8,128)S(1)}, f32[8,128,256]{2,1,0:T(8,128)S(1)}) custom-call(s32[3]{0:T(128)S(1)} %get-tuple-element.34.counts, s32[192]{0:T(256)S(1)} %get-tuple-element.35.listed, s32[192]{0:T(256)S(1)} %get-tuple-element.54.blk, s32[192]{0:T(256)S(1)} %get-tuple-element.57.row, ...), custom_call_target="tpu_custom_call" | custom-call | flops 2415919104 | bytes 9437184 | tf_op jit(solution)/shard_map/slot_products/pallas_call | solution.py:223
  110.4 0.1 collective-permute-start.21
  110.5 11.2 %collective-permute-done.22 = f32[8,128,256]{2,1,0:T(8,128)S(1)} collective-permute-done((f32[8,128,256]{2,1,0:T(8,128)S(1)}, f32[8,128,256]{2,1,0:T(8,128)S(1)}, u32[]{:S(2)}, u32[]{:S(2)}) %collective-permute-start.22) | collective-permute-done | bytes 1048608 | tf_op jit(solution)/shard_map/scatter_rows/ppermute | solution.py:33
  121.6 0.1 slice_add_fusion
  121.8 3.5 %collective-permute-start.23 = (f32[4,128,256]{2,1,0:T(8,128)S(1)}, f32[4,128,256]{2,1,0:T(8,128)S(1)}, u32[]{:S(2)}, u32[]{:S(2)}) collective-permute-start(f32[4,128,256]{2,1,0:T(8,128)S(1)} %get-tuple-element.48), channel_id=1, source_target_pairs={{0,8},{8,16},{16,24},{24,0},{32,56},{40,32},{48,40},{56,48},{1,9},... | collective-permute-start | bytes 1572872 | tf_op jit(solution)/shard_map/scatter_rows/ppermute | solution.py:33
  125.3 0.1 collective-permute-start.24
  125.4 5.8 %collective-permute-done.21 = f32[8,128,256]{2,1,0:T(8,128)S(1)} collective-permute-done((f32[8,128,256]{2,1,0:T(8,128)S(1)}, f32[8,128,256]{2,1,0:T(8,128)S(1)}, u32[]{:S(2)}, u32[]{:S(2)}) %collective-permute-start.21) | collective-permute-done | bytes 1048608 | tf_op jit(solution)/shard_map/scatter_rows/ppermute | solution.py:33
  131.2 0.6 collective-permute-done.23
  131.8 5.6 %collective-permute-done.24 = f32[4,128,256]{2,1,0:T(8,128)S(1)} collective-permute-done((f32[4,128,256]{2,1,0:T(8,128)S(1)}, f32[4,128,256]{2,1,0:T(8,128)S(1)}, u32[]{:S(2)}, u32[]{:S(2)}) %collective-permute-start.24) | collective-permute-done | bytes 524320 | tf_op jit(solution)/shard_map/scatter_rows/ppermute | solution.py:33
  137.4 0.2 maximum_add_fusion
  137.6 2.0 collective-permute-start.25
  139.6 1.9 collective-permute-done.25
  141.6 1.9 collective-permute-start.26
  143.5 3.2 %collective-permute-start.27 = (f32[2,128,256]{2,1,0:T(8,128)S(1)}, f32[2,128,256]{2,1,0:T(8,128)S(1)}, u32[]{:S(2)}, u32[]{:S(2)}) collective-permute-start(f32[2,128,256]{2,1,0:T(8,128)S(1)} %slice.74), channel_id=1, source_target_pairs={{0,6},{1,7},{2,0},{3,1},{4,2},{5,3},{6,4},{7,5},{32,34},{33,35},{3... | collective-permute-start | bytes 786440 | tf_op jit(solution)/shard_map/scatter_rows/ppermute | solution.py:33
  146.7 10.6 %collective-permute-done.26 = f32[2,128,256]{2,1,0:T(8,128)S(1)} collective-permute-done((f32[2,128,256]{2,1,0:T(8,128)S(1)}, f32[2,128,256]{2,1,0:T(8,128)S(1)}, u32[]{:S(2)}, u32[]{:S(2)}) %collective-permute-start.26) | collective-permute-done | bytes 262176 | tf_op jit(solution)/shard_map/scatter_rows/ppermute | solution.py:33
  157.3 1.5 collective-permute-done.27
  158.8 0.6 collective-permute-start.28
  159.4 2.2 collective-permute-start.29
  161.6 2.3 %collective-permute-done.28 = f32[128,256]{1,0:T(8,128)S(1)} collective-permute-done((f32[128,256]{1,0:T(8,128)S(1)}, f32[128,256]{1,0:T(8,128)S(1)}, u32[]{:S(2)}, u32[]{:S(2)}) %collective-permute-start.28) | collective-permute-done | bytes 131104 | tf_op jit(solution)/shard_map/scatter_rows/ppermute | solution.py:33
  163.9 1.0 collective-permute-done.29
  164.9 0.4 convolution_bitcast_fusion
  165.4 17.8 %all_to_all.19 = f32[32,8,256]{2,1,0:T(8,128)S(1)} all-to-all(f32[32,8,256]{2,1,0:T(8,128)S(1)} %convolution_bitcast_fusion), channel_id=1, replica_groups=mesh['y'=4,'core'=2,'x'=4,'z'=8] {'y','core','x'}, dimensions={0} | all-to-all | bytes 524288 | tf_op jit(solution)/shard_map/gram/all_to_all | solution.py:345
  183.3 13.3 %all_to_all.20 = f32[8,8,256]{2,1,0:T(8,128)S(1)} all-to-all(f32[8,8,256]{2,1,0:T(8,128)S(1)} %broadcast_in_dim.39), channel_id=1, replica_groups=mesh['y'=4,'core'=2,'x'=4,'z'=8] {'z'}, dimensions={0} | all-to-all | bytes 131072 | tf_op jit(solution)/shard_map/gram/all_to_all | solution.py:345
  196.6 14.3 %all_to_all.21 = f32[32,8,256]{2,1,0:T(8,128)S(1)} all-to-all(f32[32,8,256]{2,1,0:T(8,128)S(1)} %broadcast_in_dim.40), channel_id=1, replica_groups=mesh['y'=4,'core'=2,'x'=4,'z'=8] {'y','core','x'}, dimensions={0} | all-to-all | bytes 524288 | tf_op jit(solution)/shard_map/gram/all_to_all | solution.py:345
  210.9 9.8 %factor_and_solve.1 = (f32[128,256]{1,0:T(8,128)}, f32[256,256]{1,0:T(8,128)}) custom-call(f32[256,256]{1,0:T(8,128)S(1)} %bitcast.30, f32[128,256]{1,0:T(8,128)S(1)} %fusion.4.rows), custom_call_target="tpu_custom_call" | custom-call | tf_op jit(solution)/shard_map/factor_and_solve/pallas_call | solution.py:330
  (35 shorter events, 0.4 us)
Async XLA Ops:
  1.6 8.4 %collective-permute-start.11 = (f32[128,256]{1,0:T(8,128)S(1)}, f32[128,256]{1,0:T(8,128)S(1)}, u32[]{:S(2)}, u32[]{:S(2)}) collective-permute-start(f32[128,256]{1,0:T(8,128)S(1)} %get-tuple-element.64.refs_0_), channel_id=1, source_target_pairs={{0,1},{1,2},{2,3},{3,4},{4,5},{5,6},{6,7},{7,0},{32,39},{33,32},{3... | collective-permute-start | bytes 393224 | tf_op jit(solution)/shard_map/gather/ppermute | solution.py:33
  8.1 5.5 %collective-permute-start.9 = (f32[128,256]{1,0:T(8,128)S(1)}, f32[128,256]{1,0:T(8,128)S(1)}, u32[]{:S(2)}, u32[]{:S(2)}) collective-permute-start(f32[128,256]{1,0:T(8,128)S(1)} %get-tuple-element.64.refs_0_), channel_id=1, source_target_pairs={{0,7},{1,0},{2,1},{3,2},{4,3},{5,4},{6,5},{7,6},{32,33},{33,34},{3... | collective-permute-start | bytes 393224 | tf_op jit(solution)/shard_map/gather/ppermute | solution.py:33
  10.1 6.0 %collective-permute-start.12 = (f32[128,256]{1,0:T(8,128)S(1)}, f32[128,256]{1,0:T(8,128)S(1)}, u32[]{:S(2)}, u32[]{:S(2)}) collective-permute-start(f32[128,256]{1,0:T(8,128)S(1)} %collective-permute-done.11.refs_7_), channel_id=1, source_target_pairs={{0,1},{1,2},{2,3},{3,4},{4,5},{5,6},{6,7},{7,0},{32,39},{33,32},{3... | collective-permute-start | bytes 393224 | tf_op jit(solution)/shard_map/gather/ppermute | solution.py:33
  13.6 5.3 %collective-permute-start.10 = (f32[128,256]{1,0:T(8,128)S(1)}, f32[128,256]{1,0:T(8,128)S(1)}, u32[]{:S(2)}, u32[]{:S(2)}) collective-permute-start(f32[128,256]{1,0:T(8,128)S(1)} %collective-permute-done.9.refs_1_), channel_id=1, source_target_pairs={{0,7},{1,0},{2,1},{3,2},{4,3},{5,4},{6,5},{7,6},{32,33},{33,34},{3... | collective-permute-start | bytes 393224 | tf_op jit(solution)/shard_map/gather/ppermute | solution.py:33
  13.6 5.3 %collective-permute-start = (f32[128,256]{1,0:T(8,128)S(1)}, f32[128,256]{1,0:T(8,128)S(1)}, u32[]{:S(2)}, u32[]{:S(2)}) collective-permute-start(f32[128,256]{1,0:T(8,128)S(1)} %get-tuple-element.65.refs_0_), channel_id=1, source_target_pairs={{0,8},{8,16},{16,24},{24,0},{32,56},{40,32},{48,40},{56,48},{1,9},... | collective-permute-start | bytes 393224 | tf_op jit(solution)/shard_map/gather/ppermute | solution.py:33
  16.1 6.5 %collective-permute-start.1 = (f32[128,256]{1,0:T(8,128)S(1)}, f32[128,256]{1,0:T(8,128)S(1)}, u32[]{:S(2)}, u32[]{:S(2)}) collective-permute-start(f32[128,256]{1,0:T(8,128)S(1)} %get-tuple-element.65.refs_0_), channel_id=1, source_target_pairs={{0,24},{8,0},{16,8},{24,16},{32,40},{40,48},{48,56},{56,32},{1,25}... | collective-permute-start | bytes 393224 | tf_op jit(solution)/shard_map/gather/ppermute | solution.py:33
  16.1 6.5 %collective-permute-start.13 = (f32[128,256]{1,0:T(8,128)S(1)}, f32[128,256]{1,0:T(8,128)S(1)}, u32[]{:S(2)}, u32[]{:S(2)}) collective-permute-start(f32[128,256]{1,0:T(8,128)S(1)} %collective-permute-done.12.refs_6_), channel_id=1, source_target_pairs={{0,1},{1,2},{2,3},{3,4},{4,5},{5,6},{6,7},{7,0},{32,39},{33,32},{3... | collective-permute-start | bytes 393224 | tf_op jit(solution)/shard_map/gather/ppermute | solution.py:33
  18.9 6.4 %collective-permute-start.14 = (f32[128,256]{1,0:T(8,128)S(1)}, f32[128,256]{1,0:T(8,128)S(1)}, u32[]{:S(2)}, u32[]{:S(2)}) collective-permute-start(f32[128,256]{1,0:T(8,128)S(1)} %collective-permute-done.10.refs_2_), channel_id=1, source_target_pairs={{0,7},{1,0},{2,1},{3,2},{4,3},{5,4},{6,5},{7,6},{32,33},{33,34},{3... | collective-permute-start | bytes 393224 | tf_op jit(solution)/shard_map/gather/ppermute | solution.py:33
  22.6 3.8 %collective-permute-start.2 = (f32[128,256]{1,0:T(8,128)S(1)}, f32[128,256]{1,0:T(8,128)S(1)}, u32[]{:S(2)}, u32[]{:S(2)}) collective-permute-start(f32[128,256]{1,0:T(8,128)S(1)} %collective-permute-done.refs_3_), channel_id=1, source_target_pairs={{0,8},{8,16},{16,24},{24,0},{32,56},{40,32},{48,40},{56,48},{1,9},... | collective-permute-start | bytes 393224 | tf_op jit(solution)/shard_map/gather/ppermute | solution.py:33
  25.3 3.8 %collective-permute-start.15 = (f32[128,256]{1,0:T(8,128)S(1)}, f32[128,256]{1,0:T(8,128)S(1)}, u32[]{:S(2)}, u32[]{:S(2)}) collective-permute-start(f32[128,256]{1,0:T(8,128)S(1)} %collective-permute-done.13.refs_5_), channel_id=1, source_target_pairs={{0,1},{1,2},{2,3},{3,4},{4,5},{5,6},{6,7},{7,0},{32,39},{33,32},{3... | collective-permute-start | bytes 393224 | tf_op jit(solution)/shard_map/gather/ppermute | solution.py:33
  26.5 9.3 %collective-permute-start.5 = (f32[512,256]{1,0:T(8,128)S(1)}, f32[512,256]{1,0:T(8,128)S(1)}, u32[]{:S(2)}, u32[]{:S(2)}) collective-permute-start(f32[512,256]{1,0:T(8,128)S(1)} %join.2.refs_0_), channel_id=1, source_target_pairs={{0,1},{1,2},{2,3},{3,4},{4,5},{5,6},{6,7},{7,0},{32,39},{33,32},{3... | collective-permute-start | bytes 1572872 | tf_op jit(solution)/shard_map/gather/ppermute | solution.py:33
  28.0 13.4 %collective-permute-start.3 = (f32[512,256]{1,0:T(8,128)S(1)}, f32[512,256]{1,0:T(8,128)S(1)}, u32[]{:S(2)}, u32[]{:S(2)}) collective-permute-start(f32[512,256]{1,0:T(8,128)S(1)} %join.2.refs_0_), channel_id=1, source_target_pairs={{0,7},{1,0},{2,1},{3,2},{4,3},{5,4},{6,5},{7,6},{32,33},{33,34},{3... | collective-permute-start | bytes 1572872 | tf_op jit(solution)/shard_map/gather/ppermute | solution.py:33
  29.2 24.8 %collective-permute-start.16 = (f32[1024,256]{1,0:T(8,128)S(1)}, f32[1024,256]{1,0:T(8,128)}, u32[]{:S(2)}, u32[]{:S(2)}) collective-permute-start(f32[1024,256]{1,0:T(8,128)S(1)} %join.3.refs_7_), channel_id=1, source_target_pairs={{0,8},{8,16},{16,24},{24,0},{32,56},{40,32},{48,40},{56,48},{1,9},... | collective-permute-start | bytes 3145736 | tf_op jit(solution)/shard_map/gather/ppermute | solution.py:33
  32.1 25.4 %collective-permute-start.17 = (f32[1024,256]{1,0:T(8,128)S(1)}, f32[1024,256]{1,0:T(8,128)S(1)}, u32[]{:S(2)}, u32[]{:S(2)}) collective-permute-start(f32[1024,256]{1,0:T(8,128)S(1)} %join.3.refs_7_), channel_id=1, source_target_pairs={{0,24},{8,0},{16,8},{24,16},{32,40},{40,48},{48,56},{56,32},{1,25}... | collective-permute-start | bytes 3145736 | tf_op jit(solution)/shard_map/gather/ppermute | solution.py:33
  35.8 10.6 %collective-permute-start.6 = (f32[512,256]{1,0:T(8,128)S(1)}, f32[512,256]{1,0:T(8,128)}, u32[]{:S(2)}, u32[]{:S(2)}) collective-permute-start(f32[512,256]{1,0:T(8,128)S(1)} %collective-permute-done.5.refs_6_), channel_id=1, source_target_pairs={{0,1},{1,2},{2,3},{3,4},{4,5},{5,6},{6,7},{7,0},{32,39},{33,32},{3... | collective-permute-start | bytes 1572872 | tf_op jit(solution)/shard_map/gather/ppermute | solution.py:33
  41.4 12.6 %collective-permute-start.4 = (f32[512,256]{1,0:T(8,128)S(1)}, f32[512,256]{1,0:T(8,128)}, u32[]{:S(2)}, u32[]{:S(2)}) collective-permute-start(f32[512,256]{1,0:T(8,128)S(1)} %collective-permute-done.3.refs_1_), channel_id=1, source_target_pairs={{0,7},{1,0},{2,1},{3,2},{4,3},{5,4},{6,5},{7,6},{32,33},{33,34},{3... | collective-permute-start | bytes 1572872 | tf_op jit(solution)/shard_map/gather/ppermute | solution.py:33
  41.4 0.8 copy-start.2
  46.4 13.3 %collective-permute-start.7 = (f32[512,256]{1,0:T(8,128)}, f32[512,256]{1,0:T(8,128)}, u32[]{:S(2)}, u32[]{:S(2)}) collective-permute-start(f32[512,256]{1,0:T(8,128)} %collective-permute-done.6.refs_5_), channel_id=1, source_target_pairs={{0,1},{1,2},{2,3},{3,4},{4,5},{5,6},{6,7},{7,0},{32,39},{33,32},{3... | collective-permute-start | bytes 1572872 | tf_op jit(solution)/shard_map/gather/ppermute | solution.py:33
  54.1 11.9 %collective-permute-start.8 = (f32[512,256]{1,0:T(8,128)}, f32[512,256]{1,0:T(8,128)}, u32[]{:S(2)}, u32[]{:S(2)}) collective-permute-start(f32[512,256]{1,0:T(8,128)} %collective-permute-done.4.refs_2_), channel_id=1, source_target_pairs={{0,7},{1,0},{2,1},{3,2},{4,3},{5,4},{6,5},{7,6},{32,33},{33,34},{3... | collective-permute-start | bytes 1572872 | tf_op jit(solution)/shard_map/gather/ppermute | solution.py:33
  57.5 1.0 copy-start
  58.5 17.2 %collective-permute-start.19 = (f32[1024,256]{1,0:T(8,128)}, f32[1024,256]{1,0:T(8,128)S(1)}, u32[]{:S(2)}, u32[]{:S(2)}) collective-permute-start(f32[1024,256]{1,0:T(8,128)} %collective-permute-done.16.refs_9_), channel_id=1, source_target_pairs={{0,8},{8,16},{16,24},{24,0},{32,56},{40,32},{48,40},{56,48},{1,9},... | collective-permute-start | bytes 3145736 | tf_op jit(solution)/shard_map/gather/ppermute | solution.py:33
  66.0 9.7 %collective-permute-start.18 = (f32[512,256]{1,0:T(8,128)}, f32[512,256]{1,0:T(8,128)S(1)}, u32[]{:S(2)}, u32[]{:S(2)}) collective-permute-start(f32[512,256]{1,0:T(8,128)} %collective-permute-done.7.refs_4_), channel_id=1, source_target_pairs={{0,1},{1,2},{2,3},{3,4},{4,5},{5,6},{6,7},{7,0},{32,39},{33,32},{3... | collective-permute-start | bytes 1572872 | tf_op jit(solution)/shard_map/gather/ppermute | solution.py:33
  67.7 0.7 copy-start.4
  71.0 1.2 copy-start.1
  72.2 1.0 copy-start.3
  75.8 17.7 %collective-permute-start.20 = (f32[8192,256]{1,0:T(8,128)S(1)}, f32[8192,256]{1,0:T(8,128)S(1)}, u32[]{:S(2)}, u32[]{:S(2)}) collective-permute-start(f32[8192,256]{1,0:T(8,128)S(1)} %place.3.panels), channel_id=1, source_target_pairs={{0,32},{32,0},{1,33},{33,1},{2,34},{34,2},{3,35},{35,3},{4,36},{36... | collective-permute-start | bytes 25165832 | tf_op jit(solution)/shard_map/gather/ppermute | solution.py:37
  97.9 23.8 %collective-permute-start.22 = (f32[8,128,256]{2,1,0:T(8,128)S(1)}, f32[8,128,256]{2,1,0:T(8,128)S(1)}, u32[]{:S(2)}, u32[]{:S(2)}) collective-permute-start(f32[8,128,256]{2,1,0:T(8,128)S(1)} %slot_products.5), channel_id=1, source_target_pairs={{0,8},{8,16},{16,24},{24,0},{32,56},{40,32},{48,40},{56,48},{1,9},... | collective-permute-start | bytes 3145736 | tf_op jit(solution)/shard_map/scatter_rows/ppermute | solution.py:33
  110.4 20.8 %collective-permute-start.21 = (f32[8,128,256]{2,1,0:T(8,128)S(1)}, f32[8,128,256]{2,1,0:T(8,128)S(1)}, u32[]{:S(2)}, u32[]{:S(2)}) collective-permute-start(f32[8,128,256]{2,1,0:T(8,128)S(1)} %get-tuple-element.45), channel_id=1, source_target_pairs={{0,24},{8,0},{16,8},{24,16},{32,40},{40,48},{48,56},{56,32},{1,25}... | collective-permute-start | bytes 3145736 | tf_op jit(solution)/shard_map/scatter_rows/ppermute | solution.py:33
  121.8 10.0 %collective-permute-start.23 = (f32[4,128,256]{2,1,0:T(8,128)S(1)}, f32[4,128,256]{2,1,0:T(8,128)S(1)}, u32[]{:S(2)}, u32[]{:S(2)}) collective-permute-start(f32[4,128,256]{2,1,0:T(8,128)S(1)} %get-tuple-element.48), channel_id=1, source_target_pairs={{0,8},{8,16},{16,24},{24,0},{32,56},{40,32},{48,40},{56,48},{1,9},... | collective-permute-start | bytes 1572872 | tf_op jit(solution)/shard_map/scatter_rows/ppermute | solution.py:33
  125.3 12.1 %collective-permute-start.24 = (f32[4,128,256]{2,1,0:T(8,128)S(1)}, f32[4,128,256]{2,1,0:T(8,128)S(1)}, u32[]{:S(2)}, u32[]{:S(2)}) collective-permute-start(f32[4,128,256]{2,1,0:T(8,128)S(1)} %get-tuple-element.49), channel_id=1, source_target_pairs={{0,8},{8,16},{16,24},{24,0},{32,56},{40,32},{48,40},{56,48},{1,9},... | collective-permute-start | bytes 1572872 | tf_op jit(solution)/shard_map/scatter_rows/ppermute | solution.py:33
  137.6 3.9 %collective-permute-start.25 = (f32[128,256]{1,0:T(8,128)S(1)}, f32[128,256]{1,0:T(8,128)S(1)}, u32[]{:S(2)}, u32[]{:S(2)}) collective-permute-start(f32[128,256]{1,0:T(8,128)S(1)} %get-tuple-element.63), channel_id=1, source_target_pairs={{0,1},{1,2},{2,3},{3,4},{4,5},{5,6},{6,7},{7,0},{32,39},{33,32},{3... | collective-permute-start | bytes 393224 | tf_op jit(solution)/shard_map/scatter_rows/ppermute | solution.py:33
  141.6 15.7 %collective-permute-start.26 = (f32[2,128,256]{2,1,0:T(8,128)S(1)}, f32[2,128,256]{2,1,0:T(8,128)S(1)}, u32[]{:S(2)}, u32[]{:S(2)}) collective-permute-start(f32[2,128,256]{2,1,0:T(8,128)S(1)} %pad_maximum_fusion), channel_id=1, source_target_pairs={{0,2},{1,3},{2,4},{3,5},{4,6},{5,7},{6,0},{7,1},{32,38},{33,39},{3... | collective-permute-start | bytes 786440 | tf_op jit(solution)/shard_map/scatter_rows/ppermute | solution.py:33
  143.5 15.2 %collective-permute-start.27 = (f32[2,128,256]{2,1,0:T(8,128)S(1)}, f32[2,128,256]{2,1,0:T(8,128)S(1)}, u32[]{:S(2)}, u32[]{:S(2)}) collective-permute-start(f32[2,128,256]{2,1,0:T(8,128)S(1)} %slice.74), channel_id=1, source_target_pairs={{0,6},{1,7},{2,0},{3,1},{4,2},{5,3},{6,4},{7,5},{32,34},{33,35},{3... | collective-permute-start | bytes 786440 | tf_op jit(solution)/shard_map/scatter_rows/ppermute | solution.py:33
  158.8 5.1 %collective-permute-start.28 = (f32[128,256]{1,0:T(8,128)S(1)}, f32[128,256]{1,0:T(8,128)S(1)}, u32[]{:S(2)}, u32[]{:S(2)}) collective-permute-start(f32[128,256]{1,0:T(8,128)S(1)} %get-tuple-element.52), channel_id=1, source_target_pairs={{0,1},{1,2},{2,3},{3,4},{4,5},{5,6},{6,7},{7,0},{32,39},{33,32},{3... | collective-permute-start | bytes 393224 | tf_op jit(solution)/shard_map/scatter_rows/ppermute | solution.py:33
  159.4 5.5 %collective-permute-start.29 = (f32[128,256]{1,0:T(8,128)S(1)}, f32[128,256]{1,0:T(8,128)S(1)}, u32[]{:S(2)}, u32[]{:S(2)}) collective-permute-start(f32[128,256]{1,0:T(8,128)S(1)} %get-tuple-element.53), channel_id=1, source_target_pairs={{0,7},{1,0},{2,1},{3,2},{4,3},{5,4},{6,5},{7,6},{32,33},{33,34},{3... | collective-permute-start | bytes 393224 | tf_op jit(solution)/shard_map/scatter_rows/ppermute | solution.py:33

commit v4 on v3

--- a/solution.py
+++ b/solution.py
@@ -20,7 +20,7 @@
 GROUP = 8
 HELD = 96
 LIMIT = 30
-FAR_ROW = 24
+PARTS = 2
 
 
 def shift(value, axis, step):
@@ -35,10 +35,6 @@
 
 def swap(value):
     return lax.ppermute(value, "core", [(0, 1), (1, 0)])
-
-
-def join_rows(top, bottom):
-    return jnp.concatenate([top, bottom], axis=0)
 
 
 def ring_gather(block, axis):
@@ -110,40 +106,39 @@
     )(*([before] if late else []), *arrays)
 
 
-def plan_kernel(fill, kind, *refs):
-    plan, counts = refs[:3], refs[3]
+def plan_kernel(fill, side, *refs):
+    plan, counts = refs[:PARTS], refs[PARTS]
 
     def list_bucket(b, ends):
         def put(j, ends):
             slot = b * PER_BUCKET + j
-            which = kind[slot]
-            for k in range(3):
+            which = side[slot]
+            for k in range(PARTS):
                 plan[k][ends[k]] = slot
             return tuple(e + (which == k).astype(jnp.int32) for k, e in enumerate(ends))
 
         return lax.fori_loop(0, fill[b], put, ends)
 
-    ends = lax.fori_loop(0, BUCKETS, list_bucket, (0, 0, 0))
-    for k in range(3):
+    ends = lax.fori_loop(0, BUCKETS, list_bucket, (0,) * PARTS)
+    for k in range(PARTS):
         counts[k] = ends[k]
 
 
-def slot_plan(fill, kind):
+def slot_plan(fill, side):
     smem = pl.BlockSpec(memory_space=pltpu.SMEM)
     return pl.pallas_call(
         plan_kernel,
-        out_shape=[jax.ShapeDtypeStruct((SLOTS,), jnp.int32)] * 3
-        + [jax.ShapeDtypeStruct((3,), jnp.int32)],
+        out_shape=[jax.ShapeDtypeStruct((SLOTS,), jnp.int32)] * PARTS
+        + [jax.ShapeDtypeStruct((PARTS,), jnp.int32)],
         in_specs=[smem, smem],
-        out_specs=[smem] * 4,
+        out_specs=[smem] * (PARTS + 1),
         compiler_params=pltpu.CompilerParams(vmem_limit_bytes=1024 * 1024),
         cost_estimate=pl.CostEstimate(flops=0, bytes_accessed=12 * 1024 * 1024, transcendentals=0),
         name="slot_plan",
-    )(fill, kind)
+    )(fill, side)
 
 
 def products_kernel(part, counts, listed, blk, row, tiles, panels, *refs):
-    first_row = FAR_ROW if part == 1 else 0
     if part == 0:
         total, held, tile_sem = refs
     else:
@@ -161,7 +156,7 @@
             tile_copy(i).start()
 
     fetch(0)
-    total[...] = before[first_row : first_row + total.shape[0]] if part else jnp.zeros_like(total)
+    total[...] = before[...] if part else jnp.zeros_like(total)
 
     def product(i):
         slot = listed[i]
@@ -188,12 +183,12 @@
                 tile_copy(i).wait()
             sums = [product(i) for i in slots]
             for i, value in zip(slots, sums):
-                total[row[listed[i]] - first_row] += value
+                total[row[listed[i]]] += value
 
         @pl.loop(first + groups * GROUP, last)
         def _(i):
             tile_copy(i).wait()
-            total[row[listed[i]] - first_row] += product(i)
+            total[row[listed[i]]] += product(i)
 
         fetch(load + 1)
 
@@ -215,11 +210,9 @@
     if part == 0:
         shapes = [block(BLOCKS)]
     else:
-        shapes = [block(8)] if part == 1 else [block(8)] * 3
-        rows = BLOCKS - FAR_ROW if part == 1 else FAR_ROW
-        scratch = [pltpu.VMEM((rows, EDGE, WIDTH), jnp.float32)] + scratch
+        shapes = [block(8)] * 4
+        scratch = [pltpu.VMEM((BLOCKS, EDGE, WIDTH), jnp.float32)] + scratch
         arrays.append(before)
-    share = (4, 1, 3)[part]
     return pl.pallas_call(
         functools.partial(products_kernel, part),
         out_shape=shapes,
@@ -228,8 +221,8 @@
         scratch_shapes=scratch,
         compiler_params=pltpu.CompilerParams(vmem_limit_bytes=LIMIT * 1024 * 1024),
         cost_estimate=pl.CostEstimate(
-            flops=share * SLOTS * EDGE * EDGE * WIDTH,
-            bytes_accessed=share * 3 * 1024 * 1024,
+            flops=4 * SLOTS * EDGE * EDGE * WIDTH,
+            bytes_accessed=12 * 1024 * 1024,
             transcendentals=0,
         ),
         name="slot_products",
@@ -366,7 +359,6 @@
     ahead = ((target // 8 - here_x) * here_facing) % 4
     chunk = jnp.where(ahead == 3, 1, jnp.where(ahead == 0, 0, ahead + 1))
     row = chunk * 8 + ((target % 8 - here_z) * here_facing) % 8
-    kind = jnp.where(side == 0, 0, jnp.where(row >= FAR_ROW, 1, 2))
 
     with jax.named_scope("gather"):
         mine = lax.dynamic_slice_in_dim(sketch, here_core * 2 * EDGE, 2 * EDGE, 0)
@@ -374,7 +366,7 @@
         line = join(ring_gather(mine[EDGE:], "z"))
         first = ring_gather(slab, "z")
         second = ring_gather(line, "x")
-        slab, *plan, counts = lax.optimization_barrier((slab, *slot_plan(bucket_fill[0, 0], kind)))
+        slab, *plan, counts = lax.optimization_barrier((slab, *slot_plan(bucket_fill[0, 0], side)))
         first[0] = slab
         early, final = [], []
         base = 0
@@ -388,15 +380,12 @@
     stack = tiles[0, 0]
     tables = [(counts, listed, blk, row) for listed in plan]
     (sums,) = slot_products(0, tables[0], stack, panels)
-    (far,) = slot_products(1, tables[1], stack, panels_other, sums)
-    own, behind, ahead = slot_products(2, tables[2], stack, panels_other, sums)
+    own, behind, ahead, far = slot_products(1, tables[1], stack, panels_other, sums)
 
     with jax.named_scope("scatter_rows"):
         passing = shift(far, "x", 1)
         from_ahead = shift(behind, "x", -1)
-        low, high = ahead[:4] + passing[:4], ahead[4:] + passing[4:]
-        low, high = lax.optimization_barrier((low, high))
-        own = own + from_ahead + join_rows(shift(low, "x", 1), shift(high, "x", 1))
+        own = own + from_ahead + shift(ahead + passing, "x", 1)
         passing = shift(own[4], "z", 1)
         ahead = jnp.stack([own[2], own[3] + passing])
         ahead, behind = lax.optimization_barrier((ahead, own[5:7]))

time: 222 us -> 239 us (1.077)
  Pallas kernels: 30.6 us -> 38 us
  local copies, waits for them, and re-layouts: 5.75 us -> 13.1 us
  blocking collectives: 45.4 us -> 50.9 us
    unnamed x10 -> x30, local copies, waits for them, and re-layouts: 4.7 us -> 12 us
    ppermute x1, waiting for transfers between devices: 8.7 us -> 1.8 us  [swap(): return lax.ppermute(value, 'core', [(0, 1), (1, 0)])]
    ppermute x29 -> x28, waiting for transfers between devices: 77.1 us -> 82.8 us  [shift(): return lax.ppermute(value, ('core', axis), pairs)]
    all_to_all x3, blocking collectives: 45.4 us -> 50.9 us  [exchange(): return lax.all_to_all(value, axes, 0, 0, tiled=True)]
    pallas_call x3 -> x2, Pallas kernels: 15.6 us -> 20.1 us  [slot_products(): pl.pallas_call(functools.partial(products_kernel, part), out_shape=shapes...]
    pallas_call x2, Pallas kernels: 2.55 us -> 5.48 us  [place(): pl.pallas_call(functools.partial(place_kernel, offsets, int(late)), out_s...]
    ppermute x29 -> x28, starting transfers between devices: 44.8 us -> 44.6 us  [shift(): return lax.ppermute(value, ('core', axis), pairs)]
  transfers between devices with their start and end apart: 30 -> 29, of which waited for: 22 -> 19; matrix products, arithmetic and copies ran while one was open for 1% -> 0% of each run, Pallas kernels for 7% -> 8%
where the time goes in v4:
time: 239 us; the launch traced here: 238 us
  waiting for transfers between devices  84.6 us (35%)
  blocking collectives  50.9 us (21%)
  starting transfers between devices  49.1 us (21%)
  Pallas kernels  38 us (16%)
  local copies, waits for them, and re-layouts  13.1 us (5%)
    ppermute x28, waiting for transfers between devices, shift(): return lax.ppermute(value, ('core', axis), pairs)  82.8 us
    all_to_all x3, blocking collectives, exchange(): return lax.all_to_all(value, axes, 0, 0, tiled=True)  50.9 us
    ppermute x28, starting transfers between devices, shift(): return lax.ppermute(value, ('core', axis), pairs)  44.6 us
    pallas_call x2, Pallas kernels, slot_products(): pl.pallas_call(functools.partial(products_kernel, part), out_shape=shapes...  20.1 us
    unnamed x30, local copies, waits for them, and re-layouts  12 us
    pallas_call x1, Pallas kernels, factor_and_solve(): pl.pallas_call(factor_kernel, out_shape=[jax.ShapeDtypeStruct((EDGE, WIDT...  9.79 us
    pallas_call x2, Pallas kernels, place(): pl.pallas_call(functools.partial(place_kernel, offsets, int(late)), out_s...  5.48 us
  transfers between devices with their start and end apart: 29, of which 19 were waited for; matrix products, arithmetic and copies ran while one was open for 0% of the time, Pallas kernels for 8%

profile of v4, /device:TPU:1, one launch (start us, length us, event | category | flops | bytes accessed | tf_op | source)
XLA Modules:
  0.0 238.4 jit_solution(15814006843791918452)
XLA Ops:
  0.6 1.0 constant_dynamic-slice_fusion.1
  1.6 6.5 %collective-permute-start.11 = (f32[128,256]{1,0:T(8,128)S(1)}, f32[128,256]{1,0:T(8,128)S(1)}, u32[]{:S(2)}, u32[]{:S(2)}) collective-permute-start(f32[128,256]{1,0:T(8,128)S(1)} %get-tuple-element.54.refs_0_), channel_id=1, source_target_pairs={{0,1},{1,2},{2,3},{3,4},{4,5},{5,6},{6,7},{7,0},{32,39},{33,32},{3... | collective-permute-start | bytes 393224 | tf_op jit(solution)/shard_map/gather/ppermute | solution.py:33
  8.1 1.9 collective-permute-done.11.refs_7_
  10.1 3.5 %collective-permute-start.12 = (f32[128,256]{1,0:T(8,128)S(1)}, f32[128,256]{1,0:T(8,128)S(1)}, u32[]{:S(2)}, u32[]{:S(2)}) collective-permute-start(f32[128,256]{1,0:T(8,128)S(1)} %collective-permute-done.11.refs_7_), channel_id=1, source_target_pairs={{0,1},{1,2},{2,3},{3,4},{4,5},{5,6},{6,7},{7,0},{32,39},{33,32},{3... | collective-permute-start | bytes 393224 | tf_op jit(solution)/shard_map/gather/ppermute | solution.py:33
  13.6 2.5 %collective-permute-start = (f32[128,256]{1,0:T(8,128)S(1)}, f32[128,256]{1,0:T(8,128)S(1)}, u32[]{:S(2)}, u32[]{:S(2)}) collective-permute-start(f32[128,256]{1,0:T(8,128)S(1)} %get-tuple-element.55.refs_0_), channel_id=1, source_target_pairs={{0,8},{8,16},{16,24},{24,0},{32,56},{40,32},{48,40},{56,48},{1,9},... | collective-permute-start | bytes 393224 | tf_op jit(solution)/shard_map/gather/ppermute | solution.py:33
  16.1 2.7 %collective-permute-start.13 = (f32[128,256]{1,0:T(8,128)S(1)}, f32[128,256]{1,0:T(8,128)S(1)}, u32[]{:S(2)}, u32[]{:S(2)}) collective-permute-start(f32[128,256]{1,0:T(8,128)S(1)} %collective-permute-done.12.refs_6_), channel_id=1, source_target_pairs={{0,1},{1,2},{2,3},{3,4},{4,5},{5,6},{6,7},{7,0},{32,39},{33,32},{3... | collective-permute-start | bytes 393224 | tf_op jit(solution)/shard_map/gather/ppermute | solution.py:33
  18.8 0.2 collective-permute-done.10.refs_2_
  18.9 3.7 %collective-permute-done.1.refs_1_ = f32[128,256]{1,0:T(8,128)S(1)} collective-permute-done((f32[128,256]{1,0:T(8,128)S(1)}, f32[128,256]{1,0:T(8,128)S(1)}, u32[]{:S(2)}, u32[]{:S(2)}) %collective-permute-start.1) | collective-permute-done | bytes 131104 | tf_op jit(solution)/shard_map/gather/ppermute | solution.py:33
  22.6 2.7 %collective-permute-done.14.refs_3_ = f32[128,256]{1,0:T(8,128)S(1)} collective-permute-done((f32[128,256]{1,0:T(8,128)S(1)}, f32[128,256]{1,0:T(8,128)S(1)}, u32[]{:S(2)}, u32[]{:S(2)}) %collective-permute-start.14) | collective-permute-done | bytes 131104 | tf_op jit(solution)/shard_map/gather/ppermute | solution.py:33
  25.3 1.1 collective-permute-done.2.refs_2_
  26.5 1.5 collective-permute-start.5
  28.0 1.1 collective-permute-done.15.refs_4_
  29.2 2.9 %collective-permute-start.16 = (f32[1024,256]{1,0:T(8,128)S(1)}, f32[1024,256]{1,0:T(8,128)}, u32[]{:S(2)}, u32[]{:S(2)}) collective-permute-start(f32[1024,256]{1,0:T(8,128)S(1)} %join.3.refs_7_), channel_id=1, source_target_pairs={{0,8},{8,16},{16,24},{24,0},{32,56},{40,32},{48,40},{56,48},{1,9},... | collective-permute-start | bytes 3145736 | tf_op jit(solution)/shard_map/gather/ppermute | solution.py:33
  32.1 3.7 %collective-permute-done.5.refs_6_ = f32[512,256]{1,0:T(8,128)S(1)} collective-permute-done((f32[512,256]{1,0:T(8,128)S(1)}, f32[512,256]{1,0:T(8,128)S(1)}, u32[]{:S(2)}, u32[]{:S(2)}) %collective-permute-start.5) | collective-permute-done | bytes 524320 | tf_op jit(solution)/shard_map/gather/ppermute | solution.py:33
  35.8 2.6 %collective-permute-start.6 = (f32[512,256]{1,0:T(8,128)S(1)}, f32[512,256]{1,0:T(8,128)S(1)}, u32[]{:S(2)}, u32[]{:S(2)}) collective-permute-start(f32[512,256]{1,0:T(8,128)S(1)} %collective-permute-done.5.refs_6_), channel_id=1, source_target_pairs={{0,1},{1,2},{2,3},{3,4},{4,5},{5,6},{6,7},{7,0},{32,39},{33,32},{3... | collective-permute-start | bytes 1572872 | tf_op jit(solution)/shard_map/gather/ppermute | solution.py:33
  38.4 0.8 copy-done.2
  39.2 2.3 collective-permute-done.3.refs_1_
  41.4 0.8 copy-done.4
  42.2 4.2 %collective-permute-done.6.refs_5_ = f32[512,256]{1,0:T(8,128)S(1)} collective-permute-done((f32[512,256]{1,0:T(8,128)S(1)}, f32[512,256]{1,0:T(8,128)S(1)}, u32[]{:S(2)}, u32[]{:S(2)}) %collective-permute-start.6) | collective-permute-done | bytes 524320 | tf_op jit(solution)/shard_map/gather/ppermute | solution.py:33
  46.4 2.5 %collective-permute-start.7 = (f32[512,256]{1,0:T(8,128)S(1)}, f32[512,256]{1,0:T(8,128)}, u32[]{:S(2)}, u32[]{:S(2)}) collective-permute-start(f32[512,256]{1,0:T(8,128)S(1)} %collective-permute-done.6.refs_5_), channel_id=1, source_target_pairs={{0,1},{1,2},{2,3},{3,4},{4,5},{5,6},{6,7},{7,0},{32,39},{33,32},{3... | collective-permute-start | bytes 1572872 | tf_op jit(solution)/shard_map/gather/ppermute | solution.py:33
  48.9 0.8 copy-done.6
  49.7 4.4 %collective-permute-done.4.refs_2_ = f32[512,256]{1,0:T(8,128)S(1)} collective-permute-done((f32[512,256]{1,0:T(8,128)S(1)}, f32[512,256]{1,0:T(8,128)S(1)}, u32[]{:S(2)}, u32[]{:S(2)}) %collective-permute-start.4) | collective-permute-done | bytes 524320 | tf_op jit(solution)/shard_map/gather/ppermute | solution.py:33
  54.1 0.8 copy-done.8
  54.9 2.7 %collective-permute-done.17.refs_8_ = f32[1024,256]{1,0:T(8,128)S(1)} collective-permute-done((f32[1024,256]{1,0:T(8,128)S(1)}, f32[1024,256]{1,0:T(8,128)S(1)}, u32[]{:S(2)}, u32[]{:S(2)}) %collective-permute-start.17) | collective-permute-done | bytes 1048608 | tf_op jit(solution)/shard_map/gather/ppermute | solution.py:33
  57.5 1.0 copy-done
  58.5 1.9 collective-permute-start.19
  60.4 5.5 %collective-permute-done.8.refs_3_ = f32[512,256]{1,0:T(8,128)S(1)} collective-permute-done((f32[512,256]{1,0:T(8,128)S(1)}, f32[512,256]{1,0:T(8,128)S(1)}, u32[]{:S(2)}, u32[]{:S(2)}) %collective-permute-start.8) | collective-permute-done | bytes 524320 | tf_op jit(solution)/shard_map/gather/ppermute | solution.py:33
  65.9 0.8 copy-done.10
  66.6 0.2 collective-permute-start.18
  66.8 0.7 compare_select_fusion.12
  67.6 0.6 copy-done.12
  68.2 2.5 %slot_plan.1 = (s32[192]{0:T(256)S(1)}, s32[192]{0:T(256)S(1)}, s32[2]{0:T(128)S(1)}) custom-call(s32[32]{0:T(128)S(1)} %bitcast.31, s32[192]{0:T(256)S(1)} %and_select_fusion.10.side), custom_call_target="tpu_custom_call" | custom-call | bytes 12582912 | tf_op jit(solution)/shard_map/gather/slot_plan/pallas_call | solution.py:129
  70.8 1.2 copy-done.1
  72.0 1.0 copy-done.3
  73.0 1.0 copy-done.5
  74.1 1.0 copy-done.7
  75.1 1.0 copy-done.9
  76.2 1.0 copy-done.11
  77.2 4.3 %place.2.refs_0_ = f32[8192,256]{1,0:T(8,128)} custom-call(f32[512,256]{1,0:T(8,128)S(1)} %join.2.refs_0_, f32[512,256]{1,0:T(8,128)S(1)} %copy-done.5, f32[512,256]{1,0:T(8,128)S(1)} %copy-done.9, f32[512,256]{1,0:T(8,128)S(1)} %copy-done.11, f32[512,256]{1,0:T(8,128)} %collective-permute-done.7.refs_4_, f32[512,256]{1,0:T(8,128)S(1)} %copy-done.7, ...), custom_call_target="tpu_custom_call" | custom-call | bytes 13631488 | tf_op jit(solution)/shard_map/gather/place/pallas_call | solution.py:96
  81.6 1.1 place.3.panels
  82.7 4.5 %collective-permute-start.20 = (f32[8192,256]{1,0:T(8,128)}, f32[8192,256]{1,0:T(8,128)}, u32[]{:S(2)}, u32[]{:S(2)}) collective-permute-start(f32[8192,256]{1,0:T(8,128)} %place.3.panels), channel_id=1, source_target_pairs={{0,32},{32,0},{1,33},{33,1},{2,34},{34,2},{3,35},{35,3},{4,36},{36... | collective-permute-start | bytes 25165832 | tf_op jit(solution)/shard_map/gather/ppermute | solution.py:37
  87.3 0.1 select_reduce_fusion
  87.4 11.2 %slot_products.2.refs_0_ = f32[32,128,256]{2,1,0:T(8,128)S(1)} custom-call(s32[2]{0:T(128)S(1)} %get-tuple-element.30.counts, s32[192]{0:T(256)S(1)} %get-tuple-element.39.listed, s32[192]{0:T(256)S(1)} %get-tuple-element.48.blk, s32[192]{0:T(256)S(1)} %fusion.7.row, f32[192,128,128]{2,1,0:T(8,128)} %bitcast.32, f32[8192,256]{1,0:T(8,128)} %place.3.panels), custom_call_target="tpu_custom_call" | custom-call | flops 3221225472 | bytes 12582912 | tf_op jit(solution)/shard_map/slot_products/pallas_call | solution.py:216
  98.6 1.8 collective-permute-done.20.panels
  100.4 8.9 %slot_products.3 = (f32[8,128,256]{2,1,0:T(8,128)S(1)}, f32[8,128,256]{2,1,0:T(8,128)S(1)}, f32[8,128,256]{2,1,0:T(8,128)S(1)}, f32[8,128,256]{2,1,0:T(8,128)S(1)}) custom-call(s32[2]{0:T(128)S(1)} %get-tuple-element.30.counts, s32[192]{0:T(256)S(1)} %get-tuple-element.31.listed, s32[192]{0:T(256)S(1)} %get-tuple-element.48.blk, s32[192]{0:T(256)S(1)} %fusion.7.row, ...), custom_call_target="tpu_custom_call" | custom-call | flops 3221225472 | bytes 12582912 | tf_op jit(solution)/shard_map/slot_products/pallas_call | solution.py:216
  109.3 4.4 %collective-permute-start.22 = (f32[8,128,256]{2,1,0:T(8,128)S(1)}, f32[8,128,256]{2,1,0:T(8,128)S(1)}, u32[]{:S(2)}, u32[]{:S(2)}) collective-permute-start(f32[8,128,256]{2,1,0:T(8,128)S(1)} %get-tuple-element.43), channel_id=1, source_target_pairs={{0,8},{8,16},{16,24},{24,0},{32,56},{40,32},{48,40},{56,48},{1,9},... | collective-permute-start | bytes 3145736 | tf_op jit(solution)/shard_map/scatter_rows/ppermute | solution.py:33
  113.7 21.2 %collective-permute-done.22 = f32[8,128,256]{2,1,0:T(8,128)S(1)} collective-permute-done((f32[8,128,256]{2,1,0:T(8,128)S(1)}, f32[8,128,256]{2,1,0:T(8,128)S(1)}, u32[]{:S(2)}, u32[]{:S(2)}) %collective-permute-start.22) | collective-permute-done | bytes 1048608 | tf_op jit(solution)/shard_map/scatter_rows/ppermute | solution.py:33
  134.9 0.1 add.123
  135.0 3.5 %collective-permute-start.23 = (f32[8,128,256]{2,1,0:T(8,128)S(1)}, f32[8,128,256]{2,1,0:T(8,128)S(1)}, u32[]{:S(2)}, u32[]{:S(2)}) collective-permute-start(f32[8,128,256]{2,1,0:T(8,128)S(1)} %add.123), channel_id=1, source_target_pairs={{0,8},{8,16},{16,24},{24,0},{32,56},{40,32},{48,40},{56,48},{1,9},... | collective-permute-start | bytes 3145736 | tf_op jit(solution)/shard_map/scatter_rows/ppermute | solution.py:33
  138.6 11.7 %collective-permute-done.23 = f32[8,128,256]{2,1,0:T(8,128)S(1)} collective-permute-done((f32[8,128,256]{2,1,0:T(8,128)S(1)}, f32[8,128,256]{2,1,0:T(8,128)S(1)}, u32[]{:S(2)}, u32[]{:S(2)}) %collective-permute-start.23) | collective-permute-done | bytes 1048608 | tf_op jit(solution)/shard_map/scatter_rows/ppermute | solution.py:33
  150.3 0.2 add_add_fusion
  150.5 0.1 collective-permute-start.24
  150.6 4.7 %collective-permute-done.24 = f32[128,256]{1,0:T(8,128)S(1)} collective-permute-done((f32[128,256]{1,0:T(8,128)S(1)}, f32[128,256]{1,0:T(8,128)S(1)}, u32[]{:S(2)}, u32[]{:S(2)}) %collective-permute-start.24) | collective-permute-done | bytes 131104 | tf_op jit(solution)/shard_map/scatter_rows/ppermute | solution.py:33
  155.3 5.8 %collective-permute-start.26 = (f32[2,128,256]{2,1,0:T(8,128)S(1)}, f32[2,128,256]{2,1,0:T(8,128)S(1)}, u32[]{:S(2)}, u32[]{:S(2)}) collective-permute-start(f32[2,128,256]{2,1,0:T(8,128)S(1)} %slice.56), channel_id=1, source_target_pairs={{0,6},{1,7},{2,0},{3,1},{4,2},{5,3},{6,4},{7,5},{32,34},{33,35},{3... | collective-permute-start | bytes 786440 | tf_op jit(solution)/shard_map/scatter_rows/ppermute | solution.py:33
  161.1 6.5 %collective-permute-done.26 = f32[2,128,256]{2,1,0:T(8,128)S(1)} collective-permute-done((f32[2,128,256]{2,1,0:T(8,128)S(1)}, f32[2,128,256]{2,1,0:T(8,128)S(1)}, u32[]{:S(2)}, u32[]{:S(2)}) %collective-permute-start.26) | collective-permute-done | bytes 262176 | tf_op jit(solution)/shard_map/scatter_rows/ppermute | solution.py:33
  167.6 0.9 collective-permute-done.25
  168.6 2.7 %collective-permute-start.28 = (f32[128,256]{1,0:T(8,128)S(1)}, f32[128,256]{1,0:T(8,128)S(1)}, u32[]{:S(2)}, u32[]{:S(2)}) collective-permute-start(f32[128,256]{1,0:T(8,128)S(1)} %get-tuple-element.47), channel_id=1, source_target_pairs={{0,7},{1,0},{2,1},{3,2},{4,3},{5,4},{6,5},{7,6},{32,33},{33,34},{3... | collective-permute-start | bytes 393224 | tf_op jit(solution)/shard_map/scatter_rows/ppermute | solution.py:33
  171.3 1.4 collective-permute-start.27
  172.7 4.4 %collective-permute-done.28 = f32[128,256]{1,0:T(8,128)S(1)} collective-permute-done((f32[128,256]{1,0:T(8,128)S(1)}, f32[128,256]{1,0:T(8,128)S(1)}, u32[]{:S(2)}, u32[]{:S(2)}) %collective-permute-start.28) | collective-permute-done | bytes 131104 | tf_op jit(solution)/shard_map/scatter_rows/ppermute | solution.py:33
  177.1 0.4 convolution_bitcast_fusion
  177.6 26.2 %all_to_all.19 = f32[32,8,256]{2,1,0:T(8,128)S(1)} all-to-all(f32[32,8,256]{2,1,0:T(8,128)S(1)} %convolution_bitcast_fusion), channel_id=1, replica_groups=mesh['y'=4,'core'=2,'x'=4,'z'=8] {'y','core','x'}, dimensions={0} | all-to-all | bytes 524288 | tf_op jit(solution)/shard_map/gram/all_to_all | solution.py:338
  203.8 10.4 %all_to_all.20 = f32[8,8,256]{2,1,0:T(8,128)S(1)} all-to-all(f32[8,8,256]{2,1,0:T(8,128)S(1)} %broadcast_in_dim.33), channel_id=1, replica_groups=mesh['y'=4,'core'=2,'x'=4,'z'=8] {'z'}, dimensions={0} | all-to-all | bytes 131072 | tf_op jit(solution)/shard_map/gram/all_to_all | solution.py:338
  214.3 14.3 %all_to_all.21 = f32[32,8,256]{2,1,0:T(8,128)S(1)} all-to-all(f32[32,8,256]{2,1,0:T(8,128)S(1)} %broadcast_in_dim.34), channel_id=1, replica_groups=mesh['y'=4,'core'=2,'x'=4,'z'=8] {'y','core','x'}, dimensions={0} | all-to-all | bytes 524288 | tf_op jit(solution)/shard_map/gram/all_to_all | solution.py:338
  228.6 9.8 %factor_and_solve.1 = (f32[128,256]{1,0:T(8,128)}, f32[256,256]{1,0:T(8,128)}) custom-call(f32[256,256]{1,0:T(8,128)S(1)} %bitcast.30, f32[128,256]{1,0:T(8,128)S(1)} %fusion.4.rows), custom_call_target="tpu_custom_call" | custom-call | tf_op jit(solution)/shard_map/factor_and_solve/pallas_call | solution.py:323
  (53 shorter events, 0.5 us)
Async XLA Ops:
  1.6 8.4 %collective-permute-start.11 = (f32[128,256]{1,0:T(8,128)S(1)}, f32[128,256]{1,0:T(8,128)S(1)}, u32[]{:S(2)}, u32[]{:S(2)}) collective-permute-start(f32[128,256]{1,0:T(8,128)S(1)} %get-tuple-element.54.refs_0_), channel_id=1, source_target_pairs={{0,1},{1,2},{2,3},{3,4},{4,5},{5,6},{6,7},{7,0},{32,39},{33,32},{3... | collective-permute-start | bytes 393224 | tf_op jit(solution)/shard_map/gather/ppermute | solution.py:33
  8.1 5.5 %collective-permute-start.9 = (f32[128,256]{1,0:T(8,128)S(1)}, f32[128,256]{1,0:T(8,128)S(1)}, u32[]{:S(2)}, u32[]{:S(2)}) collective-permute-start(f32[128,256]{1,0:T(8,128)S(1)} %get-tuple-element.54.refs_0_), channel_id=1, source_target_pairs={{0,7},{1,0},{2,1},{3,2},{4,3},{5,4},{6,5},{7,6},{32,33},{33,34},{3... | collective-permute-start | bytes 393224 | tf_op jit(solution)/shard_map/gather/ppermute | solution.py:33
  10.1 6.0 %collective-permute-start.12 = (f32[128,256]{1,0:T(8,128)S(1)}, f32[128,256]{1,0:T(8,128)S(1)}, u32[]{:S(2)}, u32[]{:S(2)}) collective-permute-start(f32[128,256]{1,0:T(8,128)S(1)} %collective-permute-done.11.refs_7_), channel_id=1, source_target_pairs={{0,1},{1,2},{2,3},{3,4},{4,5},{5,6},{6,7},{7,0},{32,39},{33,32},{3... | collective-permute-start | bytes 393224 | tf_op jit(solution)/shard_map/gather/ppermute | solution.py:33
  13.6 5.3 %collective-permute-start.10 = (f32[128,256]{1,0:T(8,128)S(1)}, f32[128,256]{1,0:T(8,128)S(1)}, u32[]{:S(2)}, u32[]{:S(2)}) collective-permute-start(f32[128,256]{1,0:T(8,128)S(1)} %collective-permute-done.9.refs_1_), channel_id=1, source_target_pairs={{0,7},{1,0},{2,1},{3,2},{4,3},{5,4},{6,5},{7,6},{32,33},{33,34},{3... | collective-permute-start | bytes 393224 | tf_op jit(solution)/shard_map/gather/ppermute | solution.py:33
  13.6 5.3 %collective-permute-start = (f32[128,256]{1,0:T(8,128)S(1)}, f32[128,256]{1,0:T(8,128)S(1)}, u32[]{:S(2)}, u32[]{:S(2)}) collective-permute-start(f32[128,256]{1,0:T(8,128)S(1)} %get-tuple-element.55.refs_0_), channel_id=1, source_target_pairs={{0,8},{8,16},{16,24},{24,0},{32,56},{40,32},{48,40},{56,48},{1,9},... | collective-permute-start | bytes 393224 | tf_op jit(solution)/shard_map/gather/ppermute | solution.py:33
  16.1 6.5 %collective-permute-start.1 = (f32[128,256]{1,0:T(8,128)S(1)}, f32[128,256]{1,0:T(8,128)S(1)}, u32[]{:S(2)}, u32[]{:S(2)}) collective-permute-start(f32[128,256]{1,0:T(8,128)S(1)} %get-tuple-element.55.refs_0_), channel_id=1, source_target_pairs={{0,24},{8,0},{16,8},{24,16},{32,40},{40,48},{48,56},{56,32},{1,25}... | collective-permute-start | bytes 393224 | tf_op jit(solution)/shard_map/gather/ppermute | solution.py:33
  16.1 6.5 %collective-permute-start.13 = (f32[128,256]{1,0:T(8,128)S(1)}, f32[128,256]{1,0:T(8,128)S(1)}, u32[]{:S(2)}, u32[]{:S(2)}) collective-permute-start(f32[128,256]{1,0:T(8,128)S(1)} %collective-permute-done.12.refs_6_), channel_id=1, source_target_pairs={{0,1},{1,2},{2,3},{3,4},{4,5},{5,6},{6,7},{7,0},{32,39},{33,32},{3... | collective-permute-start | bytes 393224 | tf_op jit(solution)/shard_map/gather/ppermute | solution.py:33
  18.9 6.4 %collective-permute-start.14 = (f32[128,256]{1,0:T(8,128)S(1)}, f32[128,256]{1,0:T(8,128)S(1)}, u32[]{:S(2)}, u32[]{:S(2)}) collective-permute-start(f32[128,256]{1,0:T(8,128)S(1)} %collective-permute-done.10.refs_2_), channel_id=1, source_target_pairs={{0,7},{1,0},{2,1},{3,2},{4,3},{5,4},{6,5},{7,6},{32,33},{33,34},{3... | collective-permute-start | bytes 393224 | tf_op jit(solution)/shard_map/gather/ppermute | solution.py:33
  22.6 3.8 %collective-permute-start.2 = (f32[128,256]{1,0:T(8,128)S(1)}, f32[128,256]{1,0:T(8,128)S(1)}, u32[]{:S(2)}, u32[]{:S(2)}) collective-permute-start(f32[128,256]{1,0:T(8,128)S(1)} %collective-permute-done.refs_3_), channel_id=1, source_target_pairs={{0,8},{8,16},{16,24},{24,0},{32,56},{40,32},{48,40},{56,48},{1,9},... | collective-permute-start | bytes 393224 | tf_op jit(solution)/shard_map/gather/ppermute | solution.py:33
  25.3 3.8 %collective-permute-start.15 = (f32[128,256]{1,0:T(8,128)S(1)}, f32[128,256]{1,0:T(8,128)S(1)}, u32[]{:S(2)}, u32[]{:S(2)}) collective-permute-start(f32[128,256]{1,0:T(8,128)S(1)} %collective-permute-done.13.refs_5_), channel_id=1, source_target_pairs={{0,1},{1,2},{2,3},{3,4},{4,5},{5,6},{6,7},{7,0},{32,39},{33,32},{3... | collective-permute-start | bytes 393224 | tf_op jit(solution)/shard_map/gather/ppermute | solution.py:33
  26.5 9.3 %collective-permute-start.5 = (f32[512,256]{1,0:T(8,128)S(1)}, f32[512,256]{1,0:T(8,128)S(1)}, u32[]{:S(2)}, u32[]{:S(2)}) collective-permute-start(f32[512,256]{1,0:T(8,128)S(1)} %join.2.refs_0_), channel_id=1, source_target_pairs={{0,1},{1,2},{2,3},{3,4},{4,5},{5,6},{6,7},{7,0},{32,39},{33,32},{3... | collective-permute-start | bytes 1572872 | tf_op jit(solution)/shard_map/gather/ppermute | solution.py:33
  28.0 13.4 %collective-permute-start.3 = (f32[512,256]{1,0:T(8,128)S(1)}, f32[512,256]{1,0:T(8,128)S(1)}, u32[]{:S(2)}, u32[]{:S(2)}) collective-permute-start(f32[512,256]{1,0:T(8,128)S(1)} %join.2.refs_0_), channel_id=1, source_target_pairs={{0,7},{1,0},{2,1},{3,2},{4,3},{5,4},{6,5},{7,6},{32,33},{33,34},{3... | collective-permute-start | bytes 1572872 | tf_op jit(solution)/shard_map/gather/ppermute | solution.py:33
  29.2 25.6 %collective-permute-start.16 = (f32[1024,256]{1,0:T(8,128)S(1)}, f32[1024,256]{1,0:T(8,128)}, u32[]{:S(2)}, u32[]{:S(2)}) collective-permute-start(f32[1024,256]{1,0:T(8,128)S(1)} %join.3.refs_7_), channel_id=1, source_target_pairs={{0,8},{8,16},{16,24},{24,0},{32,56},{40,32},{48,40},{56,48},{1,9},... | collective-permute-start | bytes 3145736 | tf_op jit(solution)/shard_map/gather/ppermute | solution.py:33
  32.1 25.4 %collective-permute-start.17 = (f32[1024,256]{1,0:T(8,128)S(1)}, f32[1024,256]{1,0:T(8,128)S(1)}, u32[]{:S(2)}, u32[]{:S(2)}) collective-permute-start(f32[1024,256]{1,0:T(8,128)S(1)} %join.3.refs_7_), channel_id=1, source_target_pairs={{0,24},{8,0},{16,8},{24,16},{32,40},{40,48},{48,56},{56,32},{1,25}... | collective-permute-start | bytes 3145736 | tf_op jit(solution)/shard_map/gather/ppermute | solution.py:33
  35.8 10.6 %collective-permute-start.6 = (f32[512,256]{1,0:T(8,128)S(1)}, f32[512,256]{1,0:T(8,128)S(1)}, u32[]{:S(2)}, u32[]{:S(2)}) collective-permute-start(f32[512,256]{1,0:T(8,128)S(1)} %collective-permute-done.5.refs_6_), channel_id=1, source_target_pairs={{0,1},{1,2},{2,3},{3,4},{4,5},{5,6},{6,7},{7,0},{32,39},{33,32},{3... | collective-permute-start | bytes 1572872 | tf_op jit(solution)/shard_map/gather/ppermute | solution.py:33
  38.4 0.8 copy-start.2
  41.4 12.6 %collective-permute-start.4 = (f32[512,256]{1,0:T(8,128)S(1)}, f32[512,256]{1,0:T(8,128)S(1)}, u32[]{:S(2)}, u32[]{:S(2)}) collective-permute-start(f32[512,256]{1,0:T(8,128)S(1)} %collective-permute-done.3.refs_1_), channel_id=1, source_target_pairs={{0,7},{1,0},{2,1},{3,2},{4,3},{5,4},{6,5},{7,6},{32,33},{33,34},{3... | collective-permute-start | bytes 1572872 | tf_op jit(solution)/shard_map/gather/ppermute | solution.py:33
  41.4 0.8 copy-start.4
  46.4 14.0 %collective-permute-start.7 = (f32[512,256]{1,0:T(8,128)S(1)}, f32[512,256]{1,0:T(8,128)}, u32[]{:S(2)}, u32[]{:S(2)}) collective-permute-start(f32[512,256]{1,0:T(8,128)S(1)} %collective-permute-done.6.refs_5_), channel_id=1, source_target_pairs={{0,1},{1,2},{2,3},{3,4},{4,5},{5,6},{6,7},{7,0},{32,39},{33,32},{3... | collective-permute-start | bytes 1572872 | tf_op jit(solution)/shard_map/gather/ppermute | solution.py:33
  48.9 0.8 copy-start.6
  54.1 11.8 %collective-permute-start.8 = (f32[512,256]{1,0:T(8,128)S(1)}, f32[512,256]{1,0:T(8,128)S(1)}, u32[]{:S(2)}, u32[]{:S(2)}) collective-permute-start(f32[512,256]{1,0:T(8,128)S(1)} %collective-permute-done.4.refs_2_), channel_id=1, source_target_pairs={{0,7},{1,0},{2,1},{3,2},{4,3},{5,4},{6,5},{7,6},{32,33},{33,34},{3... | collective-permute-start | bytes 1572872 | tf_op jit(solution)/shard_map/gather/ppermute | solution.py:33
  54.1 0.8 copy-start.8
  57.5 1.0 copy-start
  58.5 23.1 %collective-permute-start.19 = (f32[1024,256]{1,0:T(8,128)}, f32[1024,256]{1,0:T(8,128)S(1)}, u32[]{:S(2)}, u32[]{:S(2)}) collective-permute-start(f32[1024,256]{1,0:T(8,128)} %collective-permute-done.16.refs_9_), channel_id=1, source_target_pairs={{0,8},{8,16},{16,24},{24,0},{32,56},{40,32},{48,40},{56,48},{1,9},... | collective-permute-start | bytes 3145736 | tf_op jit(solution)/shard_map/gather/ppermute | solution.py:33
  65.9 0.8 copy-start.10
  66.6 14.9 %collective-permute-start.18 = (f32[512,256]{1,0:T(8,128)}, f32[512,256]{1,0:T(8,128)S(1)}, u32[]{:S(2)}, u32[]{:S(2)}) collective-permute-start(f32[512,256]{1,0:T(8,128)} %collective-permute-done.7.refs_4_), channel_id=1, source_target_pairs={{0,1},{1,2},{2,3},{3,4},{4,5},{5,6},{6,7},{7,0},{32,39},{33,32},{3... | collective-permute-start | bytes 1572872 | tf_op jit(solution)/shard_map/gather/ppermute | solution.py:33
  67.6 0.7 copy-start.12
  70.8 1.2 copy-start.1
  72.0 1.0 copy-start.3
  73.0 1.0 copy-start.5
  74.1 1.0 copy-start.7
  75.1 1.0 copy-start.9
  76.2 1.0 copy-start.11
  81.5 5.7 %copy-start.13 = (s32[1,1,192]{2,1,0:T(1,128)S(1)}, s32[1,1,192]{2,1,0:T(1,128)}, u32[]{:S(2)}) copy-start(s32[1,1,192]{2,1,0:T(1,128)} %param.7) | copy-start | bytes 2308
  81.6 5.7 %copy-start.14 = (s32[1,32]{1,0:T(1,128)S(1)}, s32[1,32]{1,0:T(1,128)}, u32[]{:S(2)}) copy-start(s32[1,32]{1,0:T(1,128)} %param.10) | copy-start | bytes 388
  82.7 17.7 %collective-permute-start.20 = (f32[8192,256]{1,0:T(8,128)}, f32[8192,256]{1,0:T(8,128)}, u32[]{:S(2)}, u32[]{:S(2)}) collective-permute-start(f32[8192,256]{1,0:T(8,128)} %place.3.panels), channel_id=1, source_target_pairs={{0,32},{32,0},{1,33},{33,1},{2,34},{34,2},{3,35},{35,3},{4,36},{36... | collective-permute-start | bytes 25165832 | tf_op jit(solution)/shard_map/gather/ppermute | solution.py:37
  109.3 25.6 %collective-permute-start.22 = (f32[8,128,256]{2,1,0:T(8,128)S(1)}, f32[8,128,256]{2,1,0:T(8,128)S(1)}, u32[]{:S(2)}, u32[]{:S(2)}) collective-permute-start(f32[8,128,256]{2,1,0:T(8,128)S(1)} %get-tuple-element.43), channel_id=1, source_target_pairs={{0,8},{8,16},{16,24},{24,0},{32,56},{40,32},{48,40},{56,48},{1,9},... | collective-permute-start | bytes 3145736 | tf_op jit(solution)/shard_map/scatter_rows/ppermute | solution.py:33
  113.7 24.9 %collective-permute-start.21 = (f32[8,128,256]{2,1,0:T(8,128)S(1)}, f32[8,128,256]{2,1,0:T(8,128)S(1)}, u32[]{:S(2)}, u32[]{:S(2)}) collective-permute-start(f32[8,128,256]{2,1,0:T(8,128)S(1)} %get-tuple-element.41), channel_id=1, source_target_pairs={{0,24},{8,0},{16,8},{24,16},{32,40},{40,48},{48,56},{56,32},{1,25}... | collective-permute-start | bytes 3145736 | tf_op jit(solution)/shard_map/scatter_rows/ppermute | solution.py:33
  135.0 15.2 %collective-permute-start.23 = (f32[8,128,256]{2,1,0:T(8,128)S(1)}, f32[8,128,256]{2,1,0:T(8,128)S(1)}, u32[]{:S(2)}, u32[]{:S(2)}) collective-permute-start(f32[8,128,256]{2,1,0:T(8,128)S(1)} %add.123), channel_id=1, source_target_pairs={{0,8},{8,16},{16,24},{24,0},{32,56},{40,32},{48,40},{56,48},{1,9},... | collective-permute-start | bytes 3145736 | tf_op jit(solution)/shard_map/scatter_rows/ppermute | solution.py:33
  150.5 4.8 %collective-permute-start.24 = (f32[128,256]{1,0:T(8,128)S(1)}, f32[128,256]{1,0:T(8,128)S(1)}, u32[]{:S(2)}, u32[]{:S(2)}) collective-permute-start(f32[128,256]{1,0:T(8,128)S(1)} %get-tuple-element.53), channel_id=1, source_target_pairs={{0,1},{1,2},{2,3},{3,4},{4,5},{5,6},{6,7},{7,0},{32,39},{33,32},{3... | collective-permute-start | bytes 393224 | tf_op jit(solution)/shard_map/scatter_rows/ppermute | solution.py:33
  155.3 12.3 %collective-permute-start.26 = (f32[2,128,256]{2,1,0:T(8,128)S(1)}, f32[2,128,256]{2,1,0:T(8,128)S(1)}, u32[]{:S(2)}, u32[]{:S(2)}) collective-permute-start(f32[2,128,256]{2,1,0:T(8,128)S(1)} %slice.56), channel_id=1, source_target_pairs={{0,6},{1,7},{2,0},{3,1},{4,2},{5,3},{6,4},{7,5},{32,34},{33,35},{3... | collective-permute-start | bytes 786440 | tf_op jit(solution)/shard_map/scatter_rows/ppermute | solution.py:33
  161.1 7.4 %collective-permute-start.25 = (f32[2,128,256]{2,1,0:T(8,128)S(1)}, f32[2,128,256]{2,1,0:T(8,128)S(1)}, u32[]{:S(2)}, u32[]{:S(2)}) collective-permute-start(f32[2,128,256]{2,1,0:T(8,128)S(1)} %pad_maximum_fusion), channel_id=1, source_target_pairs={{0,2},{1,3},{2,4},{3,5},{4,6},{5,7},{6,0},{7,1},{32,38},{33,39},{3... | collective-permute-start | bytes 786440 | tf_op jit(solution)/shard_map/scatter_rows/ppermute | solution.py:33
  168.6 8.5 %collective-permute-start.28 = (f32[128,256]{1,0:T(8,128)S(1)}, f32[128,256]{1,0:T(8,128)S(1)}, u32[]{:S(2)}, u32[]{:S(2)}) collective-permute-start(f32[128,256]{1,0:T(8,128)S(1)} %get-tuple-element.47), channel_id=1, source_target_pairs={{0,7},{1,0},{2,1},{3,2},{4,3},{5,4},{6,5},{7,6},{32,33},{33,34},{3... | collective-permute-start | bytes 393224 | tf_op jit(solution)/shard_map/scatter_rows/ppermute | solution.py:33
  171.3 5.8 %collective-permute-start.27 = (f32[128,256]{1,0:T(8,128)S(1)}, f32[128,256]{1,0:T(8,128)S(1)}, u32[]{:S(2)}, u32[]{:S(2)}) collective-permute-start(f32[128,256]{1,0:T(8,128)S(1)} %get-tuple-element.46), channel_id=1, source_target_pairs={{0,1},{1,2},{2,3},{3,4},{4,5},{5,6},{6,7},{7,0},{32,39},{33,32},{3... | collective-permute-start | bytes 393224 | tf_op jit(solution)/shard_map/scatter_rows/ppermute | solution.py:33

commit v5 on v3

--- a/solution.py
+++ b/solution.py
@@ -35,10 +35,6 @@
 
 def swap(value):
     return lax.ppermute(value, "core", [(0, 1), (1, 0)])
-
-
-def join_rows(top, bottom):
-    return jnp.concatenate([top, bottom], axis=0)
 
 
 def ring_gather(block, axis):
@@ -394,9 +390,7 @@
     with jax.named_scope("scatter_rows"):
         passing = shift(far, "x", 1)
         from_ahead = shift(behind, "x", -1)
-        low, high = ahead[:4] + passing[:4], ahead[4:] + passing[4:]
-        low, high = lax.optimization_barrier((low, high))
-        own = own + from_ahead + join_rows(shift(low, "x", 1), shift(high, "x", 1))
+        own = own + from_ahead + shift(ahead + passing, "x", 1)
         passing = shift(own[4], "z", 1)
         ahead = jnp.stack([own[2], own[3] + passing])
         ahead, behind = lax.optimization_barrier((ahead, own[5:7]))

time: 222 us -> 221 us (level)
  Pallas kernels: 30.6 us -> 33.4 us
  waiting for transfers between devices: 85.8 us -> 83.1 us
    pallas_call x3, Pallas kernels: 15.6 us -> 18.2 us  [slot_products(): pl.pallas_call(functools.partial(products_kernel, part), out_shape=shapes...]
    ppermute x29 -> x28, waiting for transfers between devices: 77.1 us -> 76 us  [shift(): return lax.ppermute(value, ('core', axis), pairs)]
    ppermute x29 -> x28, starting transfers between devices: 44.8 us -> 43.9 us  [shift(): return lax.ppermute(value, ('core', axis), pairs)]
  transfers between devices with their start and end apart: 30 -> 29, of which waited for: 22 -> 20; matrix products, arithmetic and copies ran while one was open for 1% -> 1% of each run, Pallas kernels for 7% -> 8%
where the time goes in v5:
time: 221 us; the launch traced here: 220 us
  waiting for transfers between devices  83.1 us (38%)
  starting transfers between devices  48.6 us (22%)
  blocking collectives  45.8 us (21%)
  Pallas kernels  33.4 us (15%)
  local copies, waits for them, and re-layouts  5.75 us (3%)
    ppermute x28, waiting for transfers between devices, shift(): return lax.ppermute(value, ('core', axis), pairs)  76 us
    all_to_all x3, blocking collectives, exchange(): return lax.all_to_all(value, axes, 0, 0, tiled=True)  45.8 us
    ppermute x28, starting transfers between devices, shift(): return lax.ppermute(value, ('core', axis), pairs)  43.9 us
    pallas_call x3, Pallas kernels, slot_products(): pl.pallas_call(functools.partial(products_kernel, part), out_shape=shapes...  18.2 us
    pallas_call x1, Pallas kernels, factor_and_solve(): pl.pallas_call(factor_kernel, out_shape=[jax.ShapeDtypeStruct((EDGE, WIDT...  9.8 us
    ppermute x1, waiting for transfers between devices, swap(): return lax.ppermute(value, 'core', [(0, 1), (1, 0)])  7.09 us
    ppermute x1, starting transfers between devices, swap(): return lax.ppermute(value, 'core', [(0, 1), (1, 0)])  4.75 us
    unnamed x10, local copies, waits for them, and re-layouts  4.7 us
  transfers between devices with their start and end apart: 29, of which 20 were waited for; matrix products, arithmetic and copies ran while one was open for 1% of the time, Pallas kernels for 8%

profile of v5, /device:TPU:1, one launch (start us, length us, event | category | flops | bytes accessed | tf_op | source)
XLA Modules:
  0.0 220.1 jit_solution(14169446201101938614)
XLA Ops:
  0.6 1.0 constant_dynamic-slice_fusion.1
  1.6 6.5 %collective-permute-start.11 = (f32[128,256]{1,0:T(8,128)S(1)}, f32[128,256]{1,0:T(8,128)S(1)}, u32[]{:S(2)}, u32[]{:S(2)}) collective-permute-start(f32[128,256]{1,0:T(8,128)S(1)} %get-tuple-element.58.refs_0_), channel_id=1, source_target_pairs={{0,1},{1,2},{2,3},{3,4},{4,5},{5,6},{6,7},{7,0},{32,39},{33,32},{3... | collective-permute-start | bytes 393224 | tf_op jit(solution)/shard_map/gather/ppermute | solution.py:33
  8.1 1.9 collective-permute-done.11.refs_7_
  10.1 3.5 %collective-permute-start.12 = (f32[128,256]{1,0:T(8,128)S(1)}, f32[128,256]{1,0:T(8,128)S(1)}, u32[]{:S(2)}, u32[]{:S(2)}) collective-permute-start(f32[128,256]{1,0:T(8,128)S(1)} %collective-permute-done.11.refs_7_), channel_id=1, source_target_pairs={{0,1},{1,2},{2,3},{3,4},{4,5},{5,6},{6,7},{7,0},{32,39},{33,32},{3... | collective-permute-start | bytes 393224 | tf_op jit(solution)/shard_map/gather/ppermute | solution.py:33
  13.6 2.5 %collective-permute-start = (f32[128,256]{1,0:T(8,128)S(1)}, f32[128,256]{1,0:T(8,128)S(1)}, u32[]{:S(2)}, u32[]{:S(2)}) collective-permute-start(f32[128,256]{1,0:T(8,128)S(1)} %get-tuple-element.59.refs_0_), channel_id=1, source_target_pairs={{0,8},{8,16},{16,24},{24,0},{32,56},{40,32},{48,40},{56,48},{1,9},... | collective-permute-start | bytes 393224 | tf_op jit(solution)/shard_map/gather/ppermute | solution.py:33
  16.1 2.7 %collective-permute-start.13 = (f32[128,256]{1,0:T(8,128)S(1)}, f32[128,256]{1,0:T(8,128)S(1)}, u32[]{:S(2)}, u32[]{:S(2)}) collective-permute-start(f32[128,256]{1,0:T(8,128)S(1)} %collective-permute-done.12.refs_6_), channel_id=1, source_target_pairs={{0,1},{1,2},{2,3},{3,4},{4,5},{5,6},{6,7},{7,0},{32,39},{33,32},{3... | collective-permute-start | bytes 393224 | tf_op jit(solution)/shard_map/gather/ppermute | solution.py:33
  18.8 0.2 collective-permute-done.10.refs_2_
  18.9 3.7 %collective-permute-done.1.refs_1_ = f32[128,256]{1,0:T(8,128)S(1)} collective-permute-done((f32[128,256]{1,0:T(8,128)S(1)}, f32[128,256]{1,0:T(8,128)S(1)}, u32[]{:S(2)}, u32[]{:S(2)}) %collective-permute-start.1) | collective-permute-done | bytes 131104 | tf_op jit(solution)/shard_map/gather/ppermute | solution.py:33
  22.6 2.7 %collective-permute-done.14.refs_3_ = f32[128,256]{1,0:T(8,128)S(1)} collective-permute-done((f32[128,256]{1,0:T(8,128)S(1)}, f32[128,256]{1,0:T(8,128)S(1)}, u32[]{:S(2)}, u32[]{:S(2)}) %collective-permute-start.14) | collective-permute-done | bytes 131104 | tf_op jit(solution)/shard_map/gather/ppermute | solution.py:33
  25.3 1.1 collective-permute-done.2.refs_2_
  26.5 1.5 collective-permute-start.5
  28.0 0.0 collective-permute-start.3
  28.0 1.1 collective-permute-done.15.refs_4_
  29.1 0.1 join.3.refs_7_
  29.2 2.9 %collective-permute-start.16 = (f32[1024,256]{1,0:T(8,128)S(1)}, f32[1024,256]{1,0:T(8,128)}, u32[]{:S(2)}, u32[]{:S(2)}) collective-permute-start(f32[1024,256]{1,0:T(8,128)S(1)} %join.3.refs_7_), channel_id=1, source_target_pairs={{0,8},{8,16},{16,24},{24,0},{32,56},{40,32},{48,40},{56,48},{1,9},... | collective-permute-start | bytes 3145736 | tf_op jit(solution)/shard_map/gather/ppermute | solution.py:33
  32.1 3.7 %collective-permute-done.5.refs_6_ = f32[512,256]{1,0:T(8,128)S(1)} collective-permute-done((f32[512,256]{1,0:T(8,128)S(1)}, f32[512,256]{1,0:T(8,128)S(1)}, u32[]{:S(2)}, u32[]{:S(2)}) %collective-permute-start.5) | collective-permute-done | bytes 524320 | tf_op jit(solution)/shard_map/gather/ppermute | solution.py:33
  35.8 2.6 %collective-permute-start.6 = (f32[512,256]{1,0:T(8,128)S(1)}, f32[512,256]{1,0:T(8,128)}, u32[]{:S(2)}, u32[]{:S(2)}) collective-permute-start(f32[512,256]{1,0:T(8,128)S(1)} %collective-permute-done.5.refs_6_), channel_id=1, source_target_pairs={{0,1},{1,2},{2,3},{3,4},{4,5},{5,6},{6,7},{7,0},{32,39},{33,32},{3... | collective-permute-start | bytes 1572872 | tf_op jit(solution)/shard_map/gather/ppermute | solution.py:33
  38.4 3.1 %collective-permute-done.3.refs_1_ = f32[512,256]{1,0:T(8,128)S(1)} collective-permute-done((f32[512,256]{1,0:T(8,128)S(1)}, f32[512,256]{1,0:T(8,128)S(1)}, u32[]{:S(2)}, u32[]{:S(2)}) %collective-permute-start.3) | collective-permute-done | bytes 524320 | tf_op jit(solution)/shard_map/gather/ppermute | solution.py:33
  41.4 0.0 collective-permute-start.4
  41.4 0.8 copy-done.2
  42.3 4.1 %collective-permute-done.6.refs_5_ = f32[512,256]{1,0:T(8,128)} collective-permute-done((f32[512,256]{1,0:T(8,128)S(1)}, f32[512,256]{1,0:T(8,128)}, u32[]{:S(2)}, u32[]{:S(2)}) %collective-permute-start.6) | collective-permute-done | bytes 524320 | tf_op jit(solution)/shard_map/gather/ppermute | solution.py:33
  46.4 2.5 %collective-permute-start.7 = (f32[512,256]{1,0:T(8,128)}, f32[512,256]{1,0:T(8,128)}, u32[]{:S(2)}, u32[]{:S(2)}) collective-permute-start(f32[512,256]{1,0:T(8,128)} %collective-permute-done.6.refs_5_), channel_id=1, source_target_pairs={{0,1},{1,2},{2,3},{3,4},{4,5},{5,6},{6,7},{7,0},{32,39},{33,32},{3... | collective-permute-start | bytes 1572872 | tf_op jit(solution)/shard_map/gather/ppermute | solution.py:33
  48.9 5.2 %collective-permute-done.4.refs_2_ = f32[512,256]{1,0:T(8,128)} collective-permute-done((f32[512,256]{1,0:T(8,128)S(1)}, f32[512,256]{1,0:T(8,128)}, u32[]{:S(2)}, u32[]{:S(2)}) %collective-permute-start.4) | collective-permute-done | bytes 524320 | tf_op jit(solution)/shard_map/gather/ppermute | solution.py:33
  54.1 3.5 %collective-permute-done.17.refs_8_ = f32[1024,256]{1,0:T(8,128)S(1)} collective-permute-done((f32[1024,256]{1,0:T(8,128)S(1)}, f32[1024,256]{1,0:T(8,128)S(1)}, u32[]{:S(2)}, u32[]{:S(2)}) %collective-permute-start.17) | collective-permute-done | bytes 1048608 | tf_op jit(solution)/shard_map/gather/ppermute | solution.py:33
  57.5 1.0 copy-done
  58.5 1.2 collective-permute-start.19
  59.7 6.3 %collective-permute-done.8.refs_3_ = f32[512,256]{1,0:T(8,128)} collective-permute-done((f32[512,256]{1,0:T(8,128)}, f32[512,256]{1,0:T(8,128)}, u32[]{:S(2)}, u32[]{:S(2)}) %collective-permute-start.8) | collective-permute-done | bytes 524320 | tf_op jit(solution)/shard_map/gather/ppermute | solution.py:33
  66.0 0.2 collective-permute-start.18
  66.1 0.8 select_reduce_fusion
  66.9 0.7 compare_select_fusion.10
  67.7 0.0 copy-start.4
  67.7 0.6 copy-done.4
  68.3 2.8 %slot_plan.1 = (s32[192]{0:T(256)S(1)}, s32[192]{0:T(256)S(1)}, s32[192]{0:T(256)S(1)}, s32[3]{0:T(128)S(1)}) custom-call(s32[32]{0:T(128)S(1)} %bitcast.31, s32[192]{0:T(256)S(1)} %get-tuple-element.52.kind), custom_call_target="tpu_custom_call" | custom-call | bytes 12582912 | tf_op jit(solution)/shard_map/gather/slot_plan/pallas_call | solution.py:129
  71.2 1.2 copy-done.1
  72.4 1.0 copy-done.3
  73.4 2.4 %place.2.refs_0_ = f32[8192,256]{1,0:T(8,128)S(1)} custom-call(f32[512,256]{1,0:T(8,128)S(1)} %join.2.refs_0_, f32[512,256]{1,0:T(8,128)S(1)} %copy-done.3, f32[512,256]{1,0:T(8,128)} %collective-permute-done.4.refs_2_, f32[512,256]{1,0:T(8,128)} %collective-permute-done.8.refs_3_, f32[512,256]{1,0:T(8,128)} %collective-permute-done.7.refs_4_, ...), custom_call_target="tpu_custom_call" | custom-call | bytes 13631488 | tf_op jit(solution)/shard_map/gather/place/pallas_call | solution.py:96
  75.9 0.1 place.3.panels
  76.0 4.7 %collective-permute-start.20 = (f32[8192,256]{1,0:T(8,128)S(1)}, f32[8192,256]{1,0:T(8,128)S(1)}, u32[]{:S(2)}, u32[]{:S(2)}) collective-permute-start(f32[8192,256]{1,0:T(8,128)S(1)} %place.3.panels), channel_id=1, source_target_pairs={{0,32},{32,0},{1,33},{33,1},{2,34},{34,2},{3,35},{35,3},{4,36},{36... | collective-permute-start | bytes 25165832 | tf_op jit(solution)/shard_map/gather/ppermute | solution.py:37
  80.8 5.7 %slot_products.3.refs_0_ = f32[32,128,256]{2,1,0:T(8,128)S(1)} custom-call(s32[3]{0:T(128)S(1)} %get-tuple-element.32.counts, s32[192]{0:T(256)S(1)} %get-tuple-element.41.listed, s32[192]{0:T(256)S(1)} %get-tuple-element.50.blk, s32[192]{0:T(256)S(1)} %get-tuple-element.53.row, f32[192,128,128]{2,1,0:T(8,128)} %bitcast.32, f32[8192,256]{1,0:T(8,128)S(1)} %place.3.panels), custom_call_target="tpu_custom_call" | custom-call | flops 3221225472 | bytes 12582912 | tf_op jit(solution)/shard_map/slot_products/pallas_call | solution.py:219
  86.4 7.1 %collective-permute-done.20.panels = f32[8192,256]{1,0:T(8,128)S(1)} collective-permute-done((f32[8192,256]{1,0:T(8,128)S(1)}, f32[8192,256]{1,0:T(8,128)S(1)}, u32[]{:S(2)}, u32[]{:S(2)}) %collective-permute-start.20) | collective-permute-done | bytes 8388640 | tf_op jit(solution)/shard_map/gather/ppermute | solution.py:37
  93.5 5.5 %slot_products.5 = f32[8,128,256]{2,1,0:T(8,128)S(1)} custom-call(s32[3]{0:T(128)S(1)} %get-tuple-element.32.counts, s32[192]{0:T(256)S(1)} %get-tuple-element.45.listed, s32[192]{0:T(256)S(1)} %get-tuple-element.50.blk, s32[192]{0:T(256)S(1)} %get-tuple-element.53.row, f32[192,128,128]{2,1,0:T(8,128)} %bitcast.33, ...), custom_call_target="tpu_custom_call" | custom-call | flops 805306368 | bytes 3145728 | tf_op jit(solution)/shard_map/slot_products/pallas_call | solution.py:219
  99.1 3.1 %collective-permute-start.22 = (f32[8,128,256]{2,1,0:T(8,128)S(1)}, f32[8,128,256]{2,1,0:T(8,128)S(1)}, u32[]{:S(2)}, u32[]{:S(2)}) collective-permute-start(f32[8,128,256]{2,1,0:T(8,128)S(1)} %slot_products.5), channel_id=1, source_target_pairs={{0,8},{8,16},{16,24},{24,0},{32,56},{40,32},{48,40},{56,48},{1,9},... | collective-permute-start | bytes 3145736 | tf_op jit(solution)/shard_map/scatter_rows/ppermute | solution.py:33
  102.2 7.0 %slot_products.4 = (f32[8,128,256]{2,1,0:T(8,128)S(1)}, f32[8,128,256]{2,1,0:T(8,128)S(1)}, f32[8,128,256]{2,1,0:T(8,128)S(1)}) custom-call(s32[3]{0:T(128)S(1)} %get-tuple-element.32.counts, s32[192]{0:T(256)S(1)} %get-tuple-element.33.listed, s32[192]{0:T(256)S(1)} %get-tuple-element.50.blk, s32[192]{0:T(256)S(1)} %get-tuple-element.53.row, ...), custom_call_target="tpu_custom_call" | custom-call | flops 2415919104 | bytes 9437184 | tf_op jit(solution)/shard_map/slot_products/pallas_call | solution.py:219
  109.2 0.1 collective-permute-start.21
  109.2 10.0 %collective-permute-done.22 = f32[8,128,256]{2,1,0:T(8,128)S(1)} collective-permute-done((f32[8,128,256]{2,1,0:T(8,128)S(1)}, f32[8,128,256]{2,1,0:T(8,128)S(1)}, u32[]{:S(2)}, u32[]{:S(2)}) %collective-permute-start.22) | collective-permute-done | bytes 1048608 | tf_op jit(solution)/shard_map/scatter_rows/ppermute | solution.py:33
  119.2 0.1 add.123
  119.4 3.5 %collective-permute-start.23 = (f32[8,128,256]{2,1,0:T(8,128)S(1)}, f32[8,128,256]{2,1,0:T(8,128)S(1)}, u32[]{:S(2)}, u32[]{:S(2)}) collective-permute-start(f32[8,128,256]{2,1,0:T(8,128)S(1)} %add.123), channel_id=1, source_target_pairs={{0,8},{8,16},{16,24},{24,0},{32,56},{40,32},{48,40},{56,48},{1,9},... | collective-permute-start | bytes 3145736 | tf_op jit(solution)/shard_map/scatter_rows/ppermute | solution.py:33
  122.8 9.2 %collective-permute-done.21 = f32[8,128,256]{2,1,0:T(8,128)S(1)} collective-permute-done((f32[8,128,256]{2,1,0:T(8,128)S(1)}, f32[8,128,256]{2,1,0:T(8,128)S(1)}, u32[]{:S(2)}, u32[]{:S(2)}) %collective-permute-start.21) | collective-permute-done | bytes 1048608 | tf_op jit(solution)/shard_map/scatter_rows/ppermute | solution.py:33
  132.0 4.3 %collective-permute-done.23 = f32[8,128,256]{2,1,0:T(8,128)S(1)} collective-permute-done((f32[8,128,256]{2,1,0:T(8,128)S(1)}, f32[8,128,256]{2,1,0:T(8,128)S(1)}, u32[]{:S(2)}, u32[]{:S(2)}) %collective-permute-start.23) | collective-permute-done | bytes 1048608 | tf_op jit(solution)/shard_map/scatter_rows/ppermute | solution.py:33
  136.4 0.2 add_add_fusion
  136.6 2.9 %collective-permute-start.24 = (f32[128,256]{1,0:T(8,128)S(1)}, f32[128,256]{1,0:T(8,128)S(1)}, u32[]{:S(2)}, u32[]{:S(2)}) collective-permute-start(f32[128,256]{1,0:T(8,128)S(1)} %get-tuple-element.57), channel_id=1, source_target_pairs={{0,1},{1,2},{2,3},{3,4},{4,5},{5,6},{6,7},{7,0},{32,39},{33,32},{3... | collective-permute-start | bytes 393224 | tf_op jit(solution)/shard_map/scatter_rows/ppermute | solution.py:33
  139.5 1.9 collective-permute-done.24
  141.5 1.7 collective-permute-start.25
  143.1 4.4 %collective-permute-start.26 = (f32[2,128,256]{2,1,0:T(8,128)S(1)}, f32[2,128,256]{2,1,0:T(8,128)S(1)}, u32[]{:S(2)}, u32[]{:S(2)}) collective-permute-start(f32[2,128,256]{2,1,0:T(8,128)S(1)} %slice.56), channel_id=1, source_target_pairs={{0,6},{1,7},{2,0},{3,1},{4,2},{5,3},{6,4},{7,5},{32,34},{33,35},{3... | collective-permute-start | bytes 786440 | tf_op jit(solution)/shard_map/scatter_rows/ppermute | solution.py:33
  147.6 11.1 %collective-permute-done.25 = f32[2,128,256]{2,1,0:T(8,128)S(1)} collective-permute-done((f32[2,128,256]{2,1,0:T(8,128)S(1)}, f32[2,128,256]{2,1,0:T(8,128)S(1)}, u32[]{:S(2)}, u32[]{:S(2)}) %collective-permute-start.25) | collective-permute-done | bytes 262176 | tf_op jit(solution)/shard_map/scatter_rows/ppermute | solution.py:33
  158.7 0.1 collective-permute-start.27
  158.8 2.2 collective-permute-start.28
  161.0 2.3 %collective-permute-done.27 = f32[128,256]{1,0:T(8,128)S(1)} collective-permute-done((f32[128,256]{1,0:T(8,128)S(1)}, f32[128,256]{1,0:T(8,128)S(1)}, u32[]{:S(2)}, u32[]{:S(2)}) %collective-permute-start.27) | collective-permute-done | bytes 131104 | tf_op jit(solution)/shard_map/scatter_rows/ppermute | solution.py:33
  163.2 0.6 collective-permute-done.28
  163.9 0.4 convolution_bitcast_fusion
  164.3 18.9 %all_to_all.19 = f32[32,8,256]{2,1,0:T(8,128)S(1)} all-to-all(f32[32,8,256]{2,1,0:T(8,128)S(1)} %convolution_bitcast_fusion), channel_id=1, replica_groups=mesh['y'=4,'core'=2,'x'=4,'z'=8] {'y','core','x'}, dimensions={0} | all-to-all | bytes 524288 | tf_op jit(solution)/shard_map/gram/all_to_all | solution.py:341
  183.3 12.6 %all_to_all.20 = f32[8,8,256]{2,1,0:T(8,128)S(1)} all-to-all(f32[8,8,256]{2,1,0:T(8,128)S(1)} %broadcast_in_dim.39), channel_id=1, replica_groups=mesh['y'=4,'core'=2,'x'=4,'z'=8] {'z'}, dimensions={0} | all-to-all | bytes 131072 | tf_op jit(solution)/shard_map/gram/all_to_all | solution.py:341
  196.0 14.3 %all_to_all.21 = f32[32,8,256]{2,1,0:T(8,128)S(1)} all-to-all(f32[32,8,256]{2,1,0:T(8,128)S(1)} %broadcast_in_dim.40), channel_id=1, replica_groups=mesh['y'=4,'core'=2,'x'=4,'z'=8] {'y','core','x'}, dimensions={0} | all-to-all | bytes 524288 | tf_op jit(solution)/shard_map/gram/all_to_all | solution.py:341
  210.3 9.8 %factor_and_solve.1 = (f32[128,256]{1,0:T(8,128)}, f32[256,256]{1,0:T(8,128)}) custom-call(f32[256,256]{1,0:T(8,128)S(1)} %bitcast.30, f32[128,256]{1,0:T(8,128)S(1)} %fusion.4.rows), custom_call_target="tpu_custom_call" | custom-call | tf_op jit(solution)/shard_map/factor_and_solve/pallas_call | solution.py:326
  (33 shorter events, 0.3 us)
Async XLA Ops:
  1.6 8.4 %collective-permute-start.11 = (f32[128,256]{1,0:T(8,128)S(1)}, f32[128,256]{1,0:T(8,128)S(1)}, u32[]{:S(2)}, u32[]{:S(2)}) collective-permute-start(f32[128,256]{1,0:T(8,128)S(1)} %get-tuple-element.58.refs_0_), channel_id=1, source_target_pairs={{0,1},{1,2},{2,3},{3,4},{4,5},{5,6},{6,7},{7,0},{32,39},{33,32},{3... | collective-permute-start | bytes 393224 | tf_op jit(solution)/shard_map/gather/ppermute | solution.py:33
  8.1 5.5 %collective-permute-start.9 = (f32[128,256]{1,0:T(8,128)S(1)}, f32[128,256]{1,0:T(8,128)S(1)}, u32[]{:S(2)}, u32[]{:S(2)}) collective-permute-start(f32[128,256]{1,0:T(8,128)S(1)} %get-tuple-element.58.refs_0_), channel_id=1, source_target_pairs={{0,7},{1,0},{2,1},{3,2},{4,3},{5,4},{6,5},{7,6},{32,33},{33,34},{3... | collective-permute-start | bytes 393224 | tf_op jit(solution)/shard_map/gather/ppermute | solution.py:33
  10.1 6.0 %collective-permute-start.12 = (f32[128,256]{1,0:T(8,128)S(1)}, f32[128,256]{1,0:T(8,128)S(1)}, u32[]{:S(2)}, u32[]{:S(2)}) collective-permute-start(f32[128,256]{1,0:T(8,128)S(1)} %collective-permute-done.11.refs_7_), channel_id=1, source_target_pairs={{0,1},{1,2},{2,3},{3,4},{4,5},{5,6},{6,7},{7,0},{32,39},{33,32},{3... | collective-permute-start | bytes 393224 | tf_op jit(solution)/shard_map/gather/ppermute | solution.py:33
  13.6 5.3 %collective-permute-start.10 = (f32[128,256]{1,0:T(8,128)S(1)}, f32[128,256]{1,0:T(8,128)S(1)}, u32[]{:S(2)}, u32[]{:S(2)}) collective-permute-start(f32[128,256]{1,0:T(8,128)S(1)} %collective-permute-done.9.refs_1_), channel_id=1, source_target_pairs={{0,7},{1,0},{2,1},{3,2},{4,3},{5,4},{6,5},{7,6},{32,33},{33,34},{3... | collective-permute-start | bytes 393224 | tf_op jit(solution)/shard_map/gather/ppermute | solution.py:33
  13.6 5.3 %collective-permute-start = (f32[128,256]{1,0:T(8,128)S(1)}, f32[128,256]{1,0:T(8,128)S(1)}, u32[]{:S(2)}, u32[]{:S(2)}) collective-permute-start(f32[128,256]{1,0:T(8,128)S(1)} %get-tuple-element.59.refs_0_), channel_id=1, source_target_pairs={{0,8},{8,16},{16,24},{24,0},{32,56},{40,32},{48,40},{56,48},{1,9},... | collective-permute-start | bytes 393224 | tf_op jit(solution)/shard_map/gather/ppermute | solution.py:33
  16.1 6.5 %collective-permute-start.1 = (f32[128,256]{1,0:T(8,128)S(1)}, f32[128,256]{1,0:T(8,128)S(1)}, u32[]{:S(2)}, u32[]{:S(2)}) collective-permute-start(f32[128,256]{1,0:T(8,128)S(1)} %get-tuple-element.59.refs_0_), channel_id=1, source_target_pairs={{0,24},{8,0},{16,8},{24,16},{32,40},{40,48},{48,56},{56,32},{1,25}... | collective-permute-start | bytes 393224 | tf_op jit(solution)/shard_map/gather/ppermute | solution.py:33
  16.1 6.5 %collective-permute-start.13 = (f32[128,256]{1,0:T(8,128)S(1)}, f32[128,256]{1,0:T(8,128)S(1)}, u32[]{:S(2)}, u32[]{:S(2)}) collective-permute-start(f32[128,256]{1,0:T(8,128)S(1)} %collective-permute-done.12.refs_6_), channel_id=1, source_target_pairs={{0,1},{1,2},{2,3},{3,4},{4,5},{5,6},{6,7},{7,0},{32,39},{33,32},{3... | collective-permute-start | bytes 393224 | tf_op jit(solution)/shard_map/gather/ppermute | solution.py:33
  18.9 6.4 %collective-permute-start.14 = (f32[128,256]{1,0:T(8,128)S(1)}, f32[128,256]{1,0:T(8,128)S(1)}, u32[]{:S(2)}, u32[]{:S(2)}) collective-permute-start(f32[128,256]{1,0:T(8,128)S(1)} %collective-permute-done.10.refs_2_), channel_id=1, source_target_pairs={{0,7},{1,0},{2,1},{3,2},{4,3},{5,4},{6,5},{7,6},{32,33},{33,34},{3... | collective-permute-start | bytes 393224 | tf_op jit(solution)/shard_map/gather/ppermute | solution.py:33
  22.6 3.8 %collective-permute-start.2 = (f32[128,256]{1,0:T(8,128)S(1)}, f32[128,256]{1,0:T(8,128)S(1)}, u32[]{:S(2)}, u32[]{:S(2)}) collective-permute-start(f32[128,256]{1,0:T(8,128)S(1)} %collective-permute-done.refs_3_), channel_id=1, source_target_pairs={{0,8},{8,16},{16,24},{24,0},{32,56},{40,32},{48,40},{56,48},{1,9},... | collective-permute-start | bytes 393224 | tf_op jit(solution)/shard_map/gather/ppermute | solution.py:33
  25.3 3.8 %collective-permute-start.15 = (f32[128,256]{1,0:T(8,128)S(1)}, f32[128,256]{1,0:T(8,128)S(1)}, u32[]{:S(2)}, u32[]{:S(2)}) collective-permute-start(f32[128,256]{1,0:T(8,128)S(1)} %collective-permute-done.13.refs_5_), channel_id=1, source_target_pairs={{0,1},{1,2},{2,3},{3,4},{4,5},{5,6},{6,7},{7,0},{32,39},{33,32},{3... | collective-permute-start | bytes 393224 | tf_op jit(solution)/shard_map/gather/ppermute | solution.py:33
  26.5 9.3 %collective-permute-start.5 = (f32[512,256]{1,0:T(8,128)S(1)}, f32[512,256]{1,0:T(8,128)S(1)}, u32[]{:S(2)}, u32[]{:S(2)}) collective-permute-start(f32[512,256]{1,0:T(8,128)S(1)} %join.2.refs_0_), channel_id=1, source_target_pairs={{0,1},{1,2},{2,3},{3,4},{4,5},{5,6},{6,7},{7,0},{32,39},{33,32},{3... | collective-permute-start | bytes 1572872 | tf_op jit(solution)/shard_map/gather/ppermute | solution.py:33
  28.0 13.4 %collective-permute-start.3 = (f32[512,256]{1,0:T(8,128)S(1)}, f32[512,256]{1,0:T(8,128)S(1)}, u32[]{:S(2)}, u32[]{:S(2)}) collective-permute-start(f32[512,256]{1,0:T(8,128)S(1)} %join.2.refs_0_), channel_id=1, source_target_pairs={{0,7},{1,0},{2,1},{3,2},{4,3},{5,4},{6,5},{7,6},{32,33},{33,34},{3... | collective-permute-start | bytes 1572872 | tf_op jit(solution)/shard_map/gather/ppermute | solution.py:33
  29.2 24.8 %collective-permute-start.16 = (f32[1024,256]{1,0:T(8,128)S(1)}, f32[1024,256]{1,0:T(8,128)}, u32[]{:S(2)}, u32[]{:S(2)}) collective-permute-start(f32[1024,256]{1,0:T(8,128)S(1)} %join.3.refs_7_), channel_id=1, source_target_pairs={{0,8},{8,16},{16,24},{24,0},{32,56},{40,32},{48,40},{56,48},{1,9},... | collective-permute-start | bytes 3145736 | tf_op jit(solution)/shard_map/gather/ppermute | solution.py:33
  32.1 25.4 %collective-permute-start.17 = (f32[1024,256]{1,0:T(8,128)S(1)}, f32[1024,256]{1,0:T(8,128)S(1)}, u32[]{:S(2)}, u32[]{:S(2)}) collective-permute-start(f32[1024,256]{1,0:T(8,128)S(1)} %join.3.refs_7_), channel_id=1, source_target_pairs={{0,24},{8,0},{16,8},{24,16},{32,40},{40,48},{48,56},{56,32},{1,25}... | collective-permute-start | bytes 3145736 | tf_op jit(solution)/shard_map/gather/ppermute | solution.py:33
  35.8 10.6 %collective-permute-start.6 = (f32[512,256]{1,0:T(8,128)S(1)}, f32[512,256]{1,0:T(8,128)}, u32[]{:S(2)}, u32[]{:S(2)}) collective-permute-start(f32[512,256]{1,0:T(8,128)S(1)} %collective-permute-done.5.refs_6_), channel_id=1, source_target_pairs={{0,1},{1,2},{2,3},{3,4},{4,5},{5,6},{6,7},{7,0},{32,39},{33,32},{3... | collective-permute-start | bytes 1572872 | tf_op jit(solution)/shard_map/gather/ppermute | solution.py:33
  41.4 12.6 %collective-permute-start.4 = (f32[512,256]{1,0:T(8,128)S(1)}, f32[512,256]{1,0:T(8,128)}, u32[]{:S(2)}, u32[]{:S(2)}) collective-permute-start(f32[512,256]{1,0:T(8,128)S(1)} %collective-permute-done.3.refs_1_), channel_id=1, source_target_pairs={{0,7},{1,0},{2,1},{3,2},{4,3},{5,4},{6,5},{7,6},{32,33},{33,34},{3... | collective-permute-start | bytes 1572872 | tf_op jit(solution)/shard_map/gather/ppermute | solution.py:33
  41.4 0.8 copy-start.2
  46.4 13.3 %collective-permute-start.7 = (f32[512,256]{1,0:T(8,128)}, f32[512,256]{1,0:T(8,128)}, u32[]{:S(2)}, u32[]{:S(2)}) collective-permute-start(f32[512,256]{1,0:T(8,128)} %collective-permute-done.6.refs_5_), channel_id=1, source_target_pairs={{0,1},{1,2},{2,3},{3,4},{4,5},{5,6},{6,7},{7,0},{32,39},{33,32},{3... | collective-permute-start | bytes 1572872 | tf_op jit(solution)/shard_map/gather/ppermute | solution.py:33
  54.1 11.9 %collective-permute-start.8 = (f32[512,256]{1,0:T(8,128)}, f32[512,256]{1,0:T(8,128)}, u32[]{:S(2)}, u32[]{:S(2)}) collective-permute-start(f32[512,256]{1,0:T(8,128)} %collective-permute-done.4.refs_2_), channel_id=1, source_target_pairs={{0,7},{1,0},{2,1},{3,2},{4,3},{5,4},{6,5},{7,6},{32,33},{33,34},{3... | collective-permute-start | bytes 1572872 | tf_op jit(solution)/shard_map/gather/ppermute | solution.py:33
  57.5 1.0 copy-start
  58.5 17.4 %collective-permute-start.19 = (f32[1024,256]{1,0:T(8,128)}, f32[1024,256]{1,0:T(8,128)S(1)}, u32[]{:S(2)}, u32[]{:S(2)}) collective-permute-start(f32[1024,256]{1,0:T(8,128)} %collective-permute-done.16.refs_9_), channel_id=1, source_target_pairs={{0,8},{8,16},{16,24},{24,0},{32,56},{40,32},{48,40},{56,48},{1,9},... | collective-permute-start | bytes 3145736 | tf_op jit(solution)/shard_map/gather/ppermute | solution.py:33
  66.0 9.9 %collective-permute-start.18 = (f32[512,256]{1,0:T(8,128)}, f32[512,256]{1,0:T(8,128)S(1)}, u32[]{:S(2)}, u32[]{:S(2)}) collective-permute-start(f32[512,256]{1,0:T(8,128)} %collective-permute-done.7.refs_4_), channel_id=1, source_target_pairs={{0,1},{1,2},{2,3},{3,4},{4,5},{5,6},{6,7},{7,0},{32,39},{33,32},{3... | collective-permute-start | bytes 1572872 | tf_op jit(solution)/shard_map/gather/ppermute | solution.py:33
  67.7 0.7 copy-start.4
  71.1 1.2 copy-start.1
  72.4 1.0 copy-start.3
  76.0 17.5 %collective-permute-start.20 = (f32[8192,256]{1,0:T(8,128)S(1)}, f32[8192,256]{1,0:T(8,128)S(1)}, u32[]{:S(2)}, u32[]{:S(2)}) collective-permute-start(f32[8192,256]{1,0:T(8,128)S(1)} %place.3.panels), channel_id=1, source_target_pairs={{0,32},{32,0},{1,33},{33,1},{2,34},{34,2},{3,35},{35,3},{4,36},{36... | collective-permute-start | bytes 25165832 | tf_op jit(solution)/shard_map/gather/ppermute | solution.py:37
  99.1 20.2 %collective-permute-start.22 = (f32[8,128,256]{2,1,0:T(8,128)S(1)}, f32[8,128,256]{2,1,0:T(8,128)S(1)}, u32[]{:S(2)}, u32[]{:S(2)}) collective-permute-start(f32[8,128,256]{2,1,0:T(8,128)S(1)} %slot_products.5), channel_id=1, source_target_pairs={{0,8},{8,16},{16,24},{24,0},{32,56},{40,32},{48,40},{56,48},{1,9},... | collective-permute-start | bytes 3145736 | tf_op jit(solution)/shard_map/scatter_rows/ppermute | solution.py:33
  109.2 22.9 %collective-permute-start.21 = (f32[8,128,256]{2,1,0:T(8,128)S(1)}, f32[8,128,256]{2,1,0:T(8,128)S(1)}, u32[]{:S(2)}, u32[]{:S(2)}) collective-permute-start(f32[8,128,256]{2,1,0:T(8,128)S(1)} %get-tuple-element.43), channel_id=1, source_target_pairs={{0,24},{8,0},{16,8},{24,16},{32,40},{40,48},{48,56},{56,32},{1,25}... | collective-permute-start | bytes 3145736 | tf_op jit(solution)/shard_map/scatter_rows/ppermute | solution.py:33
  119.4 17.0 %collective-permute-start.23 = (f32[8,128,256]{2,1,0:T(8,128)S(1)}, f32[8,128,256]{2,1,0:T(8,128)S(1)}, u32[]{:S(2)}, u32[]{:S(2)}) collective-permute-start(f32[8,128,256]{2,1,0:T(8,128)S(1)} %add.123), channel_id=1, source_target_pairs={{0,8},{8,16},{16,24},{24,0},{32,56},{40,32},{48,40},{56,48},{1,9},... | collective-permute-start | bytes 3145736 | tf_op jit(solution)/shard_map/scatter_rows/ppermute | solution.py:33
  136.6 4.8 %collective-permute-start.24 = (f32[128,256]{1,0:T(8,128)S(1)}, f32[128,256]{1,0:T(8,128)S(1)}, u32[]{:S(2)}, u32[]{:S(2)}) collective-permute-start(f32[128,256]{1,0:T(8,128)S(1)} %get-tuple-element.57), channel_id=1, source_target_pairs={{0,1},{1,2},{2,3},{3,4},{4,5},{5,6},{6,7},{7,0},{32,39},{33,32},{3... | collective-permute-start | bytes 393224 | tf_op jit(solution)/shard_map/scatter_rows/ppermute | solution.py:33
  141.5 17.2 %collective-permute-start.25 = (f32[2,128,256]{2,1,0:T(8,128)S(1)}, f32[2,128,256]{2,1,0:T(8,128)S(1)}, u32[]{:S(2)}, u32[]{:S(2)}) collective-permute-start(f32[2,128,256]{2,1,0:T(8,128)S(1)} %pad_maximum_fusion), channel_id=1, source_target_pairs={{0,2},{1,3},{2,4},{3,5},{4,6},{5,7},{6,0},{7,1},{32,38},{33,39},{3... | collective-permute-start | bytes 786440 | tf_op jit(solution)/shard_map/scatter_rows/ppermute | solution.py:33
  143.1 15.5 %collective-permute-start.26 = (f32[2,128,256]{2,1,0:T(8,128)S(1)}, f32[2,128,256]{2,1,0:T(8,128)S(1)}, u32[]{:S(2)}, u32[]{:S(2)}) collective-permute-start(f32[2,128,256]{2,1,0:T(8,128)S(1)} %slice.56), channel_id=1, source_target_pairs={{0,6},{1,7},{2,0},{3,1},{4,2},{5,3},{6,4},{7,5},{32,34},{33,35},{3... | collective-permute-start | bytes 786440 | tf_op jit(solution)/shard_map/scatter_rows/ppermute | solution.py:33
  158.7 4.6 %collective-permute-start.27 = (f32[128,256]{1,0:T(8,128)S(1)}, f32[128,256]{1,0:T(8,128)S(1)}, u32[]{:S(2)}, u32[]{:S(2)}) collective-permute-start(f32[128,256]{1,0:T(8,128)S(1)} %get-tuple-element.48), channel_id=1, source_target_pairs={{0,1},{1,2},{2,3},{3,4},{4,5},{5,6},{6,7},{7,0},{32,39},{33,32},{3... | collective-permute-start | bytes 393224 | tf_op jit(solution)/shard_map/scatter_rows/ppermute | solution.py:33
  158.8 5.1 %collective-permute-start.28 = (f32[128,256]{1,0:T(8,128)S(1)}, f32[128,256]{1,0:T(8,128)S(1)}, u32[]{:S(2)}, u32[]{:S(2)}) collective-permute-start(f32[128,256]{1,0:T(8,128)S(1)} %get-tuple-element.49), channel_id=1, source_target_pairs={{0,7},{1,0},{2,1},{3,2},{4,3},{5,4},{6,5},{7,6},{32,33},{33,34},{3... | collective-permute-start | bytes 393224 | tf_op jit(solution)/shard_map/scatter_rows/ppermute | solution.py:33
